TPU v7x, 512 devices: a whole 4x4x16 slice. The times are simulated.
512 devices in a mesh: tensor: 16 (over z_hi, y, core), context: 32 (over x, z_lo).
Axes of the slice: x: 4, y: 4, z: 16 (z_hi: 2, z_lo: 8; z = z_hi * 8 + z_lo), core: 2. Of those that a mesh axis runs over, the one named last changes fastest.
Arguments:
- gate_act: bfloat16 [16384, 4096], P('context', 'tensor'), may hold values from -6 to 6
- key_act: bfloat16 [16384, 4096], P('context', 'tensor'), may hold values from -6 to 6
- value_act: bfloat16 [16384, 4096], P('context', 'tensor'), may hold values from -6 to 6
- decay_rate: float32 [4096, 16], P('tensor'), may hold values from 3.0517578e-05 to 0.05
- residue: float32 [4096, 16], P('tensor'), may hold values from -1.5 to 1.5
- skip: float32 [4096], P('tensor'), may hold values from 0.5 to 1.5
- out_weight: bfloat16 [4096, 4096], P(None, 'tensor'), may hold values from -0.09375 to 0.09375
Outputs:
- layer_out: bfloat16 [16384, 4096], P('context', 'tensor')
All inputs are finite; a program needn't handle non-finite values.
Results may differ from a plain program's by a relative error of at most 0.015.
Values may be sent and summed in bfloat16 or wider, within the bound.
No kernel may reach another device: no remote copies, remote signals or barrier semaphores. Data moves between devices by JAX's collectives and lax.ppermute only.
A program may use at most 64 MiB of HBM per device.

v0:
```python
import functools

import jax
import jax.numpy as jnp
from jax import lax
from jax.experimental import pallas as pl
from jax.experimental.pallas import tpu as pltpu
from jax.sharding import PartitionSpec as P

CHUNKS = 8
LANES = 128
Z, Y, CORES, X = 16, 4, 2, 4
LOW = Z // 2
AXES = ("tensor", "context")


def linear(x, y, z, core):
    x, y, z, core = x % X, y % Y, z % Z, core % CORES
    tensor = (z // LOW * Y + y) * CORES + core
    return tensor * (X * LOW) + x * LOW + z % LOW


def move(array, dy=0, dz=0, dcore=0):
    pairs = []
    for x in range(X):
        for y in range(Y):
            for z in range(Z):
                for core in range(CORES):
                    way = 1 if core == 0 else -1
                    pairs.append((linear(x, y, z, core), linear(x, y + dy, z + way * dz, core + dcore)))
    return lax.ppermute(array, AXES, pairs)


def fill_mixed(key_ref, value_ref, x_scr):
    product = key_ref[...].astype(jnp.float32) * value_ref[...].astype(jnp.float32)
    mixed = product.astype(jnp.bfloat16).astype(jnp.float32)
    for half in range(x_scr.shape[0]):
        x_scr[half] = mixed[:, half * LANES : (half + 1) * LANES]


def shifted(values, by):
    rows = lax.broadcasted_iota(jnp.int32, values.shape, 0)
    return jnp.where(rows >= by, pltpu.roll(values, by, 0), 0.0)


def ends_kernel(key_ref, value_ref, decay_ref, ends_ref, prefix_ref, x_scr, e_scr):
    fill_mixed(key_ref, value_ref, x_scr)
    tokens = x_scr.shape[1]
    length = tokens // CHUNKS
    rates = decay_ref[...].T
    modes = rates.shape[0]
    for half in range(x_scr.shape[0]):
        cols = slice(half * LANES, (half + 1) * LANES)
        rate = [jnp.broadcast_to(rates[m : m + 1, cols], (CHUNKS, LANES)) for m in range(modes)]
        decay = [jnp.exp(-r) for r in rate]

        def step(t, states):
            x = x_scr[half, pl.ds(t, CHUNKS, stride=length), :]
            return tuple(decay[m] * states[m] + x for m in range(modes))

        zero = jnp.zeros((CHUNKS, LANES), jnp.float32)
        states = lax.fori_loop(0, length, step, (zero,) * modes, unroll=4)
        for m in range(modes):
            total = states[m]
            by = 1
            while by < CHUNKS:
                total = total + jnp.exp(-(rate[m] * float(length * by))) * shifted(total, by)
                by *= 2
            prefix_ref[m, :, cols] = shifted(total, 1)
            e_scr[m : m + 1, cols] = total[CHUNKS - 1 : CHUNKS, :]
    ends_ref[...] = jnp.broadcast_to(e_scr[...].astype(jnp.bfloat16)[None], ends_ref.shape)


def conv_kernel(
    place_ref, gate_ref, key_ref, value_ref, decay_ref, residue_ref, skip_ref, prefix_ref, ends_ref, out_ref, x_scr, y_scr
):
    fill_mixed(key_ref, value_ref, x_scr)
    tokens = x_scr.shape[1]
    length = tokens // CHUNKS
    rates = decay_ref[...].T
    coefs = residue_ref[...].T * jnp.sqrt(2.0 * rates)
    modes = rates.shape[0]
    place = place_ref[0]
    whole = jnp.exp(-(rates * float(tokens)))

    def join(q, carried):
        return jnp.where(q < place, whole * carried + ends_ref[q].astype(jnp.float32), carried)

    carried = lax.fori_loop(0, ends_ref.shape[0], join, jnp.zeros_like(rates), unroll=4)
    row = lax.broadcasted_iota(jnp.int32, (CHUNKS, LANES), 0).astype(jnp.float32) * float(length)
    for half in range(x_scr.shape[0]):
        cols = slice(half * LANES, (half + 1) * LANES)

        def wide(values, m):
            return jnp.broadcast_to(values[m : m + 1, cols], (CHUNKS, LANES))

        rate = [wide(rates, m) for m in range(modes)]
        decay = [jnp.exp(-r) for r in rate]
        coef = [wide(coefs, m) for m in range(modes)]
        skip = jnp.broadcast_to(skip_ref[:, cols], (CHUNKS, LANES))
        first = tuple(prefix_ref[m, :, cols] + jnp.exp(-(rate[m] * row)) * wide(carried, m) for m in range(modes))

        def step(t, states):
            x = x_scr[half, pl.ds(t, CHUNKS, stride=length), :]
            states = tuple(decay[m] * states[m] + x for m in range(modes))
            terms = [coef[m] * states[m] for m in range(modes)]
            while len(terms) > 1:
                terms = [a + b for a, b in zip(terms[::2], terms[1::2])]
            y_scr[half, pl.ds(t, CHUNKS, stride=length), :] = terms[0] + skip * x
            return states

        lax.fori_loop(0, length, step, first, unroll=2)
        out_ref[:, cols] = (gate_ref[:, cols].astype(jnp.float32) * y_scr[half]).astype(jnp.bfloat16)


def pick_kernel(order_ref, keep_in, send_in, keep_out, send_out):
    keep_out[...] = keep_in[...]
    send_out[...] = send_in[...]


def first_product(p0, p1, p2, p3, mine_ref, other_ref, mine_out, other_out):
    for weight, out in ((mine_ref, mine_out), (other_ref, other_out)):
        total = jnp.dot(p0[...], weight[0], preferred_element_type=jnp.float32)
        for i, piece in enumerate((p1, p2, p3)):
            total += jnp.dot(piece[...], weight[i + 1], preferred_element_type=jnp.float32)
        out[...] = total


def second_product(p0, p1, p2, p3, mine_ref, other_ref, mine_in, other_in, mine_out, other_out):
    for weight, start, out in ((other_ref, other_in, other_out), (mine_ref, mine_in, mine_out)):
        total = start[...]
        for i, piece in enumerate((p0, p1, p2, p3)):
            total += jnp.dot(piece[...], weight[i], preferred_element_type=jnp.float32)
        out[...] = total.astype(out.dtype)


def full(array):
    rank = len(array.shape)
    return pl.BlockSpec(array.shape, lambda *_: (0,) * rank)


PARAMS = pltpu.CompilerParams(vmem_limit_bytes=40 * 1024 * 1024)


def call(kernel, args, outs, scratch=(), flops=0, scalars=0):
    in_specs = [pl.BlockSpec(memory_space=pltpu.SMEM)] * scalars + [full(a) for a in args[scalars:]]
    moved = sum(a.size * a.dtype.itemsize for a in (*args, *outs))
    return pl.pallas_call(
        kernel,
        grid=(1,),
        in_specs=in_specs,
        out_specs=[full(o) for o in outs],
        out_shape=list(outs),
        scratch_shapes=list(scratch),
        compiler_params=PARAMS,
        cost_estimate=pl.CostEstimate(flops=flops, bytes_accessed=moved, transcendentals=0),
    )(*args)


def body(gate_act, key_act, value_act, decay_rate, residue, skip, out_weight):
    tokens, width = gate_act.shape
    modes = decay_rate.shape[1]
    parts = lax.axis_size("context")
    place = lax.axis_index("context")
    here = lax.axis_index("tensor")
    z_hi, y, core = here // (Y * CORES), here // CORES % Y, here % CORES
    shape = jax.ShapeDtypeStruct
    f32, bf16 = jnp.float32, jnp.bfloat16
    halves = width // LANES
    block = pltpu.VMEM((halves, tokens, LANES), f32)

    ends, prefix = call(
        ends_kernel,
        (key_act, value_act, decay_rate),
        (shape((parts, modes, width), bf16), shape((modes, CHUNKS, width), f32)),
        (block, pltpu.VMEM((modes, width), f32)),
        flops=2 * tokens * width * modes,
    )
    with jax.named_scope("block_states"):
        ends = lax.all_to_all(ends, "context", 0, 0)

    ys = jnp.stack([y, (y - 1) % Y, (y + 1) % Y, (y + 2) % Y])
    rows = jnp.concatenate([z_hi * Y + ys, (1 - z_hi) * Y + ys])
    order = jnp.stack([rows * CORES + core, rows * CORES + 1 - core]).astype(jnp.int32)
    slab = (1, width, out_weight.shape[1])
    pieces = rows.shape[0]
    picked = shape((pieces, *slab[1:]), bf16)
    by_rows = out_weight.reshape(2 * pieces, *slab[1:])
    mine, theirs = pl.pallas_call(
        pick_kernel,
        grid_spec=pltpu.PrefetchScalarGridSpec(
            num_scalar_prefetch=1,
            grid=(pieces,),
            in_specs=[
                pl.BlockSpec(slab, lambda i, order: (order[0, i], 0, 0)),
                pl.BlockSpec(slab, lambda i, order: (order[1, i], 0, 0)),
            ],
            out_specs=[pl.BlockSpec(slab, lambda i, order: (i, 0, 0))] * 2,
        ),
        out_shape=[picked, picked],
        compiler_params=PARAMS,
    )(order, by_rows, by_rows)
    with jax.named_scope("weight_swap"):
        other = move(theirs, dcore=1)

    (gated,) = call(
        conv_kernel,
        (place.reshape(1), gate_act, key_act, value_act, decay_rate, residue, skip.reshape(1, width), prefix, ends),
        (shape((tokens, width), bf16),),
        (block, block),
        flops=4 * tokens * width * modes,
        scalars=1,
    )

    with jax.named_scope("along_z"):
        far = move(gated, dz=Z // 2 - 1)
    with jax.named_scope("own_along_y"):
        near = [gated] + [move(gated, dy=d) for d in (1, -1, 2)]
    sums = shape((tokens, out_weight.shape[1]), f32)
    work = 2 * 2 * tokens * (pieces // 2) * width * out_weight.shape[1]
    half = pieces // 2
    mine_sum, other_sum = call(first_product, (*near, mine[:half], other[:half]), (sums, sums), flops=work)
    with jax.named_scope("far_along_y"):
        far = [move(far, dy=d, dz=1) for d in (0, 1, -1, 2)]
    mine_sum, other_sum = call(
        second_product,
        (*far, mine[half:], other[half:], mine_sum, other_sum),
        (sums, shape(sums.shape, bf16)),
        flops=work,
    )
    with jax.named_scope("sum_swap"):
        from_other = move(other_sum, dcore=1)
    return (mine_sum + from_other.astype(f32)).astype(bf16)


def solution(mesh):
    in_specs = (
        P("context", "tensor"),
        P("context", "tensor"),
        P("context", "tensor"),
        P("tensor", None),
        P("tensor", None),
        P("tensor"),
        P(None, "tensor"),
    )
    return jax.shard_map(body, mesh=mesh, in_specs=in_specs, out_specs=P("context", "tensor"), check_vma=False)
```

profile of v0, /device:TPU:1, one launch (start us, length us, event | category | flops | bytes accessed | tf_op | source)
XLA Modules:
  0.0 106.7 jit_solution(15378449398271227906)
XLA Ops:
  0.0 0.8 copy.9.decay_ref
  0.8 0.9 copy-done.1
  1.8 0.9 copy-done.3
  2.7 2.0 %shard_map.73 = (bf16[32,16,256]{2,1,0:T(8,128)(2,1)}, f32[16,8,256]{2,1,0:T(8,128)S(1)}) custom-call(bf16[512,256]{1,0:T(8,128)(2,1)S(1)} %copy-done.1, bf16[512,256]{1,0:T(8,128)(2,1)S(1)} %copy-done.3, f32[256,16]{1,0:T(8,128)S(1)} %copy.9.decay_ref), custom_call_target="tpu_custom_call" | custom-call | flops 4194304 | bytes 933888 | tf_op jit(solution)/shard_map/pallas_call | solution.py:148
  4.7 15.9 %all-to-all-start = ((bf16[32,16,256]{2,1,0:T(8,128)(2,1)}), bf16[32,16,256]{2,1,0:T(8,128)(2,1)S(1)}, u32[]{:S(2)}, u32[]{:S(2)}) async-start(bf16[32,16,256]{2,1,0:T(8,128)(2,1)} %get-tuple-element.14), calls=%async_computation | async-start | bytes 524288 | tf_op jit(solution)/shard_map/block_states/all_to_all | solution.py:180
  20.7 0.1 add_bitcast_fusion.1
  20.8 0.1 broadcast_add_fusion
  20.9 1.6 %copy-done = bf16[4096,256]{1,0:T(8,128)(2,1)S(1)} copy-done((bf16[4096,256]{1,0:T(8,128)(2,1)S(1)}, bf16[4096,256]{1,0:T(8,128)(2,1)}, u32[]{:S(2)}) %copy-start) | copy-done | bytes 2097176
  22.5 0.8 shard_map.75
  23.3 2.9 %collective-permute-start.5 = (bf16[8,256,256]{2,1,0:T(8,128)(2,1)S(1)}, bf16[8,256,256]{2,1,0:T(8,128)(2,1)}, u32[]{:S(2)}, u32[]{:S(2)}) collective-permute-start(bf16[8,256,256]{2,1,0:T(8,128)(2,1)S(1)} %get-tuple-element.16), channel_id=1, source_target_pairs={{0,32},{32,0},{1,33},{33,1},{2,34},{34,2},{3,35},{35,3},{4,36},{36... | collective-permute-start | bytes 3145736 | tf_op jit(solution)/shard_map/weight_swap/ppermute | solution.py:31
  26.2 0.8 copy.10.residue_ref
  27.0 12.4 %all-to-all-done.ends_ref = bf16[32,16,256]{2,1,0:T(8,128)(2,1)S(1)} async-done(((bf16[32,16,256]{2,1,0:T(8,128)(2,1)}), bf16[32,16,256]{2,1,0:T(8,128)(2,1)S(1)}, u32[]{:S(2)}, u32[]{:S(2)}) %all-to-all-start) | async-done | bytes 262176 | tf_op jit(solution)/shard_map/block_states/all_to_all | solution.py:180
  39.4 2.7 %shard_map.74.p0 = bf16[512,256]{1,0:T(8,128)(2,1)S(1)} custom-call(s32[1]{0:T(128)} %bitcast.place_ref, bf16[512,256]{1,0:T(8,128)(2,1)S(1)} %copy-done.5, bf16[512,256]{1,0:T(8,128)(2,1)S(1)} %copy-done.2, bf16[512,256]{1,0:T(8,128)(2,1)S(1)} %copy-done.4, f32[256,16]{1,0:T(8,128)S(1)} %copy.9.decay_ref, f32[256,16]{1,0:T(8,128)S(1)} %copy.10.residue_ref, ...), custom_call_target="tpu_custom_call" | custom-call | flops 8388608 | bytes 1475588 | tf_op jit(solution)/shard_map/pallas_call | solution.py:148
  42.1 3.2 %collective-permute-start.6 = (bf16[512,256]{1,0:T(8,128)(2,1)S(1)}, bf16[512,256]{1,0:T(8,128)(2,1)S(1)}, u32[]{:S(2)}, u32[]{:S(2)}) collective-permute-start(bf16[512,256]{1,0:T(8,128)(2,1)S(1)} %shard_map.74.p0), channel_id=1, source_target_pairs={{0,64},{32,96},{1,65},{33,97},{2,66},{34,98},{3,67},{35,99},{4,68}... | collective-permute-start | bytes 786440 | tf_op jit(solution)/shard_map/own_along_y/ppermute | solution.py:31
  45.3 3.4 %collective-permute-start.7 = (bf16[512,256]{1,0:T(8,128)(2,1)S(1)}, bf16[512,256]{1,0:T(8,128)(2,1)S(1)}, u32[]{:S(2)}, u32[]{:S(2)}) collective-permute-start(bf16[512,256]{1,0:T(8,128)(2,1)S(1)} %shard_map.74.p0), channel_id=1, source_target_pairs={{0,192},{32,224},{1,193},{33,225},{2,194},{34,226},{3,195},{35,227... | collective-permute-start | bytes 786440 | tf_op jit(solution)/shard_map/own_along_y/ppermute | solution.py:31
  48.6 5.8 %collective-permute-start = (bf16[512,256]{1,0:T(8,128)(2,1)S(1)}, bf16[512,256]{1,0:T(8,128)(2,1)S(1)}, u32[]{:S(2)}, u32[]{:S(2)}) collective-permute-start(bf16[512,256]{1,0:T(8,128)(2,1)S(1)} %shard_map.74.p0), channel_id=1, source_target_pairs={{0,7},{32,289},{1,256},{33,290},{2,257},{34,291},{3,258},{35,292},... | collective-permute-start | bytes 786440 | tf_op jit(solution)/shard_map/along_z/ppermute | solution.py:31
  54.5 0.1 fusion.1
  54.6 3.5 %collective-permute-start.8 = (bf16[512,256]{1,0:T(8,128)(2,1)S(1)}, bf16[512,256]{1,0:T(8,128)(2,1)S(1)}, u32[]{:S(2)}, u32[]{:S(2)}) collective-permute-start(bf16[512,256]{1,0:T(8,128)(2,1)S(1)} %shard_map.74.p0), channel_id=1, source_target_pairs={{0,128},{32,160},{1,129},{33,161},{2,130},{34,162},{3,131},{35,163... | collective-permute-start | bytes 786440 | tf_op jit(solution)/shard_map/own_along_y/ppermute | solution.py:31
  58.1 11.6 %collective-permute-done = bf16[512,256]{1,0:T(8,128)(2,1)S(1)} collective-permute-done((bf16[512,256]{1,0:T(8,128)(2,1)S(1)}, bf16[512,256]{1,0:T(8,128)(2,1)S(1)}, u32[]{:S(2)}, u32[]{:S(2)}) %collective-permute-start) | collective-permute-done | bytes 262176 | tf_op jit(solution)/shard_map/along_z/ppermute | solution.py:31
  69.7 4.4 %collective-permute-start.1 = (bf16[512,256]{1,0:T(8,128)(2,1)S(1)}, bf16[512,256]{1,0:T(8,128)(2,1)S(1)}, u32[]{:S(2)}, u32[]{:S(2)}) collective-permute-start(bf16[512,256]{1,0:T(8,128)(2,1)S(1)} %collective-permute-done), channel_id=1, source_target_pairs={{0,1},{32,295},{1,2},{33,32},{2,3},{34,33},{3,4},{35,34},{4,5},{36... | collective-permute-start | bytes 786440 | tf_op jit(solution)/shard_map/far_along_y/ppermute | solution.py:31
  74.1 1.9 %collective-permute-start.2 = (bf16[512,256]{1,0:T(8,128)(2,1)S(1)}, bf16[512,256]{1,0:T(8,128)(2,1)S(1)}, u32[]{:S(2)}, u32[]{:S(2)}) collective-permute-start(bf16[512,256]{1,0:T(8,128)(2,1)S(1)} %collective-permute-done), channel_id=1, source_target_pairs={{0,65},{32,359},{1,66},{33,96},{2,67},{34,97},{3,68},{35,98},{4,69... | collective-permute-start | bytes 786440 | tf_op jit(solution)/shard_map/far_along_y/ppermute | solution.py:31
  76.0 4.3 %collective-permute-start.3 = (bf16[512,256]{1,0:T(8,128)(2,1)S(1)}, bf16[512,256]{1,0:T(8,128)(2,1)S(1)}, u32[]{:S(2)}, u32[]{:S(2)}) collective-permute-start(bf16[512,256]{1,0:T(8,128)(2,1)S(1)} %collective-permute-done), channel_id=1, source_target_pairs={{0,193},{32,487},{1,194},{33,224},{2,195},{34,225},{3,196},{35,226... | collective-permute-start | bytes 786440 | tf_op jit(solution)/shard_map/far_along_y/ppermute | solution.py:31
  80.4 5.8 %collective-permute-start.4 = (bf16[512,256]{1,0:T(8,128)(2,1)S(1)}, bf16[512,256]{1,0:T(8,128)(2,1)S(1)}, u32[]{:S(2)}, u32[]{:S(2)}) collective-permute-start(bf16[512,256]{1,0:T(8,128)(2,1)S(1)} %collective-permute-done), channel_id=1, source_target_pairs={{0,129},{32,423},{1,130},{33,160},{2,131},{34,161},{3,132},{35,162... | collective-permute-start | bytes 786440 | tf_op jit(solution)/shard_map/far_along_y/ppermute | solution.py:31
  86.2 1.3 %fusion = (bf16[4,256,256]{2,1,0:T(8,128)(2,1)S(1)}, bf16[4,256,256]{2,1,0:T(8,128)(2,1)S(1)}) fusion(bf16[8,256,256]{2,1,0:T(8,128)(2,1)} %collective-permute-done.5), kind=kLoop, calls=%fused_computation.8 | loop fusion | bytes 2097152 | tf_op jit(solution)/shard_map/slice | solution.py:222
  87.5 0.7 shard_map.76
  88.2 0.7 collective-permute-done.2.p1
  88.9 1.7 %collective-permute-done.3.p2 = bf16[512,256]{1,0:T(8,128)(2,1)S(1)} collective-permute-done((bf16[512,256]{1,0:T(8,128)(2,1)S(1)}, bf16[512,256]{1,0:T(8,128)(2,1)S(1)}, u32[]{:S(2)}, u32[]{:S(2)}) %collective-permute-start.3) | collective-permute-done | bytes 262176 | tf_op jit(solution)/shard_map/far_along_y/ppermute | solution.py:31
  90.6 6.9 %collective-permute-done.4.p3 = bf16[512,256]{1,0:T(8,128)(2,1)S(1)} collective-permute-done((bf16[512,256]{1,0:T(8,128)(2,1)S(1)}, bf16[512,256]{1,0:T(8,128)(2,1)S(1)}, u32[]{:S(2)}, u32[]{:S(2)}) %collective-permute-start.4) | collective-permute-done | bytes 262176 | tf_op jit(solution)/shard_map/far_along_y/ppermute | solution.py:31
  97.6 0.7 shard_map.77
  98.3 6.5 %collective-permute-start.9 = (bf16[512,256]{1,0:T(8,128)(2,1)S(1)}, bf16[512,256]{1,0:T(8,128)(2,1)S(1)}, u32[]{:S(2)}, u32[]{:S(2)}) collective-permute-start(bf16[512,256]{1,0:T(8,128)(2,1)S(1)} %get-tuple-element.20), channel_id=1, source_target_pairs={{0,32},{32,0},{1,33},{33,1},{2,34},{34,2},{3,35},{35,3},{4,36},{36... | collective-permute-start | bytes 786440 | tf_op jit(solution)/shard_map/sum_swap/ppermute | solution.py:31
  104.8 1.1 %collective-permute-done.9 = bf16[512,256]{1,0:T(8,128)(2,1)S(1)} collective-permute-done((bf16[512,256]{1,0:T(8,128)(2,1)S(1)}, bf16[512,256]{1,0:T(8,128)(2,1)S(1)}, u32[]{:S(2)}, u32[]{:S(2)}) %collective-permute-start.9) | collective-permute-done | bytes 262176 | tf_op jit(solution)/shard_map/sum_swap/ppermute | solution.py:31
  106.0 0.8 add_convert_fusion
  (18 shorter events, 0.1 us)
Async XLA Ops:
  0.8 1.0 copy-start.1
  1.8 0.9 copy-start.3
  4.7 34.7 %all-to-all-start = ((bf16[32,16,256]{2,1,0:T(8,128)(2,1)}), bf16[32,16,256]{2,1,0:T(8,128)(2,1)S(1)}, u32[]{:S(2)}, u32[]{:S(2)}) async-start(bf16[32,16,256]{2,1,0:T(8,128)(2,1)} %get-tuple-element.14), calls=%async_computation | async-start | bytes 524288 | tf_op jit(solution)/shard_map/block_states/all_to_all | solution.py:180
  20.9 1.6 %copy-start = (bf16[4096,256]{1,0:T(8,128)(2,1)S(1)}, bf16[4096,256]{1,0:T(8,128)(2,1)}, u32[]{:S(2)}) copy-start(bf16[4096,256]{1,0:T(8,128)(2,1)} %param.13) | copy-start | bytes 6291460
  22.5 16.9 %copy-start.2 = (bf16[512,256]{1,0:T(8,128)(2,1)S(1)}, bf16[512,256]{1,0:T(8,128)(2,1)}, u32[]{:S(2)}) copy-start(bf16[512,256]{1,0:T(8,128)(2,1)} %key_ref.3) | copy-start | bytes 786436
  22.5 16.9 %copy-start.4 = (bf16[512,256]{1,0:T(8,128)(2,1)S(1)}, bf16[512,256]{1,0:T(8,128)(2,1)}, u32[]{:S(2)}) copy-start(bf16[512,256]{1,0:T(8,128)(2,1)} %value_ref.3) | copy-start | bytes 786436
  22.5 16.9 %copy-start.5 = (bf16[512,256]{1,0:T(8,128)(2,1)S(1)}, bf16[512,256]{1,0:T(8,128)(2,1)}, u32[]{:S(2)}) copy-start(bf16[512,256]{1,0:T(8,128)(2,1)} %gate_ref.1) | copy-start | bytes 786436
  22.5 16.9 %copy-start.6 = (f32[256]{0:T(256)S(1)}, f32[256]{0:T(256)}, u32[]{:S(2)}) copy-start(f32[256]{0:T(256)} %param.12) | copy-start | bytes 3076
  23.3 50.8 %collective-permute-start.5 = (bf16[8,256,256]{2,1,0:T(8,128)(2,1)S(1)}, bf16[8,256,256]{2,1,0:T(8,128)(2,1)}, u32[]{:S(2)}, u32[]{:S(2)}) collective-permute-start(bf16[8,256,256]{2,1,0:T(8,128)(2,1)S(1)} %get-tuple-element.16), channel_id=1, source_target_pairs={{0,32},{32,0},{1,33},{33,1},{2,34},{34,2},{3,35},{35,3},{4,36},{36... | collective-permute-start | bytes 3145736 | tf_op jit(solution)/shard_map/weight_swap/ppermute | solution.py:31
  42.1 34.0 %collective-permute-start.6 = (bf16[512,256]{1,0:T(8,128)(2,1)S(1)}, bf16[512,256]{1,0:T(8,128)(2,1)S(1)}, u32[]{:S(2)}, u32[]{:S(2)}) collective-permute-start(bf16[512,256]{1,0:T(8,128)(2,1)S(1)} %shard_map.74.p0), channel_id=1, source_target_pairs={{0,64},{32,96},{1,65},{33,97},{2,66},{34,98},{3,67},{35,99},{4,68}... | collective-permute-start | bytes 786440 | tf_op jit(solution)/shard_map/own_along_y/ppermute | solution.py:31
  45.3 35.1 %collective-permute-start.7 = (bf16[512,256]{1,0:T(8,128)(2,1)S(1)}, bf16[512,256]{1,0:T(8,128)(2,1)S(1)}, u32[]{:S(2)}, u32[]{:S(2)}) collective-permute-start(bf16[512,256]{1,0:T(8,128)(2,1)S(1)} %shard_map.74.p0), channel_id=1, source_target_pairs={{0,192},{32,224},{1,193},{33,225},{2,194},{34,226},{3,195},{35,227... | collective-permute-start | bytes 786440 | tf_op jit(solution)/shard_map/own_along_y/ppermute | solution.py:31
  48.6 21.1 %collective-permute-start = (bf16[512,256]{1,0:T(8,128)(2,1)S(1)}, bf16[512,256]{1,0:T(8,128)(2,1)S(1)}, u32[]{:S(2)}, u32[]{:S(2)}) collective-permute-start(bf16[512,256]{1,0:T(8,128)(2,1)S(1)} %shard_map.74.p0), channel_id=1, source_target_pairs={{0,7},{32,289},{1,256},{33,290},{2,257},{34,291},{3,258},{35,292},... | collective-permute-start | bytes 786440 | tf_op jit(solution)/shard_map/along_z/ppermute | solution.py:31
  54.6 32.9 %collective-permute-start.8 = (bf16[512,256]{1,0:T(8,128)(2,1)S(1)}, bf16[512,256]{1,0:T(8,128)(2,1)S(1)}, u32[]{:S(2)}, u32[]{:S(2)}) collective-permute-start(bf16[512,256]{1,0:T(8,128)(2,1)S(1)} %shard_map.74.p0), channel_id=1, source_target_pairs={{0,128},{32,160},{1,129},{33,161},{2,130},{34,162},{3,131},{35,163... | collective-permute-start | bytes 786440 | tf_op jit(solution)/shard_map/own_along_y/ppermute | solution.py:31
  69.7 18.5 %collective-permute-start.1 = (bf16[512,256]{1,0:T(8,128)(2,1)S(1)}, bf16[512,256]{1,0:T(8,128)(2,1)S(1)}, u32[]{:S(2)}, u32[]{:S(2)}) collective-permute-start(bf16[512,256]{1,0:T(8,128)(2,1)S(1)} %collective-permute-done), channel_id=1, source_target_pairs={{0,1},{32,295},{1,2},{33,32},{2,3},{34,33},{3,4},{35,34},{4,5},{36... | collective-permute-start | bytes 786440 | tf_op jit(solution)/shard_map/far_along_y/ppermute | solution.py:31
  74.1 14.8 %collective-permute-start.2 = (bf16[512,256]{1,0:T(8,128)(2,1)S(1)}, bf16[512,256]{1,0:T(8,128)(2,1)S(1)}, u32[]{:S(2)}, u32[]{:S(2)}) collective-permute-start(bf16[512,256]{1,0:T(8,128)(2,1)S(1)} %collective-permute-done), channel_id=1, source_target_pairs={{0,65},{32,359},{1,66},{33,96},{2,67},{34,97},{3,68},{35,98},{4,69... | collective-permute-start | bytes 786440 | tf_op jit(solution)/shard_map/far_along_y/ppermute | solution.py:31
  76.0 14.6 %collective-permute-start.3 = (bf16[512,256]{1,0:T(8,128)(2,1)S(1)}, bf16[512,256]{1,0:T(8,128)(2,1)S(1)}, u32[]{:S(2)}, u32[]{:S(2)}) collective-permute-start(bf16[512,256]{1,0:T(8,128)(2,1)S(1)} %collective-permute-done), channel_id=1, source_target_pairs={{0,193},{32,487},{1,194},{33,224},{2,195},{34,225},{3,196},{35,226... | collective-permute-start | bytes 786440 | tf_op jit(solution)/shard_map/far_along_y/ppermute | solution.py:31
  80.4 17.2 %collective-permute-start.4 = (bf16[512,256]{1,0:T(8,128)(2,1)S(1)}, bf16[512,256]{1,0:T(8,128)(2,1)S(1)}, u32[]{:S(2)}, u32[]{:S(2)}) collective-permute-start(bf16[512,256]{1,0:T(8,128)(2,1)S(1)} %collective-permute-done), channel_id=1, source_target_pairs={{0,129},{32,423},{1,130},{33,160},{2,131},{34,161},{3,132},{35,162... | collective-permute-start | bytes 786440 | tf_op jit(solution)/shard_map/far_along_y/ppermute | solution.py:31
  98.3 7.7 %collective-permute-start.9 = (bf16[512,256]{1,0:T(8,128)(2,1)S(1)}, bf16[512,256]{1,0:T(8,128)(2,1)S(1)}, u32[]{:S(2)}, u32[]{:S(2)}) collective-permute-start(bf16[512,256]{1,0:T(8,128)(2,1)S(1)} %get-tuple-element.20), channel_id=1, source_target_pairs={{0,32},{32,0},{1,33},{33,1},{2,34},{34,2},{3,35},{35,3},{4,36},{36... | collective-permute-start | bytes 786440 | tf_op jit(solution)/shard_map/sum_swap/ppermute | solution.py:31
where the time goes:
time: 107 us
  starting transfers between devices  57.7 us (54%)
  waiting for transfers between devices  34.4 us (32%)
  Pallas kernels  6.86 us (6%)
  local copies, waits for them, and re-layouts  6.47 us (6%)
    ppermute x10, starting transfers between devices, move(): return lax.ppermute(array, AXES, pairs)  41.8 us
    ppermute x10, waiting for transfers between devices, move(): return lax.ppermute(array, AXES, pairs)  22.1 us
    all_to_all x1, starting transfers between devices, body(): ends = lax.all_to_all(ends, 'context', 0, 0)  15.9 us
    all_to_all x1, waiting for transfers between devices, body(): ends = lax.all_to_all(ends, 'context', 0, 0)  12.4 us
    pallas_call x4, Pallas kernels, call(): pl.pallas_call(kernel, grid=(1,), in_specs=in_specs, out_specs=[full(o) f...  6.04 us
    unnamed x16, local copies, waits for them, and re-layouts  5.13 us
  transfers between devices with their start and end apart: 11, of which 6 were waited for; matrix products, arithmetic and copies ran while one was open for 2% of the time, Pallas kernels for 4%

commit v1 on v0

v1 whole, which is shorter than its diff:
```python
import jax
import jax.numpy as jnp
from jax import lax
from jax.experimental import pallas as pl
from jax.experimental.pallas import tpu as pltpu
from jax.sharding import PartitionSpec as P

CHUNKS = 8
LANES = 128
Z, Y, CORES, X = 16, 4, 2, 4
LOW = Z // 2
AXES = ("tensor", "context")


def linear(x, y, z, core):
    x, y, z, core = x % X, y % Y, z % Z, core % CORES
    tensor = (z // LOW * Y + y) * CORES + core
    return tensor * (X * LOW) + x * LOW + z % LOW


def move(array, dy=0, dz=0, dcore=0):
    pairs = []
    for x in range(X):
        for y in range(Y):
            for z in range(Z):
                for core in range(CORES):
                    pairs.append((linear(x, y, z, core), linear(x, y + dy, z + dz, core + dcore)))
    return lax.ppermute(array, AXES, pairs)


def mixed_of(key_ref, value_ref):
    product = key_ref[...].astype(jnp.float32) * value_ref[...].astype(jnp.float32)
    return product.astype(jnp.bfloat16).astype(jnp.float32)


def shifted(values, by):
    rows = lax.broadcasted_iota(jnp.int32, values.shape, 0)
    return jnp.where(rows >= by, pltpu.roll(values, by, 0), 0.0)


def ends_kernel(key_ref, value_ref, decay_ref, ends_ref, states_ref, x_scr, e_scr):
    x_scr[...] = mixed_of(key_ref, value_ref)
    length = x_scr.shape[0] // CHUNKS
    modes = decay_ref.shape[0]
    rate = [jnp.broadcast_to(decay_ref[m : m + 1, :], (CHUNKS, LANES)) for m in range(modes)]
    decay = [jnp.exp(-r) for r in rate]

    def step(t, states):
        x = x_scr[pl.ds(t, CHUNKS, stride=length), :]
        return tuple(decay[m] * states[m] + x for m in range(modes))

    zero = jnp.zeros((CHUNKS, LANES), jnp.float32)
    states = lax.fori_loop(0, length, step, (zero,) * modes, unroll=4)
    later = (CHUNKS - 1 - lax.broadcasted_iota(jnp.int32, (CHUNKS, LANES), 0)).astype(jnp.float32) * float(length)
    for m in range(modes):
        states_ref[m] = states[m]
        e_scr[m : m + 1, :] = jnp.sum(jnp.exp(-(rate[m] * later)) * states[m], axis=0, keepdims=True)
    ends_ref[...] = jnp.broadcast_to(e_scr[...].astype(jnp.bfloat16)[None], ends_ref.shape)


def row_kernel(place_ref, ends_ref, decay_ref, before_ref, row_ref):
    rates = decay_ref[...]
    length = place_ref[1]
    whole = jnp.exp(-(rates * length.astype(jnp.float32)))
    before = total = jnp.zeros_like(rates)
    for q in range(ends_ref.shape[0]):
        end = ends_ref[q].astype(jnp.float32)
        before = jnp.where(q < place_ref[0], whole * before + end, before)
        total = whole * total + end
    before_ref[...] = before
    row_ref[...] = jnp.broadcast_to(total.astype(jnp.bfloat16)[None], row_ref.shape)


def wide(values, m, cols):
    return jnp.broadcast_to(values[m : m + 1, cols], (CHUNKS, LANES))


def add_up(terms):
    while len(terms) > 1:
        terms = [a + b for a, b in zip(terms[::2], terms[1::2])]
    return terms[0]


def local_kernel(gate_ref, key_ref, value_ref, decay_ref, residue_ref, skip_ref, states_ref, local_ref, x_scr, y_scr):
    x_scr[...] = mixed_of(key_ref, value_ref)
    tokens = x_scr.shape[0]
    length = tokens // CHUNKS
    rates = decay_ref[...]
    coefs = residue_ref[...] * jnp.sqrt(2.0 * rates)
    modes = rates.shape[0]
    rate = [jnp.broadcast_to(rates[m : m + 1, :], (CHUNKS, LANES)) for m in range(modes)]
    decay = [jnp.exp(-r) for r in rate]
    coef = [jnp.broadcast_to(coefs[m : m + 1, :], (CHUNKS, LANES)) for m in range(modes)]
    skip = jnp.broadcast_to(skip_ref[...], (CHUNKS, LANES))
    first = []
    for m in range(modes):
        total = states_ref[m]
        by = 1
        while by < CHUNKS:
            total = total + jnp.exp(-(rate[m] * float(length * by))) * shifted(total, by)
            by *= 2
        first.append(shifted(total, 1))

    def step(t, states):
        x = x_scr[pl.ds(t, CHUNKS, stride=length), :]
        states = tuple(decay[m] * states[m] + x for m in range(modes))
        total = add_up([coef[m] * states[m] for m in range(modes)])
        y_scr[pl.ds(t, CHUNKS, stride=length), :] = total + skip * x
        return states

    lax.fori_loop(0, length, step, tuple(first), unroll=2)
    local_ref[:tokens, :] = gate_ref[...].astype(jnp.float32) * y_scr[...]
    local_ref[tokens : tokens + modes, :] = rates
    local_ref[tokens + modes :, :] = coefs


def from_states(rates, start, y_scr, rows):
    modes = rates.shape[0]
    after = lax.broadcasted_iota(jnp.int32, (CHUNKS, LANES), 0).astype(jnp.float32) + 1.0
    for half in range(y_scr.shape[0]):
        cols = slice(half * LANES, (half + 1) * LANES)
        rate = [wide(rates, m, cols) for m in range(modes)]
        decay = [jnp.exp(-(r * float(CHUNKS))) for r in rate]
        first = tuple(wide(start, m, cols) * jnp.exp(-(rate[m] * after)) for m in range(modes))

        def step(g, terms):
            y_scr[half, pl.ds(pl.multiple_of(g * CHUNKS, CHUNKS), CHUNKS), :] = add_up(list(terms))
            return tuple(decay[m] * terms[m] for m in range(modes))

        lax.fori_loop(0, rows // CHUNKS, step, first, unroll=4)


def carry_kernel(place_ref, rows_ref, before_ref, local_ref, gate_hbm, gated_ref, y_scr, gate_ref, arrived):
    fetch = pltpu.make_async_copy(gate_hbm, gate_ref, arrived)
    fetch.start()
    tokens = y_scr.shape[1]
    modes = (local_ref.shape[0] - tokens) // 2
    rates, coefs = local_ref[tokens : tokens + modes, :], local_ref[tokens + modes :, :]
    row, here, length = place_ref[0], place_ref[1], place_ref[2]
    whole = jnp.exp(-(rates * length.astype(jnp.float32)))
    carried = jnp.zeros_like(rates)
    for q in range(rows_ref.shape[0]):
        carried = jnp.where(q < row, whole * carried + rows_ref[q].astype(jnp.float32), carried)
    start = coefs * (before_ref[...] + jnp.exp(-(rates * here.astype(jnp.float32))) * carried)
    from_states(rates, start, y_scr, tokens)
    fetch.wait()
    for half in range(y_scr.shape[0]):
        cols = slice(half * LANES, (half + 1) * LANES)
        gate = gate_ref[:, cols].astype(jnp.float32)
        gated_ref[:, cols] = (local_ref[:tokens, cols] + gate * y_scr[half]).astype(jnp.bfloat16)


def copies_kernel(in_ref, out_ref):
    for i in range(out_ref.shape[0]):
        out_ref[i] = in_ref[...]


def near_product(
    order_ref, p0, p1, p2, p3, mine_hbm, other_hbm, mine_out, other_out, far_mine, far_other, near_mine, near_other, arrived
):
    sides = ((mine_hbm, near_mine, far_mine), (other_hbm, near_other, far_other))

    def copy(side, i):
        source, near, far = sides[side]
        target = near.at[i] if i < Y else far.at[i - Y]
        return pltpu.make_async_copy(source.at[order_ref[i]], target, arrived.at[side, i])

    for i in range(2 * Y):
        for side in range(2):
            copy(side, i).start()
    totals = [0.0, 0.0]
    for i, piece in enumerate((p0, p1, p2, p3)):
        for side in range(2):
            copy(side, i).wait()
            totals[side] += jnp.dot(piece[...], sides[side][1][i], preferred_element_type=jnp.float32)
    mine_out[...], other_out[...] = totals
    for i in range(Y, 2 * Y):
        for side in range(2):
            copy(side, i).wait()


def far_product(pieces_ref, weight_ref, start_ref, out_ref):
    total = start_ref[...]
    for i in range(Y):
        total += jnp.dot(pieces_ref[i], weight_ref[i], preferred_element_type=jnp.float32)
    out_ref[...] = total.astype(out_ref.dtype)


def full(array):
    rank = len(array.shape)
    return pl.BlockSpec(array.shape, lambda *_: (0,) * rank)


def params(mebibytes):
    return pltpu.CompilerParams(vmem_limit_bytes=mebibytes * 1024 * 1024)


def cost(args, outs, flops):
    moved = sum(a.size * a.dtype.itemsize for a in (*args, *outs))
    return pl.CostEstimate(flops=flops, bytes_accessed=moved, transcendentals=0)


def call(kernel, args, outs, scratch=(), flops=0, scalars=0, limit=16, fetched=(), after=()):
    count, waits = len(args) + len(fetched), len(after)

    def run(*refs):
        kernel(*refs[:count], *refs[count + waits :])

    return pl.pallas_call(
        run,
        grid=(1,),
        in_specs=[
            *[pl.BlockSpec(memory_space=pltpu.SMEM)] * scalars,
            *[full(a) for a in args[scalars:]],
            *[pl.BlockSpec(memory_space=pl.ANY)] * (len(fetched) + waits),
        ],
        out_specs=[full(o) for o in outs],
        out_shape=list(outs),
        scratch_shapes=list(scratch),
        compiler_params=params(limit),
        cost_estimate=cost(args, outs, flops),
    )(*args, *fetched, *after)


def body(gate_act, key_act, value_act, decay_rate, residue, skip, out_weight):
    tokens, width = gate_act.shape
    columns = out_weight.shape[1]
    parts = lax.axis_size("context")
    decay_rate, residue, skip = decay_rate.T, residue.T, skip.reshape(1, width)
    modes = decay_rate.shape[0]
    place = lax.axis_index("context")
    here = lax.axis_index("tensor")
    f32, bf16 = jnp.float32, jnp.bfloat16

    def shape(dtype, *dims):
        return jax.ShapeDtypeStruct(dims, dtype)

    halves = width // LANES
    block = pltpu.VMEM((halves, tokens, LANES), f32)

    def by_half(kernel, args, outs, scratch, flops, limit):
        def spec(array):
            lead = array.shape[:-1]
            return pl.BlockSpec((*lead, LANES), lambda h: (*(0 for _ in lead), h))

        return pl.pallas_call(
            kernel,
            grid=(halves,),
            in_specs=[spec(a) for a in args],
            out_specs=[spec(o) for o in outs],
            out_shape=list(outs),
            scratch_shapes=list(scratch),
            compiler_params=params(limit),
            cost_estimate=cost(args, outs, flops),
        )(*args)

    row, spot = place // LOW, place % LOW
    column = pltpu.VMEM((tokens, LANES), f32)
    ends, states = by_half(
        ends_kernel,
        (key_act, value_act, decay_rate),
        (shape(bf16, LOW, modes, width), shape(f32, modes, CHUNKS, width)),
        (column, pltpu.VMEM((modes, LANES), f32)),
        2 * tokens * width * modes,
        58,
    )
    with jax.named_scope("states_along_z"):
        groups = [[x * LOW + z for z in range(LOW)] for x in range(X)]
        ends = lax.all_to_all(ends, "context", 0, 0, axis_index_groups=groups)
    (local,) = by_half(
        local_kernel,
        (gate_act, key_act, value_act, decay_rate, residue, skip, states),
        (shape(f32, tokens + 2 * modes, width),),
        (column, column),
        4 * tokens * width * modes,
        58,
    )
    before, rows = call(
        row_kernel,
        (jnp.stack([spot, jnp.int32(tokens)]), ends, decay_rate),
        (shape(f32, modes, width), shape(bf16, X, modes, width)),
        scalars=1,
    )
    with jax.named_scope("states_along_x"):
        groups = [[x * LOW + z for x in range(X)] for z in range(LOW)]
        rows = lax.all_to_all(rows, "context", 0, 0, axis_index_groups=groups)
    (gated,) = call(
        carry_kernel,
        (jnp.stack([row, spot * tokens, jnp.int32(tokens * LOW)]), rows, before, local),
        (shape(bf16, tokens, width),),
        (block, pltpu.VMEM((tokens, width), bf16), pltpu.SemaphoreType.DMA),
        flops=2 * tokens * width * modes,
        scalars=1,
        fetched=(gate_act,),
    )
    with jax.named_scope("along_z"):
        far = move(gated, dz=Z // 2)
    with jax.named_scope("own_along_y"):
        *near, other_weight = lax.cond(
            place < parts,
            lambda own, weight: (*[move(own, dy=d) for d in (2, 1, -1)], move(weight, dcore=1)),
            lambda own, weight: (own, own, own, weight),
            gated,
            out_weight,
        )
        near = [gated, *near]

    z_hi, y, core = here // (Y * CORES), here // CORES % Y, here % CORES
    ys = jnp.stack([y, (y + 2) % Y, (y - 1) % Y, (y + 1) % Y])
    order = (jnp.concatenate([z_hi * Y + ys, (1 - z_hi) * Y + jnp.arange(Y)]) * CORES + core).astype(jnp.int32)
    blocks = [weight.reshape(2 * Y * CORES, width, columns) for weight in (out_weight, other_weight)]
    sums, picked = shape(f32, tokens, columns), shape(bf16, Y, width, columns)
    mine_sum, other_sum, far_mine, far_other = call(
        near_product,
        (order, *near),
        (sums, sums, picked, picked),
        [pltpu.VMEM(picked.shape, bf16)] * 2 + [pltpu.SemaphoreType.DMA((2, 2 * Y))],
        flops=4 * tokens * Y * width * columns,
        scalars=1,
        fetched=blocks,
    )
    with jax.named_scope("far_along_y"):
        (far,) = call(copies_kernel, (far,), (shape(bf16, Y, tokens, width),), after=(mine_sum,))
        groups = [[(high * Y + y) * CORES + core for y in range(Y)] for high in range(Z // LOW) for core in range(CORES)]
        far = lax.all_to_all(far, "tensor", 0, 0, axis_index_groups=groups)
    work = 2 * tokens * Y * width * columns
    (other_sum,) = call(far_product, (far, far_other, other_sum), (shape(bf16, tokens, columns),), flops=work)
    with jax.named_scope("sum_swap"):
        from_other = move(other_sum, dcore=1)
    (mine_sum,) = call(far_product, (far, far_mine, mine_sum), (sums,), flops=work)
    return (mine_sum + from_other.astype(f32)).astype(bf16)


def solution(mesh):
    in_specs = (
        P("context", "tensor"),
        P("context", "tensor"),
        P("context", "tensor"),
        P("tensor", None),
        P("tensor", None),
        P("tensor"),
        P(None, "tensor"),
    )
    return jax.shard_map(body, mesh=mesh, in_specs=in_specs, out_specs=P("context", "tensor"), check_vma=False)
```

time: 107 us -> 98.4 us (0.920)
  waiting for transfers between devices: 34.4 us -> 16.4 us
  blocking collectives: 0 us -> 17.5 us
  starting transfers between devices: 57.7 us -> 46.2 us
  Pallas kernels: 6.86 us -> 14.6 us
  local copies, waits for them, and re-layouts: 6.47 us -> 1.77 us
    all_to_all x0 -> x1, blocking collectives: none -> 17.5 us  [body(): far = lax.all_to_all(far, 'tensor', 0, 0, axis_index_groups=groups)]
    ppermute x10 -> x6, waiting for transfers between devices: 22.1 us -> 6.74 us  [move(): return lax.ppermute(array, AXES, pairs)]
    ppermute x10 -> x6, starting transfers between devices: 41.8 us -> 29.1 us  [move(): return lax.ppermute(array, AXES, pairs)]
    pallas_call x5 -> x8, Pallas kernels: 6.86 us -> 14.6 us  [the longest x2 7.36 us: by_half(): pl.pallas_call(kernel, grid=(halves,), in_specs=[spec(a) for a in args],...]
    unnamed x16 -> x6, local copies, waits for them, and re-layouts: 5.13 us -> 1.77 us
    all_to_all x1 -> x2, waiting for transfers between devices: 12.4 us -> 9.68 us  [the longest x1 9.67 us: body(): ends = lax.all_to_all(ends, 'context', 0, 0, axis_index_groups=groups)]
    slice x2 -> x0, local copies, waits for them, and re-layouts: 1.34 us -> none  [the longest x1 1.27 us: body(): other[:half]]
    all_to_all x1 -> x2, starting transfers between devices: 15.9 us -> 17.1 us  [the longest x1 13.1 us: body(): ends = lax.all_to_all(ends, 'context', 0, 0, axis_index_groups=groups)]
  transfers between devices with their start and end apart: 11 -> 8, of which waited for: 6 -> 4; matrix products, arithmetic and copies ran while one was open for 2% -> 0% of each run, Pallas kernels for 4% -> 9%
where the time goes in v1:
time: 98.4 us; the launch traced here: 97.8 us
  starting transfers between devices  46.2 us (47%)
  blocking collectives  17.5 us (18%)
  waiting for transfers between devices  16.4 us (17%)
  Pallas kernels  14.6 us (15%)
  local copies, waits for them, and re-layouts  1.77 us (2%)
  other arithmetic  1.07 us (1%)
    ppermute x6, starting transfers between devices, move(): return lax.ppermute(array, AXES, pairs)  29.1 us
    all_to_all x1, blocking collectives, body(): far = lax.all_to_all(far, 'tensor', 0, 0, axis_index_groups=groups)  17.5 us
    all_to_all x1, starting transfers between devices, body(): ends = lax.all_to_all(ends, 'context', 0, 0, axis_index_groups=groups)  13.1 us
    all_to_all x1, waiting for transfers between devices, body(): ends = lax.all_to_all(ends, 'context', 0, 0, axis_index_groups=groups)  9.67 us
    pallas_call x2, Pallas kernels, by_half(): pl.pallas_call(kernel, grid=(halves,), in_specs=[spec(a) for a in args],...  7.36 us
    pallas_call x6, Pallas kernels, call(): pl.pallas_call(run, grid=(1,), in_specs=[*[pl.BlockSpec(memory_space=pltp...  7.27 us
    ppermute x6, waiting for transfers between devices, move(): return lax.ppermute(array, AXES, pairs)  6.74 us
    all_to_all x1, starting transfers between devices, body(): rows = lax.all_to_all(rows, 'context', 0, 0, axis_index_groups=groups)  4.01 us
  transfers between devices with their start and end apart: 8, of which 4 were waited for; matrix products, arithmetic and copies ran while one was open for 0% of the time, Pallas kernels for 9%

profile of v1, /device:TPU:1, one launch (start us, length us, event | category | flops | bytes accessed | tf_op | source)
XLA Modules:
  0.0 97.8 jit_solution(4331678255471521736)
XLA Ops:
  0.0 2.9 %shard_map.73 = (bf16[8,16,256]{2,1,0:T(8,128)(2,1)}, f32[16,8,256]{2,1,0:T(8,128)}) custom-call(bf16[512,256]{1,0:T(8,128)(2,1)} %key_ref.3, bf16[512,256]{1,0:T(8,128)(2,1)} %value_ref.3, f32[16,256]{1,0:T(8,128)} %bitcast.12), custom_call_target="tpu_custom_call" | custom-call | flops 4194304 | bytes 737280 | tf_op jit(solution)/shard_map/pallas_call | solution.py:246
  2.9 13.1 %all-to-all-start = ((bf16[8,16,256]{2,1,0:T(8,128)(2,1)}), bf16[8,16,256]{2,1,0:T(8,128)(2,1)S(1)}, u32[]{:S(2)}, u32[]{:S(2)}) async-start(bf16[8,16,256]{2,1,0:T(8,128)(2,1)} %get-tuple-element.29), calls=%async_computation | async-start | bytes 131072 | tf_op jit(solution)/shard_map/states_along_z/all_to_all | solution.py:269
  15.9 0.1 pad_add_fusion.1.refs_0_
  16.0 9.7 %all-to-all-done.refs_1_ = bf16[8,16,256]{2,1,0:T(8,128)(2,1)S(1)} async-done(((bf16[8,16,256]{2,1,0:T(8,128)(2,1)}), bf16[8,16,256]{2,1,0:T(8,128)(2,1)S(1)}, u32[]{:S(2)}, u32[]{:S(2)}) %all-to-all-start) | async-done | bytes 65568 | tf_op jit(solution)/shard_map/states_along_z/all_to_all | solution.py:269
  25.7 0.7 copy-done.2
  26.4 1.2 %shard_map.74 = (f32[16,256]{1,0:T(8,128)S(1)}, bf16[4,16,256]{2,1,0:T(8,128)(2,1)}) custom-call(s32[2]{0:T(128)S(1)} %pad_add_fusion.1.refs_0_, bf16[8,16,256]{2,1,0:T(8,128)(2,1)S(1)} %all-to-all-done.refs_1_, f32[16,256]{1,0:T(8,128)S(1)} %bitcast.14), custom_call_target="tpu_custom_call" | custom-call | bytes 131080 | tf_op jit(solution)/shard_map/pallas_call | solution.py:209
  27.6 4.0 %all-to-all-start.1 = ((bf16[4,16,256]{2,1,0:T(8,128)(2,1)}), bf16[4,16,256]{2,1,0:T(8,128)(2,1)S(1)}, u32[]{:S(2)}, u32[]{:S(2)}) async-start(bf16[4,16,256]{2,1,0:T(8,128)(2,1)} %get-tuple-element.30), calls=%async_computation.1 | async-start | bytes 65536 | tf_op jit(solution)/shard_map/states_along_x/all_to_all | solution.py:286
  31.6 0.1 pad_add_fusion.refs_0_
  31.7 4.5 %shard_map.75.refs_3_ = f32[544,256]{1,0:T(8,128)} custom-call(bf16[512,256]{1,0:T(8,128)(2,1)} %refs_4_.1, bf16[512,256]{1,0:T(8,128)(2,1)} %key_ref.3, bf16[512,256]{1,0:T(8,128)(2,1)} %value_ref.3, f32[16,256]{1,0:T(8,128)} %bitcast.13, f32[16,256]{1,0:T(8,128)} %bitcast.16, f32[1,256]{1,0:T(1,128)} %bitcast.17, f32[16,8,256]{2,1,0:T(8,128)} %get-tuple-element.32.states_ref), custom_call_target="tpu_custom_call" | custom-call | flops 8388608 | bytes 1508352 | tf_op jit(solution)/shard_map/pallas_call | solution.py:246
  36.2 0.0 all-to-all-done.1.refs_1_
  36.2 1.0 %copy-done = f32[544,256]{1,0:T(8,128)S(1)} copy-done((f32[544,256]{1,0:T(8,128)S(1)}, f32[544,256]{1,0:T(8,128)}, u32[]{:S(2)}) %copy-start) | copy-done | bytes 557080
  37.3 1.3 %shard_map.76.refs_1_ = bf16[512,256]{1,0:T(8,128)(2,1)S(1)} custom-call(s32[3]{0:T(128)S(1)} %pad_add_fusion.refs_0_, bf16[4,16,256]{2,1,0:T(8,128)(2,1)S(1)} %all-to-all-done.1.refs_1_, f32[16,256]{1,0:T(8,128)S(1)} %get-tuple-element.31.refs_2_, f32[544,256]{1,0:T(8,128)S(1)} %copy-done, bf16[512,256]{1,0:T(8,128)(2,1)S(1)} %copy-done.1), custom_call_target="tpu_custom_call" | custom-call | flops 4194304 | bytes 868364 | tf_op jit(solution)/shard_map/pallas_call | solution.py:209
  38.6 7.9 %collective-permute-start.4 = (bf16[512,256]{1,0:T(8,128)(2,1)S(1)}, bf16[512,256]{1,0:T(8,128)(2,1)S(1)}, u32[]{:S(2)}, u32[]{:S(2)}) collective-permute-start(bf16[512,256]{1,0:T(8,128)(2,1)S(1)} %shard_map.76.refs_1_), channel_id=1, source_target_pairs={{0,256},{32,288},{1,257},{33,289},{2,258},{34,290},{3,259},{35,291... | collective-permute-start | bytes 786440 | tf_op jit(solution)/shard_map/along_z/ppermute | solution.py:28
  46.5 0.1 add_add_fusion
  46.6 0.1 fusion.refs_0_
  46.7 22.8 %conditional.1 = (bf16[512,256]{1,0:T(8,128)(2,1)}, bf16[512,256]{1,0:T(8,128)(2,1)}, bf16[512,256]{1,0:T(8,128)(2,1)}, bf16[4096,256]{1,0:T(8,128)(2,1)}) conditional(s32[]{:T(128)} %convert_element_type.9, (bf16[512,256]{1,0:T(8,128)(2,1)S(1)}, bf16[4096,256]{1,0:T(8,128)(2,1)}) %tuple.13, (bf16[512,256]{1,0:T(8,128)(2,1)S(1)}, ...), branch_computations={%region_0.1_spmd, %region_1.2_spmd} | conditional | bytes 11534528 | solution.py:299
  46.7 5.4 %collective-permute-start.3 = (bf16[4096,256]{1,0:T(8,128)(2,1)}, bf16[4096,256]{1,0:T(8,128)(2,1)}, u32[]{:S(2)}, u32[]{:S(2)}) collective-permute-start(bf16[4096,256]{1,0:T(8,128)(2,1)} %get-tuple-element.16), channel_id=1, source_target_pairs={{0,32},{32,0},{1,33},{33,1},{2,34},{34,2},{3,35},{35,3},{4,36},{36... | collective-permute-start | bytes 6291464 | tf_op jit(solution)/shard_map/own_along_y/cond/branch_1_fun/ppermute | solution.py:28
  52.1 4.8 %collective-permute-start = (bf16[512,256]{1,0:T(8,128)(2,1)S(1)}, bf16[512,256]{1,0:T(8,128)(2,1)}, u32[]{:S(2)}, u32[]{:S(2)}) collective-permute-start(bf16[512,256]{1,0:T(8,128)(2,1)S(1)} %get-tuple-element.15), channel_id=1, source_target_pairs={{0,128},{32,160},{1,129},{33,161},{2,130},{34,162},{3,131},{35,163... | collective-permute-start | bytes 786440 | tf_op jit(solution)/shard_map/own_along_y/cond/branch_1_fun/ppermute | solution.py:28
  56.9 2.3 %collective-permute-start.1 = (bf16[512,256]{1,0:T(8,128)(2,1)S(1)}, bf16[512,256]{1,0:T(8,128)(2,1)}, u32[]{:S(2)}, u32[]{:S(2)}) collective-permute-start(bf16[512,256]{1,0:T(8,128)(2,1)S(1)} %get-tuple-element.15), channel_id=1, source_target_pairs={{0,64},{32,96},{1,65},{33,97},{2,66},{34,98},{3,67},{35,99},{4,68}... | collective-permute-start | bytes 786440 | tf_op jit(solution)/shard_map/own_along_y/cond/branch_1_fun/ppermute | solution.py:28
  59.3 4.2 %collective-permute-start.2 = (bf16[512,256]{1,0:T(8,128)(2,1)S(1)}, bf16[512,256]{1,0:T(8,128)(2,1)}, u32[]{:S(2)}, u32[]{:S(2)}) collective-permute-start(bf16[512,256]{1,0:T(8,128)(2,1)S(1)} %get-tuple-element.15), channel_id=1, source_target_pairs={{0,192},{32,224},{1,193},{33,225},{2,194},{34,226},{3,195},{35,227... | collective-permute-start | bytes 786440 | tf_op jit(solution)/shard_map/own_along_y/cond/branch_1_fun/ppermute | solution.py:28
  63.5 0.1 collective-permute-done
  63.5 5.9 %collective-permute-done.1 = bf16[512,256]{1,0:T(8,128)(2,1)} collective-permute-done((bf16[512,256]{1,0:T(8,128)(2,1)S(1)}, bf16[512,256]{1,0:T(8,128)(2,1)}, u32[]{:S(2)}, u32[]{:S(2)}) %collective-permute-start.1) | collective-permute-done | bytes 262176 | tf_op jit(solution)/shard_map/own_along_y/cond/branch_1_fun/ppermute | solution.py:28
  69.5 0.0 collective-permute-done.2
  69.5 0.0 collective-permute-done.3
  69.5 3.8 %shard_map.77 = (f32[512,256]{1,0:T(8,128)S(1)}, f32[512,256]{1,0:T(8,128)S(1)}, bf16[4,256,256]{2,1,0:T(8,128)(2,1)S(1)}, bf16[4,256,256]{2,1,0:T(8,128)(2,1)S(1)}) custom-call(s32[8]{0:T(128)S(1)} %fusion.refs_0_, bf16[512,256]{1,0:T(8,128)(2,1)S(1)} %shard_map.76.refs_1_, bf16[512,256]{1,0:T(8,128)(2,1)} %get-tuple-element.33.refs_2_, ...), custom_call_target="tpu_custom_call" | custom-call | flops 536870912 | bytes 3145760 | tf_op jit(solution)/shard_map/pallas_call | solution.py:209
  73.4 0.1 far_along_y.1
  73.4 17.5 %all_to_all.15.refs_0_ = bf16[4,512,256]{2,1,0:T(8,128)(2,1)S(1)} all-to-all(bf16[4,512,256]{2,1,0:T(8,128)(2,1)S(1)} %far_along_y.1), channel_id=1, replica_groups={{0,64,128,192},{32,96,160,224},{256,320,384,448},{288,352,416,480},{1,6..., dimensions={0} | all-to-all | bytes 2097152 | tf_op jit(solution)/shard_map/far_along_y/all_to_all | solution.py:325
  91.0 0.4 shard_map.79
  91.4 4.4 %collective-permute-start.5 = (bf16[512,256]{1,0:T(8,128)(2,1)S(1)}, bf16[512,256]{1,0:T(8,128)(2,1)S(1)}, u32[]{:S(2)}, u32[]{:S(2)}) collective-permute-start(bf16[512,256]{1,0:T(8,128)(2,1)S(1)} %shard_map.79), channel_id=1, source_target_pairs={{0,32},{32,0},{1,33},{33,1},{2,34},{34,2},{3,35},{35,3},{4,36},{36... | collective-permute-start | bytes 786440 | tf_op jit(solution)/shard_map/sum_swap/ppermute | solution.py:28
  95.9 0.4 shard_map.78
  96.3 0.7 collective-permute-done.5
  97.0 0.8 add_convert_fusion
  (5 shorter events, 0.0 us)
Async XLA Ops:
  0.0 36.2 %copy-start.1 = (bf16[512,256]{1,0:T(8,128)(2,1)S(1)}, bf16[512,256]{1,0:T(8,128)(2,1)}, u32[]{:S(2)}) copy-start(bf16[512,256]{1,0:T(8,128)(2,1)} %refs_4_.1) | copy-start | bytes 786436
  2.9 22.8 %all-to-all-start = ((bf16[8,16,256]{2,1,0:T(8,128)(2,1)}), bf16[8,16,256]{2,1,0:T(8,128)(2,1)S(1)}, u32[]{:S(2)}, u32[]{:S(2)}) async-start(bf16[8,16,256]{2,1,0:T(8,128)(2,1)} %get-tuple-element.29), calls=%async_computation | async-start | bytes 131072 | tf_op jit(solution)/shard_map/states_along_z/all_to_all | solution.py:269
  25.7 0.7 copy-start.2
  27.6 8.6 %all-to-all-start.1 = ((bf16[4,16,256]{2,1,0:T(8,128)(2,1)}), bf16[4,16,256]{2,1,0:T(8,128)(2,1)S(1)}, u32[]{:S(2)}, u32[]{:S(2)}) async-start(bf16[4,16,256]{2,1,0:T(8,128)(2,1)} %get-tuple-element.30), calls=%async_computation.1 | async-start | bytes 65536 | tf_op jit(solution)/shard_map/states_along_x/all_to_all | solution.py:286
  36.2 1.1 %copy-start = (f32[544,256]{1,0:T(8,128)S(1)}, f32[544,256]{1,0:T(8,128)}, u32[]{:S(2)}) copy-start(f32[544,256]{1,0:T(8,128)} %shard_map.75.refs_3_) | copy-start | bytes 1671172
  38.6 34.8 %collective-permute-start.4 = (bf16[512,256]{1,0:T(8,128)(2,1)S(1)}, bf16[512,256]{1,0:T(8,128)(2,1)S(1)}, u32[]{:S(2)}, u32[]{:S(2)}) collective-permute-start(bf16[512,256]{1,0:T(8,128)(2,1)S(1)} %shard_map.76.refs_1_), channel_id=1, source_target_pairs={{0,256},{32,288},{1,257},{33,289},{2,258},{34,290},{3,259},{35,291... | collective-permute-start | bytes 786440 | tf_op jit(solution)/shard_map/along_z/ppermute | solution.py:28
  46.7 22.8 %collective-permute-start.3 = (bf16[4096,256]{1,0:T(8,128)(2,1)}, bf16[4096,256]{1,0:T(8,128)(2,1)}, u32[]{:S(2)}, u32[]{:S(2)}) collective-permute-start(bf16[4096,256]{1,0:T(8,128)(2,1)} %get-tuple-element.16), channel_id=1, source_target_pairs={{0,32},{32,0},{1,33},{33,1},{2,34},{34,2},{3,35},{35,3},{4,36},{36... | collective-permute-start | bytes 6291464 | tf_op jit(solution)/shard_map/own_along_y/cond/branch_1_fun/ppermute | solution.py:28
  52.1 11.4 %collective-permute-start = (bf16[512,256]{1,0:T(8,128)(2,1)S(1)}, bf16[512,256]{1,0:T(8,128)(2,1)}, u32[]{:S(2)}, u32[]{:S(2)}) collective-permute-start(bf16[512,256]{1,0:T(8,128)(2,1)S(1)} %get-tuple-element.15), channel_id=1, source_target_pairs={{0,128},{32,160},{1,129},{33,161},{2,130},{34,162},{3,131},{35,163... | collective-permute-start | bytes 786440 | tf_op jit(solution)/shard_map/own_along_y/cond/branch_1_fun/ppermute | solution.py:28
  56.9 12.5 %collective-permute-start.1 = (bf16[512,256]{1,0:T(8,128)(2,1)S(1)}, bf16[512,256]{1,0:T(8,128)(2,1)}, u32[]{:S(2)}, u32[]{:S(2)}) collective-permute-start(bf16[512,256]{1,0:T(8,128)(2,1)S(1)} %get-tuple-element.15), channel_id=1, source_target_pairs={{0,64},{32,96},{1,65},{33,97},{2,66},{34,98},{3,67},{35,99},{4,68}... | collective-permute-start | bytes 786440 | tf_op jit(solution)/shard_map/own_along_y/cond/branch_1_fun/ppermute | solution.py:28
  59.3 10.2 %collective-permute-start.2 = (bf16[512,256]{1,0:T(8,128)(2,1)S(1)}, bf16[512,256]{1,0:T(8,128)(2,1)}, u32[]{:S(2)}, u32[]{:S(2)}) collective-permute-start(bf16[512,256]{1,0:T(8,128)(2,1)S(1)} %get-tuple-element.15), channel_id=1, source_target_pairs={{0,192},{32,224},{1,193},{33,225},{2,194},{34,226},{3,195},{35,227... | collective-permute-start | bytes 786440 | tf_op jit(solution)/shard_map/own_along_y/cond/branch_1_fun/ppermute | solution.py:28
  91.4 5.6 %collective-permute-start.5 = (bf16[512,256]{1,0:T(8,128)(2,1)S(1)}, bf16[512,256]{1,0:T(8,128)(2,1)S(1)}, u32[]{:S(2)}, u32[]{:S(2)}) collective-permute-start(bf16[512,256]{1,0:T(8,128)(2,1)S(1)} %shard_map.79), channel_id=1, source_target_pairs={{0,32},{32,0},{1,33},{33,1},{2,34},{34,2},{3,35},{35,3},{4,36},{36... | collective-permute-start | bytes 786440 | tf_op jit(solution)/shard_map/sum_swap/ppermute | solution.py:28

commit v2 on v1

--- a/solution.py
+++ b/solution.py
@@ -38,7 +38,7 @@
     return jnp.where(rows >= by, pltpu.roll(values, by, 0), 0.0)
 
 
-def ends_kernel(key_ref, value_ref, decay_ref, ends_ref, states_ref, x_scr, e_scr):
+def ends_kernel(spot_ref, key_ref, value_ref, decay_ref, ends_ref, states_ref, x_scr, e_scr):
     x_scr[...] = mixed_of(key_ref, value_ref)
     length = x_scr.shape[0] // CHUNKS
     modes = decay_ref.shape[0]
@@ -55,20 +55,21 @@
     for m in range(modes):
         states_ref[m] = states[m]
         e_scr[m : m + 1, :] = jnp.sum(jnp.exp(-(rate[m] * later)) * states[m], axis=0, keepdims=True)
-    ends_ref[...] = jnp.broadcast_to(e_scr[...].astype(jnp.bfloat16)[None], ends_ref.shape)
-
-
-def row_kernel(place_ref, ends_ref, decay_ref, before_ref, row_ref):
-    rates = decay_ref[...]
-    length = place_ref[1]
-    whole = jnp.exp(-(rates * length.astype(jnp.float32)))
-    before = total = jnp.zeros_like(rates)
+    spot, end, rates = spot_ref[0], e_scr[...], decay_ref[...]
     for q in range(ends_ref.shape[0]):
-        end = ends_ref[q].astype(jnp.float32)
-        before = jnp.where(q < place_ref[0], whole * before + end, before)
-        total = whole * total + end
-    before_ref[...] = before
-    row_ref[...] = jnp.broadcast_to(total.astype(jnp.bfloat16)[None], row_ref.shape)
+        to_row = jnp.maximum(q - 1 - spot, 0).astype(jnp.float32) * float(x_scr.shape[0])
+        to_next = (q + ends_ref.shape[0] - 1 - spot).astype(jnp.float32) * float(x_scr.shape[0])
+        ends_ref[q, :modes, :] = jnp.where(spot < q, jnp.exp(-(rates * to_row)) * end, 0.0).astype(jnp.bfloat16)
+        ends_ref[q, modes:, :] = (jnp.exp(-(rates * to_next)) * end).astype(jnp.bfloat16)
+
+
+def row_kernel(ends_ref, before_ref, row_ref):
+    modes = before_ref.shape[0]
+    total = ends_ref[0].astype(jnp.float32)
+    for q in range(1, ends_ref.shape[0]):
+        total += ends_ref[q].astype(jnp.float32)
+    before_ref[...] = total[:modes, :]
+    row_ref[...] = jnp.broadcast_to(total[modes:, :].astype(jnp.bfloat16)[None], row_ref.shape)
 
 
 def wide(values, m, cols):
@@ -81,35 +82,38 @@
     return terms[0]
 
 
-def local_kernel(gate_ref, key_ref, value_ref, decay_ref, residue_ref, skip_ref, states_ref, local_ref, x_scr, y_scr):
-    x_scr[...] = mixed_of(key_ref, value_ref)
-    tokens = x_scr.shape[0]
+def local_kernel(gate_ref, key_ref, value_ref, modal_ref, states_ref, local_ref, x_scr, y_scr):
+    mixed = mixed_of(key_ref, value_ref)
+    tokens = x_scr.shape[1]
     length = tokens // CHUNKS
-    rates = decay_ref[...]
-    coefs = residue_ref[...] * jnp.sqrt(2.0 * rates)
-    modes = rates.shape[0]
-    rate = [jnp.broadcast_to(rates[m : m + 1, :], (CHUNKS, LANES)) for m in range(modes)]
-    decay = [jnp.exp(-r) for r in rate]
-    coef = [jnp.broadcast_to(coefs[m : m + 1, :], (CHUNKS, LANES)) for m in range(modes)]
-    skip = jnp.broadcast_to(skip_ref[...], (CHUNKS, LANES))
-    first = []
-    for m in range(modes):
-        total = states_ref[m]
-        by = 1
-        while by < CHUNKS:
-            total = total + jnp.exp(-(rate[m] * float(length * by))) * shifted(total, by)
-            by *= 2
-        first.append(shifted(total, 1))
-
-    def step(t, states):
-        x = x_scr[pl.ds(t, CHUNKS, stride=length), :]
-        states = tuple(decay[m] * states[m] + x for m in range(modes))
-        total = add_up([coef[m] * states[m] for m in range(modes)])
-        y_scr[pl.ds(t, CHUNKS, stride=length), :] = total + skip * x
-        return states
-
-    lax.fori_loop(0, length, step, tuple(first), unroll=2)
-    local_ref[:tokens, :] = gate_ref[...].astype(jnp.float32) * y_scr[...]
+    modes = states_ref.shape[0]
+    rates = modal_ref[:modes, :]
+    coefs = modal_ref[modes : 2 * modes, :] * jnp.sqrt(2.0 * rates)
+    for half in range(x_scr.shape[0]):
+        cols = slice(half * LANES, (half + 1) * LANES)
+        x_scr[half] = mixed[:, cols]
+        rate = [wide(rates, m, cols) for m in range(modes)]
+        decay = [jnp.exp(-r) for r in rate]
+        coef = [wide(coefs, m, cols) for m in range(modes)]
+        skip = wide(modal_ref[2 * modes : 2 * modes + 1, :], 0, cols)
+        first = []
+        for m in range(modes):
+            total = states_ref[m, :, cols]
+            by = 1
+            while by < CHUNKS:
+                total = total + jnp.exp(-(rate[m] * float(length * by))) * shifted(total, by)
+                by *= 2
+            first.append(shifted(total, 1))
+
+        def step(t, states):
+            x = x_scr[half, pl.ds(t, CHUNKS, stride=length), :]
+            states = tuple(decay[m] * states[m] + x for m in range(modes))
+            total = add_up([coef[m] * states[m] for m in range(modes)])
+            y_scr[half, pl.ds(t, CHUNKS, stride=length), :] = total + skip * x
+            return states
+
+        lax.fori_loop(0, length, step, tuple(first), unroll=2)
+        local_ref[:tokens, cols] = gate_ref[:, cols].astype(jnp.float32) * y_scr[half]
     local_ref[tokens : tokens + modes, :] = rates
     local_ref[tokens + modes :, :] = coefs
 
@@ -136,12 +140,12 @@
     tokens = y_scr.shape[1]
     modes = (local_ref.shape[0] - tokens) // 2
     rates, coefs = local_ref[tokens : tokens + modes, :], local_ref[tokens + modes :, :]
-    row, here, length = place_ref[0], place_ref[1], place_ref[2]
+    row, length = place_ref[0], place_ref[1]
     whole = jnp.exp(-(rates * length.astype(jnp.float32)))
     carried = jnp.zeros_like(rates)
     for q in range(rows_ref.shape[0]):
         carried = jnp.where(q < row, whole * carried + rows_ref[q].astype(jnp.float32), carried)
-    start = coefs * (before_ref[...] + jnp.exp(-(rates * here.astype(jnp.float32))) * carried)
+    start = coefs * (before_ref[...] + carried)
     from_states(rates, start, y_scr, tokens)
     fetch.wait()
     for half in range(y_scr.shape[0]):
@@ -155,28 +159,19 @@
         out_ref[i] = in_ref[...]
 
 
-def near_product(
-    order_ref, p0, p1, p2, p3, mine_hbm, other_hbm, mine_out, other_out, far_mine, far_other, near_mine, near_other, arrived
-):
-    sides = ((mine_hbm, near_mine, far_mine), (other_hbm, near_other, far_other))
-
-    def copy(side, i):
-        source, near, far = sides[side]
-        target = near.at[i] if i < Y else far.at[i - Y]
-        return pltpu.make_async_copy(source.at[order_ref[i]], target, arrived.at[side, i])
-
-    for i in range(2 * Y):
-        for side in range(2):
-            copy(side, i).start()
-    totals = [0.0, 0.0]
-    for i, piece in enumerate((p0, p1, p2, p3)):
-        for side in range(2):
-            copy(side, i).wait()
-            totals[side] += jnp.dot(piece[...], sides[side][1][i], preferred_element_type=jnp.float32)
-    mine_out[...], other_out[...] = totals
-    for i in range(Y, 2 * Y):
-        for side in range(2):
-            copy(side, i).wait()
+def near_product(order_ref, p0, p1, p2, p3, mine_ref, other_ref, mine_out, other_out, far_mine, far_other):
+    for weight, out, far in ((mine_ref, mine_out, far_mine), (other_ref, other_out, far_other)):
+        total = jnp.zeros(out.shape, jnp.float32)
+        for i, piece in enumerate((p0, p1, p2, p3)):
+            total += jnp.dot(piece[...], block_of(weight, order_ref[i]), preferred_element_type=jnp.float32)
+        out[...] = total
+        for i in range(Y):
+            far[i] = block_of(weight, order_ref[Y + i])
+
+
+def block_of(weight_ref, index):
+    height = weight_ref.shape[0] // (2 * Y * CORES)
+    return weight_ref[pl.ds(pl.multiple_of(index * height, height), height), :]
 
 
 def far_product(pieces_ref, weight_ref, start_ref, out_ref):
@@ -238,55 +233,40 @@
     halves = width // LANES
     block = pltpu.VMEM((halves, tokens, LANES), f32)
 
-    def by_half(kernel, args, outs, scratch, flops, limit):
-        def spec(array):
-            lead = array.shape[:-1]
-            return pl.BlockSpec((*lead, LANES), lambda h: (*(0 for _ in lead), h))
-
-        return pl.pallas_call(
-            kernel,
-            grid=(halves,),
-            in_specs=[spec(a) for a in args],
-            out_specs=[spec(o) for o in outs],
-            out_shape=list(outs),
-            scratch_shapes=list(scratch),
-            compiler_params=params(limit),
-            cost_estimate=cost(args, outs, flops),
-        )(*args)
-
     row, spot = place // LOW, place % LOW
-    column = pltpu.VMEM((tokens, LANES), f32)
-    ends, states = by_half(
+    ends_out = (shape(bf16, LOW, 2 * modes, width), shape(f32, modes, CHUNKS, width))
+    ends, states = pl.pallas_call(
         ends_kernel,
-        (key_act, value_act, decay_rate),
-        (shape(bf16, LOW, modes, width), shape(f32, modes, CHUNKS, width)),
-        (column, pltpu.VMEM((modes, LANES), f32)),
-        2 * tokens * width * modes,
-        58,
-    )
+        grid=(halves,),
+        in_specs=[
+            pl.BlockSpec(memory_space=pltpu.SMEM),
+            *[pl.BlockSpec((rows, LANES), lambda h: (0, h)) for rows in (tokens, tokens, modes)],
+        ],
+        out_specs=[pl.BlockSpec((*out.shape[:2], LANES), lambda h: (0, 0, h)) for out in ends_out],
+        out_shape=list(ends_out),
+        scratch_shapes=[pltpu.VMEM((tokens, LANES), f32), pltpu.VMEM((modes, LANES), f32)],
+        compiler_params=params(58),
+        cost_estimate=cost((key_act, value_act), ends_out, 2 * tokens * width * modes),
+    )(spot.reshape(1), key_act, value_act, decay_rate)
     with jax.named_scope("states_along_z"):
         groups = [[x * LOW + z for z in range(LOW)] for x in range(X)]
         ends = lax.all_to_all(ends, "context", 0, 0, axis_index_groups=groups)
-    (local,) = by_half(
+    (local,) = call(
         local_kernel,
-        (gate_act, key_act, value_act, decay_rate, residue, skip, states),
+        (gate_act, key_act, value_act, jnp.concatenate([decay_rate, residue, skip]), states),
         (shape(f32, tokens + 2 * modes, width),),
-        (column, column),
-        4 * tokens * width * modes,
-        58,
+        (block, block),
+        flops=4 * tokens * width * modes,
     )
     before, rows = call(
-        row_kernel,
-        (jnp.stack([spot, jnp.int32(tokens)]), ends, decay_rate),
-        (shape(f32, modes, width), shape(bf16, X, modes, width)),
-        scalars=1,
+        row_kernel, (ends,), (shape(f32, modes, width), shape(bf16, X, modes, width)), after=(local,)
     )
     with jax.named_scope("states_along_x"):
         groups = [[x * LOW + z for x in range(X)] for z in range(LOW)]
         rows = lax.all_to_all(rows, "context", 0, 0, axis_index_groups=groups)
     (gated,) = call(
         carry_kernel,
-        (jnp.stack([row, spot * tokens, jnp.int32(tokens * LOW)]), rows, before, local),
+        (jnp.stack([row, jnp.int32(tokens * LOW)]), rows, before, local),
         (shape(bf16, tokens, width),),
         (block, pltpu.VMEM((tokens, width), bf16), pltpu.SemaphoreType.DMA),
         flops=2 * tokens * width * modes,
@@ -308,22 +288,20 @@
     z_hi, y, core = here // (Y * CORES), here // CORES % Y, here % CORES
     ys = jnp.stack([y, (y + 2) % Y, (y - 1) % Y, (y + 1) % Y])
     order = (jnp.concatenate([z_hi * Y + ys, (1 - z_hi) * Y + jnp.arange(Y)]) * CORES + core).astype(jnp.int32)
-    blocks = [weight.reshape(2 * Y * CORES, width, columns) for weight in (out_weight, other_weight)]
-    sums, picked = shape(f32, tokens, columns), shape(bf16, Y, width, columns)
+    sums = shape(f32, tokens, columns)
+    work = 2 * tokens * Y * width * columns
+    picked = shape(bf16, Y, width, columns)
     mine_sum, other_sum, far_mine, far_other = call(
         near_product,
-        (order, *near),
+        (order, *near, out_weight, other_weight),
         (sums, sums, picked, picked),
-        [pltpu.VMEM(picked.shape, bf16)] * 2 + [pltpu.SemaphoreType.DMA((2, 2 * Y))],
-        flops=4 * tokens * Y * width * columns,
+        flops=2 * work,
         scalars=1,
-        fetched=blocks,
     )
     with jax.named_scope("far_along_y"):
         (far,) = call(copies_kernel, (far,), (shape(bf16, Y, tokens, width),), after=(mine_sum,))
         groups = [[(high * Y + y) * CORES + core for y in range(Y)] for high in range(Z // LOW) for core in range(CORES)]
         far = lax.all_to_all(far, "tensor", 0, 0, axis_index_groups=groups)
-    work = 2 * tokens * Y * width * columns
     (other_sum,) = call(far_product, (far, far_other, other_sum), (shape(bf16, tokens, columns),), flops=work)
     with jax.named_scope("sum_swap"):
         from_other = move(other_sum, dcore=1)

time: 98.4 us -> 95.9 us (0.975)
  Pallas kernels: 14.6 us -> 10.9 us
  waiting for transfers between devices: 16.4 us -> 14.2 us
  local copies, waits for them, and re-layouts: 1.77 us -> 3.76 us
    all_to_all x1, waiting for transfers between devices: 9.67 us -> 3.24 us  [body(): ends = lax.all_to_all(ends, 'context', 0, 0, axis_index_groups=groups)]
    pallas_call x2 -> x1, Pallas kernels: 7.36 us -> 2.89 us  [body(): pl.pallas_call(ends_kernel, grid=(halves,), in_specs=[pl.BlockSpec(memory...]
    all_to_all x1, waiting for transfers between devices: 0.01 us -> 4.2 us  [body(): rows = lax.all_to_all(rows, 'context', 0, 0, axis_index_groups=groups)]
    unnamed x6 -> x12, local copies, waits for them, and re-layouts: 1.77 us -> 3.76 us
    pallas_call x6 -> x7, Pallas kernels: 7.27 us -> 8.04 us  [call(): pl.pallas_call(run, grid=(1,), in_specs=[*[pl.BlockSpec(memory_space=pltp...]
  transfers between devices with their start and end apart: 8 -> 8, of which waited for: 4 -> 5; matrix products, arithmetic and copies ran while one was open for 0% -> 1% of each run, Pallas kernels for 9% -> 6%
where the time goes in v2:
time: 95.9 us; the launch traced here: 95.2 us
  starting transfers between devices  47 us (49%)
  blocking collectives  17.5 us (18%)
  waiting for transfers between devices  14.2 us (15%)
  Pallas kernels  10.9 us (11%)
  local copies, waits for them, and re-layouts  3.76 us (4%)
  other arithmetic  1.75 us (2%)
    ppermute x6, starting transfers between devices, move(): return lax.ppermute(array, AXES, pairs)  29.9 us
    all_to_all x1, blocking collectives, body(): far = lax.all_to_all(far, 'tensor', 0, 0, axis_index_groups=groups)  17.5 us
    all_to_all x1, starting transfers between devices, body(): ends = lax.all_to_all(ends, 'context', 0, 0, axis_index_groups=groups)  13.1 us
    pallas_call x7, Pallas kernels, call(): pl.pallas_call(run, grid=(1,), in_specs=[*[pl.BlockSpec(memory_space=pltp...  8.04 us
    ppermute x6, waiting for transfers between devices, move(): return lax.ppermute(array, AXES, pairs)  6.74 us
    all_to_all x1, waiting for transfers between devices, body(): rows = lax.all_to_all(rows, 'context', 0, 0, axis_index_groups=groups)  4.2 us
    all_to_all x1, starting transfers between devices, body(): rows = lax.all_to_all(rows, 'context', 0, 0, axis_index_groups=groups)  4.01 us
    unnamed x12, local copies, waits for them, and re-layouts  3.76 us
  transfers between devices with their start and end apart: 8, of which 5 were waited for; matrix products, arithmetic and copies ran while one was open for 1% of the time, Pallas kernels for 6%

profile of v2, /device:TPU:1, one launch (start us, length us, event | category | flops | bytes accessed | tf_op | source)
XLA Modules:
  0.0 95.2 jit_solution(638271155767727962)
XLA Ops:
  0.0 2.9 %shard_map.73 = (bf16[8,32,256]{2,1,0:T(8,128)(2,1)}, f32[16,8,256]{2,1,0:T(8,128)}) custom-call(s32[1]{0:T(128)} %bitcast.1.spot_ref, bf16[512,256]{1,0:T(8,128)(2,1)} %refs_1_.1, bf16[512,256]{1,0:T(8,128)(2,1)} %refs_2_.1, f32[16,256]{1,0:T(8,128)} %bitcast.9), custom_call_target="tpu_custom_call" | custom-call | flops 4194304 | bytes 786432 | tf_op jit(solution)/shard_map/pallas_call | solution.py:238
  2.9 13.1 %all-to-all-start = ((bf16[8,32,256]{2,1,0:T(8,128)(2,1)}), bf16[8,32,256]{2,1,0:T(8,128)(2,1)S(1)}, u32[]{:S(2)}, u32[]{:S(2)}) async-start(bf16[8,32,256]{2,1,0:T(8,128)(2,1)} %get-tuple-element.29), calls=%async_computation | async-start | bytes 262144 | tf_op jit(solution)/shard_map/states_along_z/all_to_all | solution.py:253
  16.0 0.8 pad_maximum_fusion.refs_3_
  16.7 0.9 copy-done
  17.7 0.9 copy-done.1
  18.6 0.9 copy-done.2
  19.6 0.9 copy-done.4
  20.5 2.6 %shard_map.74.refs_1_.refs_3_ = f32[544,256]{1,0:T(8,128)S(1)} custom-call(bf16[512,256]{1,0:T(8,128)(2,1)S(1)} %copy-done.2, bf16[512,256]{1,0:T(8,128)(2,1)S(1)} %copy-done, bf16[512,256]{1,0:T(8,128)(2,1)S(1)} %copy-done.1, f32[33,256]{1,0:T(8,128)S(1)} %pad_maximum_fusion.refs_3_, f32[16,8,256]{2,1,0:T(8,128)S(1)} %copy-done.4), custom_call_target="tpu_custom_call" | custom-call | flops 8388608 | bytes 1508352 | tf_op jit(solution)/shard_map/pallas_call | solution.py:204
  23.1 3.2 %all-to-all-done.refs_0_ = bf16[8,32,256]{2,1,0:T(8,128)(2,1)S(1)} async-done(((bf16[8,32,256]{2,1,0:T(8,128)(2,1)}), bf16[8,32,256]{2,1,0:T(8,128)(2,1)S(1)}, u32[]{:S(2)}, u32[]{:S(2)}) %all-to-all-start) | async-done | bytes 131104 | tf_op jit(solution)/shard_map/states_along_z/all_to_all | solution.py:253
  26.3 0.6 shard_map.75
  26.9 4.0 %all-to-all-start.1 = ((bf16[4,16,256]{2,1,0:T(8,128)(2,1)}), bf16[4,16,256]{2,1,0:T(8,128)(2,1)S(1)}, u32[]{:S(2)}, u32[]{:S(2)}) async-start(bf16[4,16,256]{2,1,0:T(8,128)(2,1)} %get-tuple-element.31), calls=%async_computation.1 | async-start | bytes 65536 | tf_op jit(solution)/shard_map/states_along_x/all_to_all | solution.py:266
  30.9 0.1 pad_add_fusion.refs_0_
  31.0 4.2 %all-to-all-done.1.refs_1_ = bf16[4,16,256]{2,1,0:T(8,128)(2,1)S(1)} async-done(((bf16[4,16,256]{2,1,0:T(8,128)(2,1)}), bf16[4,16,256]{2,1,0:T(8,128)(2,1)S(1)}, u32[]{:S(2)}, u32[]{:S(2)}) %all-to-all-start.1) | async-done | bytes 32800 | tf_op jit(solution)/shard_map/states_along_x/all_to_all | solution.py:266
  35.2 1.3 %shard_map.76.refs_1_ = bf16[512,256]{1,0:T(8,128)(2,1)S(1)} custom-call(s32[2]{0:T(128)S(1)} %pad_add_fusion.refs_0_, bf16[4,16,256]{2,1,0:T(8,128)(2,1)S(1)} %all-to-all-done.1.refs_1_, f32[16,256]{1,0:T(8,128)S(1)} %get-tuple-element.32.refs_2_, f32[544,256]{1,0:T(8,128)S(1)} %shard_map.74.refs_1_.refs_3_, bf16[512,256]{1,0:T(8,128)(2,1)S(1)} %copy-done.3), custom_call_target="tpu_custom_call" | custom-call | flops 4194304 | bytes 868360 | tf_op jit(solution)/shard_map/pallas_call | solution.py:204
  36.5 7.9 %collective-permute-start.4 = (bf16[512,256]{1,0:T(8,128)(2,1)S(1)}, bf16[512,256]{1,0:T(8,128)(2,1)S(1)}, u32[]{:S(2)}, u32[]{:S(2)}) collective-permute-start(bf16[512,256]{1,0:T(8,128)(2,1)S(1)} %shard_map.76.refs_1_), channel_id=1, source_target_pairs={{0,256},{32,288},{1,257},{33,289},{2,258},{34,290},{3,259},{35,291... | collective-permute-start | bytes 786440 | tf_op jit(solution)/shard_map/along_z/ppermute | solution.py:28
  44.5 0.1 add_add_fusion
  44.6 0.1 fusion.refs_0_
  44.7 23.6 %conditional.1 = (bf16[512,256]{1,0:T(8,128)(2,1)}, bf16[512,256]{1,0:T(8,128)(2,1)}, bf16[512,256]{1,0:T(8,128)(2,1)}, bf16[4096,256]{1,0:T(8,128)(2,1)}) conditional(s32[]{:T(128)} %convert_element_type.9, (bf16[512,256]{1,0:T(8,128)(2,1)S(1)}, bf16[4096,256]{1,0:T(8,128)(2,1)S(1)}) %tuple.17, (bf16[512,256]{1,0:T(8,128)(2,1)S(1)}, ...), branch_computations={%region_0.1_spmd, %region_1.2_spmd} | conditional | bytes 11534528 | solution.py:279
  44.7 6.2 %collective-permute-start.3 = (bf16[4096,256]{1,0:T(8,128)(2,1)S(1)}, bf16[4096,256]{1,0:T(8,128)(2,1)}, u32[]{:S(2)}, u32[]{:S(2)}) collective-permute-start(bf16[4096,256]{1,0:T(8,128)(2,1)S(1)} %get-tuple-element.16), channel_id=1, source_target_pairs={{0,32},{32,0},{1,33},{33,1},{2,34},{34,2},{3,35},{35,3},{4,36},{36... | collective-permute-start | bytes 6291464 | tf_op jit(solution)/shard_map/own_along_y/cond/branch_1_fun/ppermute | solution.py:28
  50.8 4.8 %collective-permute-start = (bf16[512,256]{1,0:T(8,128)(2,1)S(1)}, bf16[512,256]{1,0:T(8,128)(2,1)}, u32[]{:S(2)}, u32[]{:S(2)}) collective-permute-start(bf16[512,256]{1,0:T(8,128)(2,1)S(1)} %get-tuple-element.15), channel_id=1, source_target_pairs={{0,128},{32,160},{1,129},{33,161},{2,130},{34,162},{3,131},{35,163... | collective-permute-start | bytes 786440 | tf_op jit(solution)/shard_map/own_along_y/cond/branch_1_fun/ppermute | solution.py:28
  55.7 2.3 %collective-permute-start.1 = (bf16[512,256]{1,0:T(8,128)(2,1)S(1)}, bf16[512,256]{1,0:T(8,128)(2,1)}, u32[]{:S(2)}, u32[]{:S(2)}) collective-permute-start(bf16[512,256]{1,0:T(8,128)(2,1)S(1)} %get-tuple-element.15), channel_id=1, source_target_pairs={{0,64},{32,96},{1,65},{33,97},{2,66},{34,98},{3,67},{35,99},{4,68}... | collective-permute-start | bytes 786440 | tf_op jit(solution)/shard_map/own_along_y/cond/branch_1_fun/ppermute | solution.py:28
  58.0 4.2 %collective-permute-start.2 = (bf16[512,256]{1,0:T(8,128)(2,1)S(1)}, bf16[512,256]{1,0:T(8,128)(2,1)}, u32[]{:S(2)}, u32[]{:S(2)}) collective-permute-start(bf16[512,256]{1,0:T(8,128)(2,1)S(1)} %get-tuple-element.15), channel_id=1, source_target_pairs={{0,192},{32,224},{1,193},{33,225},{2,194},{34,226},{3,195},{35,227... | collective-permute-start | bytes 786440 | tf_op jit(solution)/shard_map/own_along_y/cond/branch_1_fun/ppermute | solution.py:28
  62.2 0.1 collective-permute-done
  62.3 5.9 %collective-permute-done.1 = bf16[512,256]{1,0:T(8,128)(2,1)} collective-permute-done((bf16[512,256]{1,0:T(8,128)(2,1)S(1)}, bf16[512,256]{1,0:T(8,128)(2,1)}, u32[]{:S(2)}, u32[]{:S(2)}) %collective-permute-start.1) | collective-permute-done | bytes 262176 | tf_op jit(solution)/shard_map/own_along_y/cond/branch_1_fun/ppermute | solution.py:28
  68.2 2.6 %shard_map.77 = (f32[512,256]{1,0:T(8,128)S(1)}, f32[512,256]{1,0:T(8,128)S(1)}, bf16[4,256,256]{2,1,0:T(8,128)(2,1)S(1)}, bf16[4,256,256]{2,1,0:T(8,128)(2,1)S(1)}) custom-call(s32[8]{0:T(128)S(1)} %fusion.refs_0_, bf16[512,256]{1,0:T(8,128)(2,1)S(1)} %shard_map.76.refs_1_, bf16[512,256]{1,0:T(8,128)(2,1)} %get-tuple-element.33.refs_2_, ...), custom_call_target="tpu_custom_call" | custom-call | flops 536870912 | bytes 7340064 | tf_op jit(solution)/shard_map/pallas_call | solution.py:204
  70.8 0.1 far_along_y.1
  70.9 17.5 %all_to_all.15.refs_0_ = bf16[4,512,256]{2,1,0:T(8,128)(2,1)S(1)} all-to-all(bf16[4,512,256]{2,1,0:T(8,128)(2,1)S(1)} %far_along_y.1), channel_id=1, replica_groups={{0,64,128,192},{32,96,160,224},{256,320,384,448},{288,352,416,480},{1,6..., dimensions={0} | all-to-all | bytes 2097152 | tf_op jit(solution)/shard_map/far_along_y/all_to_all | solution.py:304
  88.4 0.4 shard_map.79
  88.9 4.4 %collective-permute-start.5 = (bf16[512,256]{1,0:T(8,128)(2,1)S(1)}, bf16[512,256]{1,0:T(8,128)(2,1)S(1)}, u32[]{:S(2)}, u32[]{:S(2)}) collective-permute-start(bf16[512,256]{1,0:T(8,128)(2,1)S(1)} %shard_map.79), channel_id=1, source_target_pairs={{0,32},{32,0},{1,33},{33,1},{2,34},{34,2},{3,35},{35,3},{4,36},{36... | collective-permute-start | bytes 786440 | tf_op jit(solution)/shard_map/sum_swap/ppermute | solution.py:28
  93.3 0.4 shard_map.78
  93.8 0.7 collective-permute-done.5
  94.5 0.8 add_convert_fusion
  (11 shorter events, 0.0 us)
Async XLA Ops:
  0.0 35.2 %copy-start.3 = (bf16[512,256]{1,0:T(8,128)(2,1)S(1)}, bf16[512,256]{1,0:T(8,128)(2,1)}, u32[]{:S(2)}) copy-start(bf16[512,256]{1,0:T(8,128)(2,1)} %refs_4_.1) | copy-start | bytes 786436
  2.9 23.4 %all-to-all-start = ((bf16[8,32,256]{2,1,0:T(8,128)(2,1)}), bf16[8,32,256]{2,1,0:T(8,128)(2,1)S(1)}, u32[]{:S(2)}, u32[]{:S(2)}) async-start(bf16[8,32,256]{2,1,0:T(8,128)(2,1)} %get-tuple-element.29), calls=%async_computation | async-start | bytes 262144 | tf_op jit(solution)/shard_map/states_along_z/all_to_all | solution.py:253
  16.7 0.9 copy-start
  17.7 0.9 copy-start.1
  18.6 0.9 copy-start.2
  19.6 0.9 copy-start.4
  20.5 24.2 %copy-start.5 = (bf16[4096,256]{1,0:T(8,128)(2,1)S(1)}, bf16[4096,256]{1,0:T(8,128)(2,1)}, u32[]{:S(2)}) copy-start(bf16[4096,256]{1,0:T(8,128)(2,1)} %refs_5_.1) | copy-start | bytes 6291460
  26.9 8.3 %all-to-all-start.1 = ((bf16[4,16,256]{2,1,0:T(8,128)(2,1)}), bf16[4,16,256]{2,1,0:T(8,128)(2,1)S(1)}, u32[]{:S(2)}, u32[]{:S(2)}) async-start(bf16[4,16,256]{2,1,0:T(8,128)(2,1)} %get-tuple-element.31), calls=%async_computation.1 | async-start | bytes 65536 | tf_op jit(solution)/shard_map/states_along_x/all_to_all | solution.py:266
  36.5 34.3 %collective-permute-start.4 = (bf16[512,256]{1,0:T(8,128)(2,1)S(1)}, bf16[512,256]{1,0:T(8,128)(2,1)S(1)}, u32[]{:S(2)}, u32[]{:S(2)}) collective-permute-start(bf16[512,256]{1,0:T(8,128)(2,1)S(1)} %shard_map.76.refs_1_), channel_id=1, source_target_pairs={{0,256},{32,288},{1,257},{33,289},{2,258},{34,290},{3,259},{35,291... | collective-permute-start | bytes 786440 | tf_op jit(solution)/shard_map/along_z/ppermute | solution.py:28
  44.7 23.6 %collective-permute-start.3 = (bf16[4096,256]{1,0:T(8,128)(2,1)S(1)}, bf16[4096,256]{1,0:T(8,128)(2,1)}, u32[]{:S(2)}, u32[]{:S(2)}) collective-permute-start(bf16[4096,256]{1,0:T(8,128)(2,1)S(1)} %get-tuple-element.16), channel_id=1, source_target_pairs={{0,32},{32,0},{1,33},{33,1},{2,34},{34,2},{3,35},{35,3},{4,36},{36... | collective-permute-start | bytes 6291464 | tf_op jit(solution)/shard_map/own_along_y/cond/branch_1_fun/ppermute | solution.py:28
  50.8 11.4 %collective-permute-start = (bf16[512,256]{1,0:T(8,128)(2,1)S(1)}, bf16[512,256]{1,0:T(8,128)(2,1)}, u32[]{:S(2)}, u32[]{:S(2)}) collective-permute-start(bf16[512,256]{1,0:T(8,128)(2,1)S(1)} %get-tuple-element.15), channel_id=1, source_target_pairs={{0,128},{32,160},{1,129},{33,161},{2,130},{34,162},{3,131},{35,163... | collective-permute-start | bytes 786440 | tf_op jit(solution)/shard_map/own_along_y/cond/branch_1_fun/ppermute | solution.py:28
  55.7 12.5 %collective-permute-start.1 = (bf16[512,256]{1,0:T(8,128)(2,1)S(1)}, bf16[512,256]{1,0:T(8,128)(2,1)}, u32[]{:S(2)}, u32[]{:S(2)}) collective-permute-start(bf16[512,256]{1,0:T(8,128)(2,1)S(1)} %get-tuple-element.15), channel_id=1, source_target_pairs={{0,64},{32,96},{1,65},{33,97},{2,66},{34,98},{3,67},{35,99},{4,68}... | collective-permute-start | bytes 786440 | tf_op jit(solution)/shard_map/own_along_y/cond/branch_1_fun/ppermute | solution.py:28
  58.0 10.2 %collective-permute-start.2 = (bf16[512,256]{1,0:T(8,128)(2,1)S(1)}, bf16[512,256]{1,0:T(8,128)(2,1)}, u32[]{:S(2)}, u32[]{:S(2)}) collective-permute-start(bf16[512,256]{1,0:T(8,128)(2,1)S(1)} %get-tuple-element.15), channel_id=1, source_target_pairs={{0,192},{32,224},{1,193},{33,225},{2,194},{34,226},{3,195},{35,227... | collective-permute-start | bytes 786440 | tf_op jit(solution)/shard_map/own_along_y/cond/branch_1_fun/ppermute | solution.py:28
  88.9 5.6 %collective-permute-start.5 = (bf16[512,256]{1,0:T(8,128)(2,1)S(1)}, bf16[512,256]{1,0:T(8,128)(2,1)S(1)}, u32[]{:S(2)}, u32[]{:S(2)}) collective-permute-start(bf16[512,256]{1,0:T(8,128)(2,1)S(1)} %shard_map.79), channel_id=1, source_target_pairs={{0,32},{32,0},{1,33},{33,1},{2,34},{34,2},{3,35},{35,3},{4,36},{36... | collective-permute-start | bytes 786440 | tf_op jit(solution)/shard_map/sum_swap/ppermute | solution.py:28

commit v3 on v2

--- a/solution.py
+++ b/solution.py
@@ -9,6 +9,7 @@
 LANES = 128
 Z, Y, CORES, X = 16, 4, 2, 4
 LOW = Z // 2
+AWAY = (0, 2, 1, -1)
 AXES = ("tensor", "context")
 
 
@@ -38,7 +39,7 @@
     return jnp.where(rows >= by, pltpu.roll(values, by, 0), 0.0)
 
 
-def ends_kernel(spot_ref, key_ref, value_ref, decay_ref, ends_ref, states_ref, x_scr, e_scr):
+def ends_kernel(key_ref, value_ref, decay_ref, ends_ref, states_ref, x_scr, e_scr):
     x_scr[...] = mixed_of(key_ref, value_ref)
     length = x_scr.shape[0] // CHUNKS
     modes = decay_ref.shape[0]
@@ -55,7 +56,8 @@
     for m in range(modes):
         states_ref[m] = states[m]
         e_scr[m : m + 1, :] = jnp.sum(jnp.exp(-(rate[m] * later)) * states[m], axis=0, keepdims=True)
-    spot, end, rates = spot_ref[0], e_scr[...], decay_ref[...]
+    spot = lax.rem(lax.axis_index("context"), LOW)
+    end, rates = e_scr[...], decay_ref[...]
     for q in range(ends_ref.shape[0]):
         to_row = jnp.maximum(q - 1 - spot, 0).astype(jnp.float32) * float(x_scr.shape[0])
         to_next = (q + ends_ref.shape[0] - 1 - spot).astype(jnp.float32) * float(x_scr.shape[0])
@@ -134,14 +136,14 @@
         lax.fori_loop(0, rows // CHUNKS, step, first, unroll=4)
 
 
-def carry_kernel(place_ref, rows_ref, before_ref, local_ref, gate_hbm, gated_ref, y_scr, gate_ref, arrived):
+def carry_kernel(rows_ref, before_ref, local_ref, gate_hbm, gated_ref, y_scr, gate_ref, arrived):
     fetch = pltpu.make_async_copy(gate_hbm, gate_ref, arrived)
     fetch.start()
     tokens = y_scr.shape[1]
     modes = (local_ref.shape[0] - tokens) // 2
     rates, coefs = local_ref[tokens : tokens + modes, :], local_ref[tokens + modes :, :]
-    row, length = place_ref[0], place_ref[1]
-    whole = jnp.exp(-(rates * length.astype(jnp.float32)))
+    row = lax.div(lax.axis_index("context"), LOW)
+    whole = jnp.exp(-(rates * float(tokens * LOW)))
     carried = jnp.zeros_like(rates)
     for q in range(rows_ref.shape[0]):
         carried = jnp.where(q < row, whole * carried + rows_ref[q].astype(jnp.float32), carried)
@@ -154,30 +156,32 @@
         gated_ref[:, cols] = (local_ref[:tokens, cols] + gate * y_scr[half]).astype(jnp.bfloat16)
 
 
-def copies_kernel(in_ref, out_ref):
-    for i in range(out_ref.shape[0]):
-        out_ref[i] = in_ref[...]
-
-
-def near_product(order_ref, p0, p1, p2, p3, mine_ref, other_ref, mine_out, other_out, far_mine, far_other):
+def copy_kernel(in_ref, out_ref):
+    out_ref[...] = in_ref[...]
+
+
+def near_product(p0, p1, p2, p3, mine_ref, other_ref, mine_out, other_out, far_mine, far_other):
+    here = lax.axis_index("tensor")
+    core, y, z_hi = lax.rem(here, CORES), lax.rem(lax.div(here, CORES), Y), lax.div(here, Y * CORES)
+
+    def block(weight_ref, z_hi, y):
+        height = weight_ref.shape[0] // (2 * Y * CORES)
+        first = ((z_hi * Y + y) * CORES + core) * height
+        return weight_ref[pl.ds(pl.multiple_of(first, height), height), :]
+
     for weight, out, far in ((mine_ref, mine_out, far_mine), (other_ref, other_out, far_other)):
         total = jnp.zeros(out.shape, jnp.float32)
         for i, piece in enumerate((p0, p1, p2, p3)):
-            total += jnp.dot(piece[...], block_of(weight, order_ref[i]), preferred_element_type=jnp.float32)
+            source = lax.rem(y + Y - AWAY[i], Y)
+            total += jnp.dot(piece[...], block(weight, z_hi, source), preferred_element_type=jnp.float32)
+            far[i] = block(weight, 1 - z_hi, source)
         out[...] = total
-        for i in range(Y):
-            far[i] = block_of(weight, order_ref[Y + i])
-
-
-def block_of(weight_ref, index):
-    height = weight_ref.shape[0] // (2 * Y * CORES)
-    return weight_ref[pl.ds(pl.multiple_of(index * height, height), height), :]
-
-
-def far_product(pieces_ref, weight_ref, start_ref, out_ref):
+
+
+def far_product(p0, p1, p2, p3, weight_ref, start_ref, out_ref):
     total = start_ref[...]
-    for i in range(Y):
-        total += jnp.dot(pieces_ref[i], weight_ref[i], preferred_element_type=jnp.float32)
+    for i, piece in enumerate((p0, p1, p2, p3)):
+        total += jnp.dot(piece[...], weight_ref[i], preferred_element_type=jnp.float32)
     out_ref[...] = total.astype(out_ref.dtype)
 
 
@@ -195,7 +199,7 @@
     return pl.CostEstimate(flops=flops, bytes_accessed=moved, transcendentals=0)
 
 
-def call(kernel, args, outs, scratch=(), flops=0, scalars=0, limit=16, fetched=(), after=()):
+def call(kernel, args, outs, scratch=(), flops=0, limit=16, fetched=(), after=()):
     count, waits = len(args) + len(fetched), len(after)
 
     def run(*refs):
@@ -205,8 +209,7 @@
         run,
         grid=(1,),
         in_specs=[
-            *[pl.BlockSpec(memory_space=pltpu.SMEM)] * scalars,
-            *[full(a) for a in args[scalars:]],
+            *[full(a) for a in args],
             *[pl.BlockSpec(memory_space=pl.ANY)] * (len(fetched) + waits),
         ],
         out_specs=[full(o) for o in outs],
@@ -233,21 +236,17 @@
     halves = width // LANES
     block = pltpu.VMEM((halves, tokens, LANES), f32)
 
-    row, spot = place // LOW, place % LOW
     ends_out = (shape(bf16, LOW, 2 * modes, width), shape(f32, modes, CHUNKS, width))
     ends, states = pl.pallas_call(
         ends_kernel,
         grid=(halves,),
-        in_specs=[
-            pl.BlockSpec(memory_space=pltpu.SMEM),
-            *[pl.BlockSpec((rows, LANES), lambda h: (0, h)) for rows in (tokens, tokens, modes)],
-        ],
+        in_specs=[pl.BlockSpec((rows, LANES), lambda h: (0, h)) for rows in (tokens, tokens, modes)],
         out_specs=[pl.BlockSpec((*out.shape[:2], LANES), lambda h: (0, 0, h)) for out in ends_out],
         out_shape=list(ends_out),
         scratch_shapes=[pltpu.VMEM((tokens, LANES), f32), pltpu.VMEM((modes, LANES), f32)],
         compiler_params=params(58),
         cost_estimate=cost((key_act, value_act), ends_out, 2 * tokens * width * modes),
-    )(spot.reshape(1), key_act, value_act, decay_rate)
+    )(key_act, value_act, decay_rate)
     with jax.named_scope("states_along_z"):
         groups = [[x * LOW + z for z in range(LOW)] for x in range(X)]
         ends = lax.all_to_all(ends, "context", 0, 0, axis_index_groups=groups)
@@ -266,11 +265,10 @@
         rows = lax.all_to_all(rows, "context", 0, 0, axis_index_groups=groups)
     (gated,) = call(
         carry_kernel,
-        (jnp.stack([row, jnp.int32(tokens * LOW)]), rows, before, local),
+        (rows, before, local),
         (shape(bf16, tokens, width),),
         (block, pltpu.VMEM((tokens, width), bf16), pltpu.SemaphoreType.DMA),
         flops=2 * tokens * width * modes,
-        scalars=1,
         fetched=(gate_act,),
     )
     with jax.named_scope("along_z"):
@@ -278,34 +276,29 @@
     with jax.named_scope("own_along_y"):
         *near, other_weight = lax.cond(
             place < parts,
-            lambda own, weight: (*[move(own, dy=d) for d in (2, 1, -1)], move(weight, dcore=1)),
+            lambda own, weight: (*[move(own, dy=d) for d in AWAY[1:]], move(weight, dcore=1)),
             lambda own, weight: (own, own, own, weight),
             gated,
             out_weight,
         )
         near = [gated, *near]
 
-    z_hi, y, core = here // (Y * CORES), here // CORES % Y, here % CORES
-    ys = jnp.stack([y, (y + 2) % Y, (y - 1) % Y, (y + 1) % Y])
-    order = (jnp.concatenate([z_hi * Y + ys, (1 - z_hi) * Y + jnp.arange(Y)]) * CORES + core).astype(jnp.int32)
     sums = shape(f32, tokens, columns)
     work = 2 * tokens * Y * width * columns
     picked = shape(bf16, Y, width, columns)
     mine_sum, other_sum, far_mine, far_other = call(
         near_product,
-        (order, *near, out_weight, other_weight),
+        (*near, out_weight, other_weight),
         (sums, sums, picked, picked),
         flops=2 * work,
-        scalars=1,
     )
     with jax.named_scope("far_along_y"):
-        (far,) = call(copies_kernel, (far,), (shape(bf16, Y, tokens, width),), after=(mine_sum,))
-        groups = [[(high * Y + y) * CORES + core for y in range(Y)] for high in range(Z // LOW) for core in range(CORES)]
-        far = lax.all_to_all(far, "tensor", 0, 0, axis_index_groups=groups)
-    (other_sum,) = call(far_product, (far, far_other, other_sum), (shape(bf16, tokens, columns),), flops=work)
+        (far,) = call(copy_kernel, (far,), (shape(bf16, tokens, width),), after=near[1:2])
+        far = [far] + [move(far, dy=d) for d in AWAY[1:]]
+    (other_sum,) = call(far_product, (*far, far_other, other_sum), (shape(bf16, tokens, columns),), flops=work)
     with jax.named_scope("sum_swap"):
         from_other = move(other_sum, dcore=1)
-    (mine_sum,) = call(far_product, (far, far_mine, mine_sum), (sums,), flops=work)
+    (mine_sum,) = call(far_product, (*far, far_mine, mine_sum), (sums,), flops=work)
     return (mine_sum + from_other.astype(f32)).astype(bf16)
 
 

time: 95.9 us -> 89.6 us (0.934)
  blocking collectives: 17.5 us -> 8.11 us
  starting transfers between devices: 47 us -> 52.8 us
  waiting for transfers between devices: 14.2 us -> 12.9 us
  Pallas kernels: 10.9 us -> 9.74 us
    ppermute x6 -> x9, starting transfers between devices: 29.9 us -> 39.7 us  [move(): return lax.ppermute(array, AXES, pairs)]
    all_to_all x1, blocking collectives: 17.5 us -> 8.11 us  [body(): rows = lax.all_to_all(rows, 'context', 0, 0, axis_index_groups=groups)]
    all_to_all x1 -> x0, waiting for transfers between devices: 4.2 us -> none  [body(): rows = lax.all_to_all(rows, 'context', 0, 0, axis_index_groups=groups)]
    all_to_all x1 -> x0, starting transfers between devices: 4.01 us -> none  [body(): rows = lax.all_to_all(rows, 'context', 0, 0, axis_index_groups=groups)]
    ppermute x6 -> x9, waiting for transfers between devices: 6.74 us -> 9.63 us  [move(): return lax.ppermute(array, AXES, pairs)]
    pallas_call x8, Pallas kernels: 10.9 us -> 9.74 us  [the longest x7 6.8 us: call(): pl.pallas_call(run, grid=(1,), in_specs=[*[full(a) for a in args], *[pl.B...]
  transfers between devices with their start and end apart: 8 -> 10, of which waited for: 5 -> 5; matrix products, arithmetic and copies ran while one was open for 1% -> 1% of each run, Pallas kernels for 6% -> 6%
where the time goes in v3:
time: 89.6 us; the launch traced here: 89 us
  starting transfers between devices  52.8 us (59%)
  waiting for transfers between devices  12.9 us (14%)
  Pallas kernels  9.74 us (11%)
  blocking collectives  8.11 us (9%)
  local copies, waits for them, and re-layouts  3.76 us (4%)
  other arithmetic  1.51 us (2%)
    ppermute x9, starting transfers between devices, move(): return lax.ppermute(array, AXES, pairs)  39.7 us
    all_to_all x1, starting transfers between devices, body(): ends = lax.all_to_all(ends, 'context', 0, 0, axis_index_groups=groups)  13.1 us
    ppermute x9, waiting for transfers between devices, move(): return lax.ppermute(array, AXES, pairs)  9.63 us
    all_to_all x1, blocking collectives, body(): rows = lax.all_to_all(rows, 'context', 0, 0, axis_index_groups=groups)  8.11 us
    pallas_call x7, Pallas kernels, call(): pl.pallas_call(run, grid=(1,), in_specs=[*[full(a) for a in args], *[pl.B...  6.8 us
    unnamed x12, local copies, waits for them, and re-layouts  3.76 us
    all_to_all x1, waiting for transfers between devices, body(): ends = lax.all_to_all(ends, 'context', 0, 0, axis_index_groups=groups)  3.26 us
    pallas_call x1, Pallas kernels, body(): pl.pallas_call(ends_kernel, grid=(halves,), in_specs=[pl.BlockSpec((rows,...  2.94 us
  transfers between devices with their start and end apart: 10, of which 5 were waited for; matrix products, arithmetic and copies ran while one was open for 1% of the time, Pallas kernels for 6%

profile of v3, /device:TPU:1, one launch (start us, length us, event | category | flops | bytes accessed | tf_op | source)
XLA Modules:
  0.0 89.0 jit_solution(14203797078611693749)
XLA Ops:
  0.0 2.9 %shard_map.73 = (bf16[8,32,256]{2,1,0:T(8,128)(2,1)}, f32[16,8,256]{2,1,0:T(8,128)}) custom-call(bf16[512,256]{1,0:T(8,128)(2,1)} %refs_1_.1, bf16[512,256]{1,0:T(8,128)(2,1)} %refs_2_.1, f32[16,256]{1,0:T(8,128)} %bitcast.3), custom_call_target="tpu_custom_call" | custom-call | flops 4194304 | bytes 786432 | tf_op jit(solution)/shard_map/pallas_call | solution.py:240
  2.9 13.1 %all-to-all-start = ((bf16[8,32,256]{2,1,0:T(8,128)(2,1)}), bf16[8,32,256]{2,1,0:T(8,128)(2,1)S(1)}, u32[]{:S(2)}, u32[]{:S(2)}) async-start(bf16[8,32,256]{2,1,0:T(8,128)(2,1)} %get-tuple-element.29), calls=%async_computation | async-start | bytes 262144 | tf_op jit(solution)/shard_map/states_along_z/all_to_all | solution.py:252
  16.0 0.8 pad_maximum_fusion.refs_3_
  16.8 0.9 %copy-done = bf16[512,256]{1,0:T(8,128)(2,1)S(1)} copy-done((bf16[512,256]{1,0:T(8,128)(2,1)S(1)}, bf16[512,256]{1,0:T(8,128)(2,1)}, u32[]{:S(2)}) %copy-start) | copy-done | bytes 262168
  17.7 0.9 %copy-done.2 = bf16[512,256]{1,0:T(8,128)(2,1)S(1)} copy-done((bf16[512,256]{1,0:T(8,128)(2,1)S(1)}, bf16[512,256]{1,0:T(8,128)(2,1)}, u32[]{:S(2)}) %copy-start.2) | copy-done | bytes 262168
  18.7 0.9 %copy-done.3 = bf16[512,256]{1,0:T(8,128)(2,1)S(1)} copy-done((bf16[512,256]{1,0:T(8,128)(2,1)S(1)}, bf16[512,256]{1,0:T(8,128)(2,1)}, u32[]{:S(2)}) %copy-start.3) | copy-done | bytes 262168
  19.6 0.9 %copy-done.4 = f32[16,8,256]{2,1,0:T(8,128)S(1)} copy-done((f32[16,8,256]{2,1,0:T(8,128)S(1)}, f32[16,8,256]{2,1,0:T(8,128)}, u32[]{:S(2)}) %copy-start.4) | copy-done | bytes 131096
  20.5 2.6 %shard_map.74.refs_1_.refs_2_ = f32[544,256]{1,0:T(8,128)S(1)} custom-call(bf16[512,256]{1,0:T(8,128)(2,1)S(1)} %copy-done, bf16[512,256]{1,0:T(8,128)(2,1)S(1)} %copy-done.2, bf16[512,256]{1,0:T(8,128)(2,1)S(1)} %copy-done.3, f32[33,256]{1,0:T(8,128)S(1)} %pad_maximum_fusion.refs_3_, f32[16,8,256]{2,1,0:T(8,128)S(1)} %copy-done.4), custom_call_target="tpu_custom_call" | custom-call | flops 8388608 | bytes 1508352 | tf_op jit(solution)/shard_map/pallas_call | solution.py:208
  23.1 3.3 %all-to-all-done.refs_0_ = bf16[8,32,256]{2,1,0:T(8,128)(2,1)S(1)} async-done(((bf16[8,32,256]{2,1,0:T(8,128)(2,1)}), bf16[8,32,256]{2,1,0:T(8,128)(2,1)S(1)}, u32[]{:S(2)}, u32[]{:S(2)}) %all-to-all-start) | async-done | bytes 131104 | tf_op jit(solution)/shard_map/states_along_z/all_to_all | solution.py:252
  26.4 8.1 %all_to_all.10.refs_0_ = bf16[4,16,256]{2,1,0:T(8,128)(2,1)S(1)} all-to-all(bf16[4,16,256]{2,1,0:T(8,128)(2,1)S(1)} %get-tuple-element.31), channel_id=1, replica_groups={{0,8,16,24},{1,9,17,25},{2,10,18,26},{3,11,19,27},{4,12,20,28},{5,13,21..., dimensions={0} | all-to-all | bytes 65536 | tf_op jit(solution)/shard_map/states_along_x/all_to_all | solution.py:265
  34.5 0.7 shard_map.76.refs_0_
  35.2 7.9 %collective-permute-start.4 = (bf16[512,256]{1,0:T(8,128)(2,1)S(1)}, bf16[512,256]{1,0:T(8,128)(2,1)S(1)}, u32[]{:S(2)}, u32[]{:S(2)}) collective-permute-start(bf16[512,256]{1,0:T(8,128)(2,1)S(1)} %shard_map.76.refs_0_), channel_id=1, source_target_pairs={{0,256},{32,288},{1,257},{33,289},{2,258},{34,290},{3,259},{35,291... | collective-permute-start | bytes 786440 | tf_op jit(solution)/shard_map/along_z/ppermute | solution.py:29
  43.2 23.6 %conditional.1 = (bf16[512,256]{1,0:T(8,128)(2,1)}, bf16[512,256]{1,0:T(8,128)(2,1)}, bf16[512,256]{1,0:T(8,128)(2,1)}, bf16[4096,256]{1,0:T(8,128)(2,1)}) conditional(s32[]{:T(128)} %convert_element_type.9, (bf16[512,256]{1,0:T(8,128)(2,1)S(1)}, bf16[4096,256]{1,0:T(8,128)(2,1)S(1)}) %tuple.16, (bf16[512,256]{1,0:T(8,128)(2,1)S(1)}, ...), branch_computations={%region_0.0_spmd, %region_1.0_spmd} | conditional | bytes 11534528 | solution.py:277
  43.2 6.2 %collective-permute-start.3 = (bf16[4096,256]{1,0:T(8,128)(2,1)S(1)}, bf16[4096,256]{1,0:T(8,128)(2,1)}, u32[]{:S(2)}, u32[]{:S(2)}) collective-permute-start(bf16[4096,256]{1,0:T(8,128)(2,1)S(1)} %get-tuple-element.16), channel_id=1, source_target_pairs={{0,32},{32,0},{1,33},{33,1},{2,34},{34,2},{3,35},{35,3},{4,36},{36... | collective-permute-start | bytes 6291464 | tf_op jit(solution)/shard_map/own_along_y/cond/branch_1_fun/ppermute | solution.py:29
  49.4 4.8 %collective-permute-start = (bf16[512,256]{1,0:T(8,128)(2,1)S(1)}, bf16[512,256]{1,0:T(8,128)(2,1)}, u32[]{:S(2)}, u32[]{:S(2)}) collective-permute-start(bf16[512,256]{1,0:T(8,128)(2,1)S(1)} %get-tuple-element.15), channel_id=1, source_target_pairs={{0,128},{32,160},{1,129},{33,161},{2,130},{34,162},{3,131},{35,163... | collective-permute-start | bytes 786440 | tf_op jit(solution)/shard_map/own_along_y/cond/branch_1_fun/ppermute | solution.py:29
  54.2 2.3 %collective-permute-start.1 = (bf16[512,256]{1,0:T(8,128)(2,1)S(1)}, bf16[512,256]{1,0:T(8,128)(2,1)}, u32[]{:S(2)}, u32[]{:S(2)}) collective-permute-start(bf16[512,256]{1,0:T(8,128)(2,1)S(1)} %get-tuple-element.15), channel_id=1, source_target_pairs={{0,64},{32,96},{1,65},{33,97},{2,66},{34,98},{3,67},{35,99},{4,68}... | collective-permute-start | bytes 786440 | tf_op jit(solution)/shard_map/own_along_y/cond/branch_1_fun/ppermute | solution.py:29
  56.6 4.2 %collective-permute-start.2 = (bf16[512,256]{1,0:T(8,128)(2,1)S(1)}, bf16[512,256]{1,0:T(8,128)(2,1)}, u32[]{:S(2)}, u32[]{:S(2)}) collective-permute-start(bf16[512,256]{1,0:T(8,128)(2,1)S(1)} %get-tuple-element.15), channel_id=1, source_target_pairs={{0,192},{32,224},{1,193},{33,225},{2,194},{34,226},{3,195},{35,227... | collective-permute-start | bytes 786440 | tf_op jit(solution)/shard_map/own_along_y/cond/branch_1_fun/ppermute | solution.py:29
  60.7 0.1 collective-permute-done
  60.8 5.9 %collective-permute-done.1 = bf16[512,256]{1,0:T(8,128)(2,1)} collective-permute-done((bf16[512,256]{1,0:T(8,128)(2,1)S(1)}, bf16[512,256]{1,0:T(8,128)(2,1)}, u32[]{:S(2)}, u32[]{:S(2)}) %collective-permute-start.1) | collective-permute-done | bytes 262176 | tf_op jit(solution)/shard_map/own_along_y/cond/branch_1_fun/ppermute | solution.py:29
  66.8 0.0 collective-permute-done.2
  66.8 4.8 %collective-permute-start.5 = (bf16[512,256]{1,0:T(8,128)(2,1)S(1)}, bf16[512,256]{1,0:T(8,128)(2,1)S(1)}, u32[]{:S(2)}, u32[]{:S(2)}) collective-permute-start(bf16[512,256]{1,0:T(8,128)(2,1)S(1)} %far_along_y.1.refs_0_), channel_id=1, source_target_pairs={{0,128},{32,160},{1,129},{33,161},{2,130},{34,162},{3,131},{35,163... | collective-permute-start | bytes 786440 | tf_op jit(solution)/shard_map/far_along_y/ppermute | solution.py:29
  71.7 2.1 %collective-permute-start.6 = (bf16[512,256]{1,0:T(8,128)(2,1)S(1)}, bf16[512,256]{1,0:T(8,128)(2,1)S(1)}, u32[]{:S(2)}, u32[]{:S(2)}) collective-permute-start(bf16[512,256]{1,0:T(8,128)(2,1)S(1)} %far_along_y.1.refs_0_), channel_id=1, source_target_pairs={{0,64},{32,96},{1,65},{33,97},{2,66},{34,98},{3,67},{35,99},{4,68}... | collective-permute-start | bytes 786440 | tf_op jit(solution)/shard_map/far_along_y/ppermute | solution.py:29
  73.8 4.4 %collective-permute-start.7 = (bf16[512,256]{1,0:T(8,128)(2,1)S(1)}, bf16[512,256]{1,0:T(8,128)(2,1)S(1)}, u32[]{:S(2)}, u32[]{:S(2)}) collective-permute-start(bf16[512,256]{1,0:T(8,128)(2,1)S(1)} %far_along_y.1.refs_0_), channel_id=1, source_target_pairs={{0,192},{32,224},{1,193},{33,225},{2,194},{34,226},{3,195},{35,227... | collective-permute-start | bytes 786440 | tf_op jit(solution)/shard_map/far_along_y/ppermute | solution.py:29
  78.2 2.6 %shard_map.77 = (f32[512,256]{1,0:T(8,128)S(1)}, f32[512,256]{1,0:T(8,128)S(1)}, bf16[4,256,256]{2,1,0:T(8,128)(2,1)S(1)}, bf16[4,256,256]{2,1,0:T(8,128)(2,1)S(1)}) custom-call(bf16[512,256]{1,0:T(8,128)(2,1)S(1)} %shard_map.76.refs_0_, bf16[512,256]{1,0:T(8,128)(2,1)} %get-tuple-element.33.refs_1_, bf16[512,256]{1,0:T(8,128)(2,1)} %get-tuple-element.34.refs_2_, ...), custom_call_target="tpu_custom_call" | custom-call | flops 536870912 | bytes 7340032 | tf_op jit(solution)/shard_map/pallas_call | solution.py:208
  80.8 0.0 collective-permute-done.5.refs_1_
  80.8 2.9 %collective-permute-done.6.refs_2_ = bf16[512,256]{1,0:T(8,128)(2,1)S(1)} collective-permute-done((bf16[512,256]{1,0:T(8,128)(2,1)S(1)}, bf16[512,256]{1,0:T(8,128)(2,1)S(1)}, u32[]{:S(2)}, u32[]{:S(2)}) %collective-permute-start.6) | collective-permute-done | bytes 262176 | tf_op jit(solution)/shard_map/far_along_y/ppermute | solution.py:29
  83.7 0.0 collective-permute-done.7.refs_3_
  83.7 0.4 shard_map.79
  84.1 2.9 %collective-permute-start.8 = (bf16[512,256]{1,0:T(8,128)(2,1)S(1)}, bf16[512,256]{1,0:T(8,128)(2,1)S(1)}, u32[]{:S(2)}, u32[]{:S(2)}) collective-permute-start(bf16[512,256]{1,0:T(8,128)(2,1)S(1)} %shard_map.79), channel_id=1, source_target_pairs={{0,32},{32,0},{1,33},{33,1},{2,34},{34,2},{3,35},{35,3},{4,36},{36... | collective-permute-start | bytes 786440 | tf_op jit(solution)/shard_map/sum_swap/ppermute | solution.py:29
  87.1 0.4 shard_map.78
  87.5 0.7 collective-permute-done.8
  88.2 0.8 add_convert_fusion
  (12 shorter events, 0.1 us)
Async XLA Ops:
  0.0 34.5 %copy-start.1 = (bf16[512,256]{1,0:T(8,128)(2,1)S(1)}, bf16[512,256]{1,0:T(8,128)(2,1)}, u32[]{:S(2)}) copy-start(bf16[512,256]{1,0:T(8,128)(2,1)} %refs_3_.1) | copy-start | bytes 786436
  2.9 23.4 %all-to-all-start = ((bf16[8,32,256]{2,1,0:T(8,128)(2,1)}), bf16[8,32,256]{2,1,0:T(8,128)(2,1)S(1)}, u32[]{:S(2)}, u32[]{:S(2)}) async-start(bf16[8,32,256]{2,1,0:T(8,128)(2,1)} %get-tuple-element.29), calls=%async_computation | async-start | bytes 262144 | tf_op jit(solution)/shard_map/states_along_z/all_to_all | solution.py:252
  16.8 0.9 %copy-start = (bf16[512,256]{1,0:T(8,128)(2,1)S(1)}, bf16[512,256]{1,0:T(8,128)(2,1)}, u32[]{:S(2)}) copy-start(bf16[512,256]{1,0:T(8,128)(2,1)} %refs_3_.1) | copy-start | bytes 786436
  17.7 0.9 %copy-start.2 = (bf16[512,256]{1,0:T(8,128)(2,1)S(1)}, bf16[512,256]{1,0:T(8,128)(2,1)}, u32[]{:S(2)}) copy-start(bf16[512,256]{1,0:T(8,128)(2,1)} %refs_1_.1) | copy-start | bytes 786436
  18.7 0.9 %copy-start.3 = (bf16[512,256]{1,0:T(8,128)(2,1)S(1)}, bf16[512,256]{1,0:T(8,128)(2,1)}, u32[]{:S(2)}) copy-start(bf16[512,256]{1,0:T(8,128)(2,1)} %refs_2_.1) | copy-start | bytes 786436
  19.6 0.9 %copy-start.4 = (f32[16,8,256]{2,1,0:T(8,128)S(1)}, f32[16,8,256]{2,1,0:T(8,128)}, u32[]{:S(2)}) copy-start(f32[16,8,256]{2,1,0:T(8,128)} %get-tuple-element.30.refs_4_) | copy-start | bytes 393220
  20.5 22.7 %copy-start.5 = (bf16[4096,256]{1,0:T(8,128)(2,1)S(1)}, bf16[4096,256]{1,0:T(8,128)(2,1)}, u32[]{:S(2)}) copy-start(bf16[4096,256]{1,0:T(8,128)(2,1)} %refs_4_.1) | copy-start | bytes 6291460
  35.2 31.5 %collective-permute-start.4 = (bf16[512,256]{1,0:T(8,128)(2,1)S(1)}, bf16[512,256]{1,0:T(8,128)(2,1)S(1)}, u32[]{:S(2)}, u32[]{:S(2)}) collective-permute-start(bf16[512,256]{1,0:T(8,128)(2,1)S(1)} %shard_map.76.refs_0_), channel_id=1, source_target_pairs={{0,256},{32,288},{1,257},{33,289},{2,258},{34,290},{3,259},{35,291... | collective-permute-start | bytes 786440 | tf_op jit(solution)/shard_map/along_z/ppermute | solution.py:29
  43.2 23.6 %collective-permute-start.3 = (bf16[4096,256]{1,0:T(8,128)(2,1)S(1)}, bf16[4096,256]{1,0:T(8,128)(2,1)}, u32[]{:S(2)}, u32[]{:S(2)}) collective-permute-start(bf16[4096,256]{1,0:T(8,128)(2,1)S(1)} %get-tuple-element.16), channel_id=1, source_target_pairs={{0,32},{32,0},{1,33},{33,1},{2,34},{34,2},{3,35},{35,3},{4,36},{36... | collective-permute-start | bytes 6291464 | tf_op jit(solution)/shard_map/own_along_y/cond/branch_1_fun/ppermute | solution.py:29
  49.4 11.4 %collective-permute-start = (bf16[512,256]{1,0:T(8,128)(2,1)S(1)}, bf16[512,256]{1,0:T(8,128)(2,1)}, u32[]{:S(2)}, u32[]{:S(2)}) collective-permute-start(bf16[512,256]{1,0:T(8,128)(2,1)S(1)} %get-tuple-element.15), channel_id=1, source_target_pairs={{0,128},{32,160},{1,129},{33,161},{2,130},{34,162},{3,131},{35,163... | collective-permute-start | bytes 786440 | tf_op jit(solution)/shard_map/own_along_y/cond/branch_1_fun/ppermute | solution.py:29
  54.2 12.5 %collective-permute-start.1 = (bf16[512,256]{1,0:T(8,128)(2,1)S(1)}, bf16[512,256]{1,0:T(8,128)(2,1)}, u32[]{:S(2)}, u32[]{:S(2)}) collective-permute-start(bf16[512,256]{1,0:T(8,128)(2,1)S(1)} %get-tuple-element.15), channel_id=1, source_target_pairs={{0,64},{32,96},{1,65},{33,97},{2,66},{34,98},{3,67},{35,99},{4,68}... | collective-permute-start | bytes 786440 | tf_op jit(solution)/shard_map/own_along_y/cond/branch_1_fun/ppermute | solution.py:29
  56.6 10.2 %collective-permute-start.2 = (bf16[512,256]{1,0:T(8,128)(2,1)S(1)}, bf16[512,256]{1,0:T(8,128)(2,1)}, u32[]{:S(2)}, u32[]{:S(2)}) collective-permute-start(bf16[512,256]{1,0:T(8,128)(2,1)S(1)} %get-tuple-element.15), channel_id=1, source_target_pairs={{0,192},{32,224},{1,193},{33,225},{2,194},{34,226},{3,195},{35,227... | collective-permute-start | bytes 786440 | tf_op jit(solution)/shard_map/own_along_y/cond/branch_1_fun/ppermute | solution.py:29
  66.8 14.0 %collective-permute-start.5 = (bf16[512,256]{1,0:T(8,128)(2,1)S(1)}, bf16[512,256]{1,0:T(8,128)(2,1)S(1)}, u32[]{:S(2)}, u32[]{:S(2)}) collective-permute-start(bf16[512,256]{1,0:T(8,128)(2,1)S(1)} %far_along_y.1.refs_0_), channel_id=1, source_target_pairs={{0,128},{32,160},{1,129},{33,161},{2,130},{34,162},{3,131},{35,163... | collective-permute-start | bytes 786440 | tf_op jit(solution)/shard_map/far_along_y/ppermute | solution.py:29
  71.7 12.0 %collective-permute-start.6 = (bf16[512,256]{1,0:T(8,128)(2,1)S(1)}, bf16[512,256]{1,0:T(8,128)(2,1)S(1)}, u32[]{:S(2)}, u32[]{:S(2)}) collective-permute-start(bf16[512,256]{1,0:T(8,128)(2,1)S(1)} %far_along_y.1.refs_0_), channel_id=1, source_target_pairs={{0,64},{32,96},{1,65},{33,97},{2,66},{34,98},{3,67},{35,99},{4,68}... | collective-permute-start | bytes 786440 | tf_op jit(solution)/shard_map/far_along_y/ppermute | solution.py:29
  73.8 9.9 %collective-permute-start.7 = (bf16[512,256]{1,0:T(8,128)(2,1)S(1)}, bf16[512,256]{1,0:T(8,128)(2,1)S(1)}, u32[]{:S(2)}, u32[]{:S(2)}) collective-permute-start(bf16[512,256]{1,0:T(8,128)(2,1)S(1)} %far_along_y.1.refs_0_), channel_id=1, source_target_pairs={{0,192},{32,224},{1,193},{33,225},{2,194},{34,226},{3,195},{35,227... | collective-permute-start | bytes 786440 | tf_op jit(solution)/shard_map/far_along_y/ppermute | solution.py:29
  84.1 4.1 %collective-permute-start.8 = (bf16[512,256]{1,0:T(8,128)(2,1)S(1)}, bf16[512,256]{1,0:T(8,128)(2,1)S(1)}, u32[]{:S(2)}, u32[]{:S(2)}) collective-permute-start(bf16[512,256]{1,0:T(8,128)(2,1)S(1)} %shard_map.79), channel_id=1, source_target_pairs={{0,32},{32,0},{1,33},{33,1},{2,34},{34,2},{3,35},{35,3},{4,36},{36... | collective-permute-start | bytes 786440 | tf_op jit(solution)/shard_map/sum_swap/ppermute | solution.py:29

commit v4 on v3

--- a/solution.py
+++ b/solution.py
@@ -9,7 +9,7 @@
 LANES = 128
 Z, Y, CORES, X = 16, 4, 2, 4
 LOW = Z // 2
-AWAY = (0, 2, 1, -1)
+AWAY = (0, -1, 1, 2)
 AXES = ("tensor", "context")
 
 
@@ -165,8 +165,9 @@
     core, y, z_hi = lax.rem(here, CORES), lax.rem(lax.div(here, CORES), Y), lax.div(here, Y * CORES)
 
     def block(weight_ref, z_hi, y):
-        height = weight_ref.shape[0] // (2 * Y * CORES)
-        first = ((z_hi * Y + y) * CORES + core) * height
+        height = p0.shape[1]
+        cores = weight_ref.shape[0] // (2 * Y * height)
+        first = ((z_hi * Y + y) * cores + core * (cores - 1)) * height
         return weight_ref[pl.ds(pl.multiple_of(first, height), height), :]
 
     for weight, out, far in ((mine_ref, mine_out, far_mine), (other_ref, other_out, far_other)):
@@ -274,14 +275,15 @@
     with jax.named_scope("along_z"):
         far = move(gated, dz=Z // 2)
     with jax.named_scope("own_along_y"):
-        *near, other_weight = lax.cond(
-            place < parts,
-            lambda own, weight: (*[move(own, dy=d) for d in AWAY[1:]], move(weight, dcore=1)),
-            lambda own, weight: (own, own, own, weight),
-            gated,
-            out_weight,
-        )
-        near = [gated, *near]
+        def theirs(weight):
+            by_core = weight.reshape(2 * Y, CORES, width, columns)
+            other = 1 - lax.rem(lax.axis_index("tensor"), CORES)
+            return lax.dynamic_index_in_dim(by_core, other, 1, keepdims=False).reshape(-1, columns)
+
+        (own,) = call(copy_kernel, (gated,), (shape(bf16, tokens, width),))
+        near = [own] + [move(own, dy=d) for d in AWAY[1:]]
+    with jax.named_scope("weight_swap"):
+        other_weight = lax.cond(place < parts, lambda weight: move(theirs(weight), dcore=1), theirs, out_weight)
 
     sums = shape(f32, tokens, columns)
     work = 2 * tokens * Y * width * columns
@@ -293,7 +295,7 @@
         flops=2 * work,
     )
     with jax.named_scope("far_along_y"):
-        (far,) = call(copy_kernel, (far,), (shape(bf16, tokens, width),), after=near[1:2])
+        (far,) = call(copy_kernel, (far,), (shape(bf16, tokens, width),), after=(other_weight,))
         far = [far] + [move(far, dy=d) for d in AWAY[1:]]
     (other_sum,) = call(far_product, (*far, far_other, other_sum), (shape(bf16, tokens, columns),), flops=work)
     with jax.named_scope("sum_swap"):

time: 89.6 us -> 88 us (0.982)
  starting transfers between devices: 52.8 us -> 50.2 us
  local copies, waits for them, and re-layouts: 3.76 us -> 5.06 us
    ppermute x9, starting transfers between devices: 39.7 us -> 37.1 us  [move(): return lax.ppermute(array, AXES, pairs)]
    dynamic_slice x0 -> x1, local copies, waits for them, and re-layouts: none -> 1.3 us  [theirs(): lax.dynamic_index_in_dim(by_core, other, 1, keepdims=False)]
    pallas_call x7 -> x8, Pallas kernels: 6.8 us -> 6.84 us  [call(): pl.pallas_call(run, grid=(1,), in_specs=[*[full(a) for a in args], *[pl.B...]
    unnamed x12 -> x10, local copies, waits for them, and re-layouts: 3.76 us -> 3.76 us
  transfers between devices with their start and end apart: 10 -> 10, of which waited for: 5 -> 4; matrix products, arithmetic and copies ran while one was open for 1% -> 2% of each run, Pallas kernels for 6% -> 6%
where the time goes in v4:
time: 88 us; the launch traced here: 87.3 us
  starting transfers between devices  50.2 us (57%)
  waiting for transfers between devices  12.5 us (14%)
  Pallas kernels  9.78 us (11%)
  blocking collectives  8.11 us (9%)
  local copies, waits for them, and re-layouts  5.06 us (6%)
  other arithmetic  1.51 us (2%)
    ppermute x9, starting transfers between devices, move(): return lax.ppermute(array, AXES, pairs)  37.1 us
    all_to_all x1, starting transfers between devices, body(): ends = lax.all_to_all(ends, 'context', 0, 0, axis_index_groups=groups)  13.1 us
    ppermute x9, waiting for transfers between devices, move(): return lax.ppermute(array, AXES, pairs)  9.3 us
    all_to_all x1, blocking collectives, body(): rows = lax.all_to_all(rows, 'context', 0, 0, axis_index_groups=groups)  8.11 us
    pallas_call x8, Pallas kernels, call(): pl.pallas_call(run, grid=(1,), in_specs=[*[full(a) for a in args], *[pl.B...  6.84 us
    unnamed x10, local copies, waits for them, and re-layouts  3.76 us
    all_to_all x1, waiting for transfers between devices, body(): ends = lax.all_to_all(ends, 'context', 0, 0, axis_index_groups=groups)  3.25 us
    pallas_call x1, Pallas kernels, body(): pl.pallas_call(ends_kernel, grid=(halves,), in_specs=[pl.BlockSpec((rows,...  2.94 us
  transfers between devices with their start and end apart: 10, of which 4 were waited for; matrix products, arithmetic and copies ran while one was open for 2% of the time, Pallas kernels for 6%

profile of v4, /device:TPU:1, one launch (start us, length us, event | category | flops | bytes accessed | tf_op | source)
XLA Modules:
  0.0 87.3 jit_solution(16361705548447624119)
XLA Ops:
  0.0 2.9 %shard_map.79 = (bf16[8,32,256]{2,1,0:T(8,128)(2,1)}, f32[16,8,256]{2,1,0:T(8,128)}) custom-call(bf16[512,256]{1,0:T(8,128)(2,1)} %refs_1_.1, bf16[512,256]{1,0:T(8,128)(2,1)} %refs_2_.1, f32[16,256]{1,0:T(8,128)} %bitcast.14), custom_call_target="tpu_custom_call" | custom-call | flops 4194304 | bytes 786432 | tf_op jit(solution)/shard_map/pallas_call | solution.py:241
  2.9 13.1 %all-to-all-start = ((bf16[8,32,256]{2,1,0:T(8,128)(2,1)}), bf16[8,32,256]{2,1,0:T(8,128)(2,1)S(1)}, u32[]{:S(2)}, u32[]{:S(2)}) async-start(bf16[8,32,256]{2,1,0:T(8,128)(2,1)} %get-tuple-element.18), calls=%async_computation | async-start | bytes 262144 | tf_op jit(solution)/shard_map/states_along_z/all_to_all | solution.py:253
  16.0 0.8 pad_maximum_fusion.refs_3_
  16.8 0.9 %copy-done = bf16[512,256]{1,0:T(8,128)(2,1)S(1)} copy-done((bf16[512,256]{1,0:T(8,128)(2,1)S(1)}, bf16[512,256]{1,0:T(8,128)(2,1)}, u32[]{:S(2)}) %copy-start) | copy-done | bytes 262168
  17.7 0.9 %copy-done.2 = bf16[512,256]{1,0:T(8,128)(2,1)S(1)} copy-done((bf16[512,256]{1,0:T(8,128)(2,1)S(1)}, bf16[512,256]{1,0:T(8,128)(2,1)}, u32[]{:S(2)}) %copy-start.2) | copy-done | bytes 262168
  18.7 0.9 %copy-done.3 = bf16[512,256]{1,0:T(8,128)(2,1)S(1)} copy-done((bf16[512,256]{1,0:T(8,128)(2,1)S(1)}, bf16[512,256]{1,0:T(8,128)(2,1)}, u32[]{:S(2)}) %copy-start.3) | copy-done | bytes 262168
  19.6 0.9 %copy-done.4 = f32[16,8,256]{2,1,0:T(8,128)S(1)} copy-done((f32[16,8,256]{2,1,0:T(8,128)S(1)}, f32[16,8,256]{2,1,0:T(8,128)}, u32[]{:S(2)}) %copy-start.4) | copy-done | bytes 131096
  20.5 2.6 %shard_map.80.refs_1_.refs_2_ = f32[544,256]{1,0:T(8,128)S(1)} custom-call(bf16[512,256]{1,0:T(8,128)(2,1)S(1)} %copy-done, bf16[512,256]{1,0:T(8,128)(2,1)S(1)} %copy-done.2, bf16[512,256]{1,0:T(8,128)(2,1)S(1)} %copy-done.3, f32[33,256]{1,0:T(8,128)S(1)} %pad_maximum_fusion.refs_3_, f32[16,8,256]{2,1,0:T(8,128)S(1)} %copy-done.4), custom_call_target="tpu_custom_call" | custom-call | flops 8388608 | bytes 1508352 | tf_op jit(solution)/shard_map/pallas_call | solution.py:209
  23.1 3.2 %all-to-all-done.refs_0_ = bf16[8,32,256]{2,1,0:T(8,128)(2,1)S(1)} async-done(((bf16[8,32,256]{2,1,0:T(8,128)(2,1)}), bf16[8,32,256]{2,1,0:T(8,128)(2,1)S(1)}, u32[]{:S(2)}, u32[]{:S(2)}) %all-to-all-start) | async-done | bytes 131104 | tf_op jit(solution)/shard_map/states_along_z/all_to_all | solution.py:253
  26.4 8.1 %all_to_all.10.refs_0_ = bf16[4,16,256]{2,1,0:T(8,128)(2,1)S(1)} all-to-all(bf16[4,16,256]{2,1,0:T(8,128)(2,1)S(1)} %get-tuple-element.20), channel_id=1, replica_groups={{0,8,16,24},{1,9,17,25},{2,10,18,26},{3,11,19,27},{4,12,20,28},{5,13,21..., dimensions={0} | all-to-all | bytes 65536 | tf_op jit(solution)/shard_map/states_along_x/all_to_all | solution.py:266
  34.5 0.7 shard_map.82.refs_0_
  35.2 7.9 %collective-permute-start.1 = (bf16[512,256]{1,0:T(8,128)(2,1)S(1)}, bf16[512,256]{1,0:T(8,128)(2,1)S(1)}, u32[]{:S(2)}, u32[]{:S(2)}) collective-permute-start(bf16[512,256]{1,0:T(8,128)(2,1)S(1)} %shard_map.82.refs_0_), channel_id=1, source_target_pairs={{0,256},{32,288},{1,257},{33,289},{2,258},{34,290},{3,259},{35,291... | collective-permute-start | bytes 786440 | tf_op jit(solution)/shard_map/along_z/ppermute | solution.py:29
  43.2 4.8 %collective-permute-start.7 = (bf16[512,256]{1,0:T(8,128)(2,1)S(1)}, bf16[512,256]{1,0:T(8,128)(2,1)S(1)}, u32[]{:S(2)}, u32[]{:S(2)}) collective-permute-start(bf16[512,256]{1,0:T(8,128)(2,1)S(1)} %own_along_y.1.refs_0_), channel_id=1, source_target_pairs={{0,128},{32,160},{1,129},{33,161},{2,130},{34,162},{3,131},{35,163... | collective-permute-start | bytes 786440 | tf_op jit(solution)/shard_map/own_along_y/ppermute | solution.py:29
  48.1 2.3 %collective-permute-start.6 = (bf16[512,256]{1,0:T(8,128)(2,1)S(1)}, bf16[512,256]{1,0:T(8,128)(2,1)S(1)}, u32[]{:S(2)}, u32[]{:S(2)}) collective-permute-start(bf16[512,256]{1,0:T(8,128)(2,1)S(1)} %own_along_y.1.refs_0_), channel_id=1, source_target_pairs={{0,64},{32,96},{1,65},{33,97},{2,66},{34,98},{3,67},{35,99},{4,68}... | collective-permute-start | bytes 786440 | tf_op jit(solution)/shard_map/own_along_y/ppermute | solution.py:29
  50.4 4.2 %collective-permute-start.5 = (bf16[512,256]{1,0:T(8,128)(2,1)S(1)}, bf16[512,256]{1,0:T(8,128)(2,1)S(1)}, u32[]{:S(2)}, u32[]{:S(2)}) collective-permute-start(bf16[512,256]{1,0:T(8,128)(2,1)S(1)} %own_along_y.1.refs_0_), channel_id=1, source_target_pairs={{0,192},{32,224},{1,193},{33,225},{2,194},{34,226},{3,195},{35,227... | collective-permute-start | bytes 786440 | tf_op jit(solution)/shard_map/own_along_y/ppermute | solution.py:29
  54.6 10.7 %conditional.1 = (bf16[2048,256]{1,0:T(8,128)(2,1)}) conditional(s32[]{:T(128)} %convert_element_type.9, bf16[4096,256]{1,0:T(8,128)(2,1)} %refs_4_.1, bf16[4096,256]{1,0:T(8,128)(2,1)} %refs_4_.1), branch_computations={%region_0.1_spmd, %region_1.2_spmd} | conditional | flops 13 | bytes 6291649 | solution.py:286
  54.6 1.3 %constant_dynamic-slice_fusion.1 = bf16[8,1,256,256]{3,2,1,0:T(8,128)(2,1)S(1)} fusion(bf16[8,2,256,256]{3,2,1,0:T(8,128)(2,1)} %bitcast.12, s32[]{:T(128)S(6)} %select_n.6), kind=kLoop, calls=%fused_computation.1 | loop fusion | bytes 2097156 | tf_op jit(solution)/shard_map/weight_swap/cond/branch_1_fun/jit(dynamic_index_in_dim)/dynamic_slice | solution.py:281
  55.9 7.0 %collective-permute-start = (bf16[2048,256]{1,0:T(8,128)(2,1)S(1)}, bf16[2048,256]{1,0:T(8,128)(2,1)}, u32[]{:S(2)}, u32[]{:S(2)}) collective-permute-start(bf16[2048,256]{1,0:T(8,128)(2,1)S(1)} %bitcast.13), channel_id=1, source_target_pairs={{0,32},{32,0},{1,33},{33,1},{2,34},{34,2},{3,35},{35,3},{4,36},{36... | collective-permute-start | bytes 3145736 | tf_op jit(solution)/shard_map/weight_swap/cond/branch_1_fun/ppermute | solution.py:29
  62.9 2.4 %collective-permute-done = bf16[2048,256]{1,0:T(8,128)(2,1)} collective-permute-done((bf16[2048,256]{1,0:T(8,128)(2,1)S(1)}, bf16[2048,256]{1,0:T(8,128)(2,1)}, u32[]{:S(2)}, u32[]{:S(2)}) %collective-permute-start) | collective-permute-done | bytes 1048608 | tf_op jit(solution)/shard_map/weight_swap/cond/branch_1_fun/ppermute | solution.py:29
  65.3 0.0 collective-permute-done.1.refs_0_
  65.3 1.9 %collective-permute-start.4 = (bf16[512,256]{1,0:T(8,128)(2,1)S(1)}, bf16[512,256]{1,0:T(8,128)(2,1)S(1)}, u32[]{:S(2)}, u32[]{:S(2)}) collective-permute-start(bf16[512,256]{1,0:T(8,128)(2,1)S(1)} %far_along_y.1.refs_0_), channel_id=1, source_target_pairs={{0,128},{32,160},{1,129},{33,161},{2,130},{34,162},{3,131},{35,163... | collective-permute-start | bytes 786440 | tf_op jit(solution)/shard_map/far_along_y/ppermute | solution.py:29
  67.3 2.2 %collective-permute-start.3 = (bf16[512,256]{1,0:T(8,128)(2,1)S(1)}, bf16[512,256]{1,0:T(8,128)(2,1)S(1)}, u32[]{:S(2)}, u32[]{:S(2)}) collective-permute-start(bf16[512,256]{1,0:T(8,128)(2,1)S(1)} %far_along_y.1.refs_0_), channel_id=1, source_target_pairs={{0,64},{32,96},{1,65},{33,97},{2,66},{34,98},{3,67},{35,99},{4,68}... | collective-permute-start | bytes 786440 | tf_op jit(solution)/shard_map/far_along_y/ppermute | solution.py:29
  69.5 0.0 collective-permute-done.7.refs_3_
  69.5 4.3 %collective-permute-start.2 = (bf16[512,256]{1,0:T(8,128)(2,1)S(1)}, bf16[512,256]{1,0:T(8,128)(2,1)S(1)}, u32[]{:S(2)}, u32[]{:S(2)}) collective-permute-start(bf16[512,256]{1,0:T(8,128)(2,1)S(1)} %far_along_y.1.refs_0_), channel_id=1, source_target_pairs={{0,192},{32,224},{1,193},{33,225},{2,194},{34,226},{3,195},{35,227... | collective-permute-start | bytes 786440 | tf_op jit(solution)/shard_map/far_along_y/ppermute | solution.py:29
  73.8 0.0 collective-permute-done.5.refs_1_
  73.8 2.6 %shard_map.83 = (f32[512,256]{1,0:T(8,128)S(1)}, f32[512,256]{1,0:T(8,128)S(1)}, bf16[4,256,256]{2,1,0:T(8,128)(2,1)S(1)}, bf16[4,256,256]{2,1,0:T(8,128)(2,1)S(1)}) custom-call(bf16[512,256]{1,0:T(8,128)(2,1)S(1)} %own_along_y.1.refs_0_, bf16[512,256]{1,0:T(8,128)(2,1)S(1)} %collective-permute-done.5.refs_1_, ...), custom_call_target="tpu_custom_call" | custom-call | flops 536870912 | bytes 6291456 | tf_op jit(solution)/shard_map/pallas_call | solution.py:209
  76.4 6.2 %collective-permute-done.3.refs_2_ = bf16[512,256]{1,0:T(8,128)(2,1)S(1)} collective-permute-done((bf16[512,256]{1,0:T(8,128)(2,1)S(1)}, bf16[512,256]{1,0:T(8,128)(2,1)S(1)}, u32[]{:S(2)}, u32[]{:S(2)}) %collective-permute-start.3) | collective-permute-done | bytes 262176 | tf_op jit(solution)/shard_map/far_along_y/ppermute | solution.py:29
  82.6 0.4 shard_map.85
  83.0 2.4 %collective-permute-start.8 = (bf16[512,256]{1,0:T(8,128)(2,1)S(1)}, bf16[512,256]{1,0:T(8,128)(2,1)S(1)}, u32[]{:S(2)}, u32[]{:S(2)}) collective-permute-start(bf16[512,256]{1,0:T(8,128)(2,1)S(1)} %shard_map.85), channel_id=1, source_target_pairs={{0,32},{32,0},{1,33},{33,1},{2,34},{34,2},{3,35},{35,3},{4,36},{36... | collective-permute-start | bytes 786440 | tf_op jit(solution)/shard_map/sum_swap/ppermute | solution.py:29
  85.4 0.4 shard_map.84
  85.9 0.7 collective-permute-done.8
  86.6 0.8 add_convert_fusion
  (12 shorter events, 0.1 us)
Async XLA Ops:
  0.0 34.5 %copy-start.1 = (bf16[512,256]{1,0:T(8,128)(2,1)S(1)}, bf16[512,256]{1,0:T(8,128)(2,1)}, u32[]{:S(2)}) copy-start(bf16[512,256]{1,0:T(8,128)(2,1)} %refs_3_.1) | copy-start | bytes 786436
  2.9 23.4 %all-to-all-start = ((bf16[8,32,256]{2,1,0:T(8,128)(2,1)}), bf16[8,32,256]{2,1,0:T(8,128)(2,1)S(1)}, u32[]{:S(2)}, u32[]{:S(2)}) async-start(bf16[8,32,256]{2,1,0:T(8,128)(2,1)} %get-tuple-element.18), calls=%async_computation | async-start | bytes 262144 | tf_op jit(solution)/shard_map/states_along_z/all_to_all | solution.py:253
  16.8 0.9 %copy-start = (bf16[512,256]{1,0:T(8,128)(2,1)S(1)}, bf16[512,256]{1,0:T(8,128)(2,1)}, u32[]{:S(2)}) copy-start(bf16[512,256]{1,0:T(8,128)(2,1)} %refs_3_.1) | copy-start | bytes 786436
  17.7 0.9 %copy-start.2 = (bf16[512,256]{1,0:T(8,128)(2,1)S(1)}, bf16[512,256]{1,0:T(8,128)(2,1)}, u32[]{:S(2)}) copy-start(bf16[512,256]{1,0:T(8,128)(2,1)} %refs_1_.1) | copy-start | bytes 786436
  18.7 0.9 %copy-start.3 = (bf16[512,256]{1,0:T(8,128)(2,1)S(1)}, bf16[512,256]{1,0:T(8,128)(2,1)}, u32[]{:S(2)}) copy-start(bf16[512,256]{1,0:T(8,128)(2,1)} %refs_2_.1) | copy-start | bytes 786436
  19.6 0.9 %copy-start.4 = (f32[16,8,256]{2,1,0:T(8,128)S(1)}, f32[16,8,256]{2,1,0:T(8,128)}, u32[]{:S(2)}) copy-start(f32[16,8,256]{2,1,0:T(8,128)} %get-tuple-element.19.refs_4_) | copy-start | bytes 393220
  35.2 30.1 %collective-permute-start.1 = (bf16[512,256]{1,0:T(8,128)(2,1)S(1)}, bf16[512,256]{1,0:T(8,128)(2,1)S(1)}, u32[]{:S(2)}, u32[]{:S(2)}) collective-permute-start(bf16[512,256]{1,0:T(8,128)(2,1)S(1)} %shard_map.82.refs_0_), channel_id=1, source_target_pairs={{0,256},{32,288},{1,257},{33,289},{2,258},{34,290},{3,259},{35,291... | collective-permute-start | bytes 786440 | tf_op jit(solution)/shard_map/along_z/ppermute | solution.py:29
  43.2 26.3 %collective-permute-start.7 = (bf16[512,256]{1,0:T(8,128)(2,1)S(1)}, bf16[512,256]{1,0:T(8,128)(2,1)S(1)}, u32[]{:S(2)}, u32[]{:S(2)}) collective-permute-start(bf16[512,256]{1,0:T(8,128)(2,1)S(1)} %own_along_y.1.refs_0_), channel_id=1, source_target_pairs={{0,128},{32,160},{1,129},{33,161},{2,130},{34,162},{3,131},{35,163... | collective-permute-start | bytes 786440 | tf_op jit(solution)/shard_map/own_along_y/ppermute | solution.py:29
  48.1 25.7 %collective-permute-start.6 = (bf16[512,256]{1,0:T(8,128)(2,1)S(1)}, bf16[512,256]{1,0:T(8,128)(2,1)S(1)}, u32[]{:S(2)}, u32[]{:S(2)}) collective-permute-start(bf16[512,256]{1,0:T(8,128)(2,1)S(1)} %own_along_y.1.refs_0_), channel_id=1, source_target_pairs={{0,64},{32,96},{1,65},{33,97},{2,66},{34,98},{3,67},{35,99},{4,68}... | collective-permute-start | bytes 786440 | tf_op jit(solution)/shard_map/own_along_y/ppermute | solution.py:29
  50.4 23.4 %collective-permute-start.5 = (bf16[512,256]{1,0:T(8,128)(2,1)S(1)}, bf16[512,256]{1,0:T(8,128)(2,1)S(1)}, u32[]{:S(2)}, u32[]{:S(2)}) collective-permute-start(bf16[512,256]{1,0:T(8,128)(2,1)S(1)} %own_along_y.1.refs_0_), channel_id=1, source_target_pairs={{0,192},{32,224},{1,193},{33,225},{2,194},{34,226},{3,195},{35,227... | collective-permute-start | bytes 786440 | tf_op jit(solution)/shard_map/own_along_y/ppermute | solution.py:29
  55.9 9.4 %collective-permute-start = (bf16[2048,256]{1,0:T(8,128)(2,1)S(1)}, bf16[2048,256]{1,0:T(8,128)(2,1)}, u32[]{:S(2)}, u32[]{:S(2)}) collective-permute-start(bf16[2048,256]{1,0:T(8,128)(2,1)S(1)} %bitcast.13), channel_id=1, source_target_pairs={{0,32},{32,0},{1,33},{33,1},{2,34},{34,2},{3,35},{35,3},{4,36},{36... | collective-permute-start | bytes 3145736 | tf_op jit(solution)/shard_map/weight_swap/cond/branch_1_fun/ppermute | solution.py:29
  65.3 11.1 %collective-permute-start.4 = (bf16[512,256]{1,0:T(8,128)(2,1)S(1)}, bf16[512,256]{1,0:T(8,128)(2,1)S(1)}, u32[]{:S(2)}, u32[]{:S(2)}) collective-permute-start(bf16[512,256]{1,0:T(8,128)(2,1)S(1)} %far_along_y.1.refs_0_), channel_id=1, source_target_pairs={{0,128},{32,160},{1,129},{33,161},{2,130},{34,162},{3,131},{35,163... | collective-permute-start | bytes 786440 | tf_op jit(solution)/shard_map/far_along_y/ppermute | solution.py:29
  67.3 15.3 %collective-permute-start.3 = (bf16[512,256]{1,0:T(8,128)(2,1)S(1)}, bf16[512,256]{1,0:T(8,128)(2,1)S(1)}, u32[]{:S(2)}, u32[]{:S(2)}) collective-permute-start(bf16[512,256]{1,0:T(8,128)(2,1)S(1)} %far_along_y.1.refs_0_), channel_id=1, source_target_pairs={{0,64},{32,96},{1,65},{33,97},{2,66},{34,98},{3,67},{35,99},{4,68}... | collective-permute-start | bytes 786440 | tf_op jit(solution)/shard_map/far_along_y/ppermute | solution.py:29
  69.5 13.1 %collective-permute-start.2 = (bf16[512,256]{1,0:T(8,128)(2,1)S(1)}, bf16[512,256]{1,0:T(8,128)(2,1)S(1)}, u32[]{:S(2)}, u32[]{:S(2)}) collective-permute-start(bf16[512,256]{1,0:T(8,128)(2,1)S(1)} %far_along_y.1.refs_0_), channel_id=1, source_target_pairs={{0,192},{32,224},{1,193},{33,225},{2,194},{34,226},{3,195},{35,227... | collective-permute-start | bytes 786440 | tf_op jit(solution)/shard_map/far_along_y/ppermute | solution.py:29
  83.0 3.5 %collective-permute-start.8 = (bf16[512,256]{1,0:T(8,128)(2,1)S(1)}, bf16[512,256]{1,0:T(8,128)(2,1)S(1)}, u32[]{:S(2)}, u32[]{:S(2)}) collective-permute-start(bf16[512,256]{1,0:T(8,128)(2,1)S(1)} %shard_map.85), channel_id=1, source_target_pairs={{0,32},{32,0},{1,33},{33,1},{2,34},{34,2},{3,35},{35,3},{4,36},{36... | collective-permute-start | bytes 786440 | tf_op jit(solution)/shard_map/sum_swap/ppermute | solution.py:29

commit v5 on v4

--- a/solution.py
+++ b/solution.py
@@ -51,7 +51,7 @@
         return tuple(decay[m] * states[m] + x for m in range(modes))
 
     zero = jnp.zeros((CHUNKS, LANES), jnp.float32)
-    states = lax.fori_loop(0, length, step, (zero,) * modes, unroll=4)
+    states = lax.fori_loop(0, length, step, (zero,) * modes, unroll=16)
     later = (CHUNKS - 1 - lax.broadcasted_iota(jnp.int32, (CHUNKS, LANES), 0)).astype(jnp.float32) * float(length)
     for m in range(modes):
         states_ref[m] = states[m]
@@ -133,7 +133,7 @@
             y_scr[half, pl.ds(pl.multiple_of(g * CHUNKS, CHUNKS), CHUNKS), :] = add_up(list(terms))
             return tuple(decay[m] * terms[m] for m in range(modes))
 
-        lax.fori_loop(0, rows // CHUNKS, step, first, unroll=4)
+        lax.fori_loop(0, rows // CHUNKS, step, first, unroll=16)
 
 
 def carry_kernel(rows_ref, before_ref, local_ref, gate_hbm, gated_ref, y_scr, gate_ref, arrived):

time: 88 us -> 87.7 us (level)
  no operation moved by 1% of the time
where the time goes in v5:
time: 87.7 us; the launch traced here: 87 us
  starting transfers between devices  50.2 us (57%)
  waiting for transfers between devices  12.5 us (14%)
  Pallas kernels  9.46 us (11%)
  blocking collectives  8.11 us (9%)
  local copies, waits for them, and re-layouts  5.06 us (6%)
  other arithmetic  1.51 us (2%)
    ppermute x9, starting transfers between devices, move(): return lax.ppermute(array, AXES, pairs)  37.1 us
    all_to_all x1, starting transfers between devices, body(): ends = lax.all_to_all(ends, 'context', 0, 0, axis_index_groups=groups)  13.1 us
    ppermute x9, waiting for transfers between devices, move(): return lax.ppermute(array, AXES, pairs)  9.3 us
    all_to_all x1, blocking collectives, body(): rows = lax.all_to_all(rows, 'context', 0, 0, axis_index_groups=groups)  8.11 us
    pallas_call x8, Pallas kernels, call(): pl.pallas_call(run, grid=(1,), in_specs=[*[full(a) for a in args], *[pl.B...  6.8 us
    unnamed x10, local copies, waits for them, and re-layouts  3.76 us
    all_to_all x1, waiting for transfers between devices, body(): ends = lax.all_to_all(ends, 'context', 0, 0, axis_index_groups=groups)  3.25 us
    pallas_call x1, Pallas kernels, body(): pl.pallas_call(ends_kernel, grid=(halves,), in_specs=[pl.BlockSpec((rows,...  2.66 us
  transfers between devices with their start and end apart: 10, of which 4 were waited for; matrix products, arithmetic and copies ran while one was open for 2% of the time, Pallas kernels for 6%

profile of v5, /device:TPU:1, one launch (start us, length us, event | category | flops | bytes accessed | tf_op | source)
XLA Modules:
  0.0 87.0 jit_solution(7879766471607674013)
XLA Ops:
  0.0 2.7 %shard_map.79 = (bf16[8,32,256]{2,1,0:T(8,128)(2,1)}, f32[16,8,256]{2,1,0:T(8,128)}) custom-call(bf16[512,256]{1,0:T(8,128)(2,1)} %refs_1_.1, bf16[512,256]{1,0:T(8,128)(2,1)} %refs_2_.1, f32[16,256]{1,0:T(8,128)} %bitcast.14), custom_call_target="tpu_custom_call" | custom-call | flops 4194304 | bytes 786432 | tf_op jit(solution)/shard_map/pallas_call | solution.py:241
  2.7 13.1 %all-to-all-start = ((bf16[8,32,256]{2,1,0:T(8,128)(2,1)}), bf16[8,32,256]{2,1,0:T(8,128)(2,1)S(1)}, u32[]{:S(2)}, u32[]{:S(2)}) async-start(bf16[8,32,256]{2,1,0:T(8,128)(2,1)} %get-tuple-element.18), calls=%async_computation | async-start | bytes 262144 | tf_op jit(solution)/shard_map/states_along_z/all_to_all | solution.py:253
  15.7 0.8 pad_maximum_fusion.refs_3_
  16.5 0.9 %copy-done = bf16[512,256]{1,0:T(8,128)(2,1)S(1)} copy-done((bf16[512,256]{1,0:T(8,128)(2,1)S(1)}, bf16[512,256]{1,0:T(8,128)(2,1)}, u32[]{:S(2)}) %copy-start) | copy-done | bytes 262168
  17.5 0.9 %copy-done.2 = bf16[512,256]{1,0:T(8,128)(2,1)S(1)} copy-done((bf16[512,256]{1,0:T(8,128)(2,1)S(1)}, bf16[512,256]{1,0:T(8,128)(2,1)}, u32[]{:S(2)}) %copy-start.2) | copy-done | bytes 262168
  18.4 0.9 %copy-done.3 = bf16[512,256]{1,0:T(8,128)(2,1)S(1)} copy-done((bf16[512,256]{1,0:T(8,128)(2,1)S(1)}, bf16[512,256]{1,0:T(8,128)(2,1)}, u32[]{:S(2)}) %copy-start.3) | copy-done | bytes 262168
  19.4 0.9 %copy-done.4 = f32[16,8,256]{2,1,0:T(8,128)S(1)} copy-done((f32[16,8,256]{2,1,0:T(8,128)S(1)}, f32[16,8,256]{2,1,0:T(8,128)}, u32[]{:S(2)}) %copy-start.4) | copy-done | bytes 131096
  20.3 2.6 %shard_map.80.refs_1_.refs_2_ = f32[544,256]{1,0:T(8,128)S(1)} custom-call(bf16[512,256]{1,0:T(8,128)(2,1)S(1)} %copy-done, bf16[512,256]{1,0:T(8,128)(2,1)S(1)} %copy-done.2, bf16[512,256]{1,0:T(8,128)(2,1)S(1)} %copy-done.3, f32[33,256]{1,0:T(8,128)S(1)} %pad_maximum_fusion.refs_3_, f32[16,8,256]{2,1,0:T(8,128)S(1)} %copy-done.4), custom_call_target="tpu_custom_call" | custom-call | flops 8388608 | bytes 1508352 | tf_op jit(solution)/shard_map/pallas_call | solution.py:209
  22.8 3.2 %all-to-all-done.refs_0_ = bf16[8,32,256]{2,1,0:T(8,128)(2,1)S(1)} async-done(((bf16[8,32,256]{2,1,0:T(8,128)(2,1)}), bf16[8,32,256]{2,1,0:T(8,128)(2,1)S(1)}, u32[]{:S(2)}, u32[]{:S(2)}) %all-to-all-start) | async-done | bytes 131104 | tf_op jit(solution)/shard_map/states_along_z/all_to_all | solution.py:253
  26.1 8.1 %all_to_all.10.refs_0_ = bf16[4,16,256]{2,1,0:T(8,128)(2,1)S(1)} all-to-all(bf16[4,16,256]{2,1,0:T(8,128)(2,1)S(1)} %get-tuple-element.20), channel_id=1, replica_groups={{0,8,16,24},{1,9,17,25},{2,10,18,26},{3,11,19,27},{4,12,20,28},{5,13,21..., dimensions={0} | all-to-all | bytes 65536 | tf_op jit(solution)/shard_map/states_along_x/all_to_all | solution.py:266
  34.2 0.7 shard_map.82.refs_0_
  34.9 7.9 %collective-permute-start.1 = (bf16[512,256]{1,0:T(8,128)(2,1)S(1)}, bf16[512,256]{1,0:T(8,128)(2,1)S(1)}, u32[]{:S(2)}, u32[]{:S(2)}) collective-permute-start(bf16[512,256]{1,0:T(8,128)(2,1)S(1)} %shard_map.82.refs_0_), channel_id=1, source_target_pairs={{0,256},{32,288},{1,257},{33,289},{2,258},{34,290},{3,259},{35,291... | collective-permute-start | bytes 786440 | tf_op jit(solution)/shard_map/along_z/ppermute | solution.py:29
  42.9 4.8 %collective-permute-start.7 = (bf16[512,256]{1,0:T(8,128)(2,1)S(1)}, bf16[512,256]{1,0:T(8,128)(2,1)S(1)}, u32[]{:S(2)}, u32[]{:S(2)}) collective-permute-start(bf16[512,256]{1,0:T(8,128)(2,1)S(1)} %own_along_y.1.refs_0_), channel_id=1, source_target_pairs={{0,128},{32,160},{1,129},{33,161},{2,130},{34,162},{3,131},{35,163... | collective-permute-start | bytes 786440 | tf_op jit(solution)/shard_map/own_along_y/ppermute | solution.py:29
  47.7 2.3 %collective-permute-start.6 = (bf16[512,256]{1,0:T(8,128)(2,1)S(1)}, bf16[512,256]{1,0:T(8,128)(2,1)S(1)}, u32[]{:S(2)}, u32[]{:S(2)}) collective-permute-start(bf16[512,256]{1,0:T(8,128)(2,1)S(1)} %own_along_y.1.refs_0_), channel_id=1, source_target_pairs={{0,64},{32,96},{1,65},{33,97},{2,66},{34,98},{3,67},{35,99},{4,68}... | collective-permute-start | bytes 786440 | tf_op jit(solution)/shard_map/own_along_y/ppermute | solution.py:29
  50.0 4.2 %collective-permute-start.5 = (bf16[512,256]{1,0:T(8,128)(2,1)S(1)}, bf16[512,256]{1,0:T(8,128)(2,1)S(1)}, u32[]{:S(2)}, u32[]{:S(2)}) collective-permute-start(bf16[512,256]{1,0:T(8,128)(2,1)S(1)} %own_along_y.1.refs_0_), channel_id=1, source_target_pairs={{0,192},{32,224},{1,193},{33,225},{2,194},{34,226},{3,195},{35,227... | collective-permute-start | bytes 786440 | tf_op jit(solution)/shard_map/own_along_y/ppermute | solution.py:29
  54.2 10.7 %conditional.1 = (bf16[2048,256]{1,0:T(8,128)(2,1)}) conditional(s32[]{:T(128)} %convert_element_type.9, bf16[4096,256]{1,0:T(8,128)(2,1)} %refs_4_.1, bf16[4096,256]{1,0:T(8,128)(2,1)} %refs_4_.1), branch_computations={%region_0.1_spmd, %region_1.2_spmd} | conditional | flops 13 | bytes 6291649 | solution.py:286
  54.3 1.3 %constant_dynamic-slice_fusion.1 = bf16[8,1,256,256]{3,2,1,0:T(8,128)(2,1)S(1)} fusion(bf16[8,2,256,256]{3,2,1,0:T(8,128)(2,1)} %bitcast.12, s32[]{:T(128)S(6)} %select_n.6), kind=kLoop, calls=%fused_computation.1 | loop fusion | bytes 2097156 | tf_op jit(solution)/shard_map/weight_swap/cond/branch_1_fun/jit(dynamic_index_in_dim)/dynamic_slice | solution.py:281
  55.6 7.0 %collective-permute-start = (bf16[2048,256]{1,0:T(8,128)(2,1)S(1)}, bf16[2048,256]{1,0:T(8,128)(2,1)}, u32[]{:S(2)}, u32[]{:S(2)}) collective-permute-start(bf16[2048,256]{1,0:T(8,128)(2,1)S(1)} %bitcast.13), channel_id=1, source_target_pairs={{0,32},{32,0},{1,33},{33,1},{2,34},{34,2},{3,35},{35,3},{4,36},{36... | collective-permute-start | bytes 3145736 | tf_op jit(solution)/shard_map/weight_swap/cond/branch_1_fun/ppermute | solution.py:29
  62.6 2.4 %collective-permute-done = bf16[2048,256]{1,0:T(8,128)(2,1)} collective-permute-done((bf16[2048,256]{1,0:T(8,128)(2,1)S(1)}, bf16[2048,256]{1,0:T(8,128)(2,1)}, u32[]{:S(2)}, u32[]{:S(2)}) %collective-permute-start) | collective-permute-done | bytes 1048608 | tf_op jit(solution)/shard_map/weight_swap/cond/branch_1_fun/ppermute | solution.py:29
  65.0 0.0 collective-permute-done.1.refs_0_
  65.0 1.9 %collective-permute-start.4 = (bf16[512,256]{1,0:T(8,128)(2,1)S(1)}, bf16[512,256]{1,0:T(8,128)(2,1)S(1)}, u32[]{:S(2)}, u32[]{:S(2)}) collective-permute-start(bf16[512,256]{1,0:T(8,128)(2,1)S(1)} %far_along_y.1.refs_0_), channel_id=1, source_target_pairs={{0,128},{32,160},{1,129},{33,161},{2,130},{34,162},{3,131},{35,163... | collective-permute-start | bytes 786440 | tf_op jit(solution)/shard_map/far_along_y/ppermute | solution.py:29
  66.9 2.2 %collective-permute-start.3 = (bf16[512,256]{1,0:T(8,128)(2,1)S(1)}, bf16[512,256]{1,0:T(8,128)(2,1)S(1)}, u32[]{:S(2)}, u32[]{:S(2)}) collective-permute-start(bf16[512,256]{1,0:T(8,128)(2,1)S(1)} %far_along_y.1.refs_0_), channel_id=1, source_target_pairs={{0,64},{32,96},{1,65},{33,97},{2,66},{34,98},{3,67},{35,99},{4,68}... | collective-permute-start | bytes 786440 | tf_op jit(solution)/shard_map/far_along_y/ppermute | solution.py:29
  69.2 0.0 collective-permute-done.7.refs_3_
  69.2 4.3 %collective-permute-start.2 = (bf16[512,256]{1,0:T(8,128)(2,1)S(1)}, bf16[512,256]{1,0:T(8,128)(2,1)S(1)}, u32[]{:S(2)}, u32[]{:S(2)}) collective-permute-start(bf16[512,256]{1,0:T(8,128)(2,1)S(1)} %far_along_y.1.refs_0_), channel_id=1, source_target_pairs={{0,192},{32,224},{1,193},{33,225},{2,194},{34,226},{3,195},{35,227... | collective-permute-start | bytes 786440 | tf_op jit(solution)/shard_map/far_along_y/ppermute | solution.py:29
  73.5 0.0 collective-permute-done.6.refs_2_
  73.5 2.6 %shard_map.83 = (f32[512,256]{1,0:T(8,128)S(1)}, f32[512,256]{1,0:T(8,128)S(1)}, bf16[4,256,256]{2,1,0:T(8,128)(2,1)S(1)}, bf16[4,256,256]{2,1,0:T(8,128)(2,1)S(1)}) custom-call(bf16[512,256]{1,0:T(8,128)(2,1)S(1)} %own_along_y.1.refs_0_, bf16[512,256]{1,0:T(8,128)(2,1)S(1)} %collective-permute-done.5.refs_1_, ...), custom_call_target="tpu_custom_call" | custom-call | flops 536870912 | bytes 6291456 | tf_op jit(solution)/shard_map/pallas_call | solution.py:209
  76.1 6.2 %collective-permute-done.3.refs_2_ = bf16[512,256]{1,0:T(8,128)(2,1)S(1)} collective-permute-done((bf16[512,256]{1,0:T(8,128)(2,1)S(1)}, bf16[512,256]{1,0:T(8,128)(2,1)S(1)}, u32[]{:S(2)}, u32[]{:S(2)}) %collective-permute-start.3) | collective-permute-done | bytes 262176 | tf_op jit(solution)/shard_map/far_along_y/ppermute | solution.py:29
  82.3 0.4 shard_map.85
  82.7 2.4 %collective-permute-start.8 = (bf16[512,256]{1,0:T(8,128)(2,1)S(1)}, bf16[512,256]{1,0:T(8,128)(2,1)S(1)}, u32[]{:S(2)}, u32[]{:S(2)}) collective-permute-start(bf16[512,256]{1,0:T(8,128)(2,1)S(1)} %shard_map.85), channel_id=1, source_target_pairs={{0,32},{32,0},{1,33},{33,1},{2,34},{34,2},{3,35},{35,3},{4,36},{36... | collective-permute-start | bytes 786440 | tf_op jit(solution)/shard_map/sum_swap/ppermute | solution.py:29
  85.1 0.4 shard_map.84
  85.6 0.7 collective-permute-done.8
  86.3 0.8 add_convert_fusion
  (12 shorter events, 0.1 us)
Async XLA Ops:
  0.0 34.2 %copy-start.1 = (bf16[512,256]{1,0:T(8,128)(2,1)S(1)}, bf16[512,256]{1,0:T(8,128)(2,1)}, u32[]{:S(2)}) copy-start(bf16[512,256]{1,0:T(8,128)(2,1)} %refs_3_.1) | copy-start | bytes 786436
  2.7 23.4 %all-to-all-start = ((bf16[8,32,256]{2,1,0:T(8,128)(2,1)}), bf16[8,32,256]{2,1,0:T(8,128)(2,1)S(1)}, u32[]{:S(2)}, u32[]{:S(2)}) async-start(bf16[8,32,256]{2,1,0:T(8,128)(2,1)} %get-tuple-element.18), calls=%async_computation | async-start | bytes 262144 | tf_op jit(solution)/shard_map/states_along_z/all_to_all | solution.py:253
  16.5 0.9 %copy-start = (bf16[512,256]{1,0:T(8,128)(2,1)S(1)}, bf16[512,256]{1,0:T(8,128)(2,1)}, u32[]{:S(2)}) copy-start(bf16[512,256]{1,0:T(8,128)(2,1)} %refs_3_.1) | copy-start | bytes 786436
  17.4 0.9 %copy-start.2 = (bf16[512,256]{1,0:T(8,128)(2,1)S(1)}, bf16[512,256]{1,0:T(8,128)(2,1)}, u32[]{:S(2)}) copy-start(bf16[512,256]{1,0:T(8,128)(2,1)} %refs_1_.1) | copy-start | bytes 786436
  18.4 0.9 %copy-start.3 = (bf16[512,256]{1,0:T(8,128)(2,1)S(1)}, bf16[512,256]{1,0:T(8,128)(2,1)}, u32[]{:S(2)}) copy-start(bf16[512,256]{1,0:T(8,128)(2,1)} %refs_2_.1) | copy-start | bytes 786436
  19.4 0.9 %copy-start.4 = (f32[16,8,256]{2,1,0:T(8,128)S(1)}, f32[16,8,256]{2,1,0:T(8,128)}, u32[]{:S(2)}) copy-start(f32[16,8,256]{2,1,0:T(8,128)} %get-tuple-element.19.refs_4_) | copy-start | bytes 393220
  34.9 30.1 %collective-permute-start.1 = (bf16[512,256]{1,0:T(8,128)(2,1)S(1)}, bf16[512,256]{1,0:T(8,128)(2,1)S(1)}, u32[]{:S(2)}, u32[]{:S(2)}) collective-permute-start(bf16[512,256]{1,0:T(8,128)(2,1)S(1)} %shard_map.82.refs_0_), channel_id=1, source_target_pairs={{0,256},{32,288},{1,257},{33,289},{2,258},{34,290},{3,259},{35,291... | collective-permute-start | bytes 786440 | tf_op jit(solution)/shard_map/along_z/ppermute | solution.py:29
  42.9 26.3 %collective-permute-start.7 = (bf16[512,256]{1,0:T(8,128)(2,1)S(1)}, bf16[512,256]{1,0:T(8,128)(2,1)S(1)}, u32[]{:S(2)}, u32[]{:S(2)}) collective-permute-start(bf16[512,256]{1,0:T(8,128)(2,1)S(1)} %own_along_y.1.refs_0_), channel_id=1, source_target_pairs={{0,128},{32,160},{1,129},{33,161},{2,130},{34,162},{3,131},{35,163... | collective-permute-start | bytes 786440 | tf_op jit(solution)/shard_map/own_along_y/ppermute | solution.py:29
  47.7 25.7 %collective-permute-start.6 = (bf16[512,256]{1,0:T(8,128)(2,1)S(1)}, bf16[512,256]{1,0:T(8,128)(2,1)S(1)}, u32[]{:S(2)}, u32[]{:S(2)}) collective-permute-start(bf16[512,256]{1,0:T(8,128)(2,1)S(1)} %own_along_y.1.refs_0_), channel_id=1, source_target_pairs={{0,64},{32,96},{1,65},{33,97},{2,66},{34,98},{3,67},{35,99},{4,68}... | collective-permute-start | bytes 786440 | tf_op jit(solution)/shard_map/own_along_y/ppermute | solution.py:29
  50.0 23.4 %collective-permute-start.5 = (bf16[512,256]{1,0:T(8,128)(2,1)S(1)}, bf16[512,256]{1,0:T(8,128)(2,1)S(1)}, u32[]{:S(2)}, u32[]{:S(2)}) collective-permute-start(bf16[512,256]{1,0:T(8,128)(2,1)S(1)} %own_along_y.1.refs_0_), channel_id=1, source_target_pairs={{0,192},{32,224},{1,193},{33,225},{2,194},{34,226},{3,195},{35,227... | collective-permute-start | bytes 786440 | tf_op jit(solution)/shard_map/own_along_y/ppermute | solution.py:29
  55.6 9.4 %collective-permute-start = (bf16[2048,256]{1,0:T(8,128)(2,1)S(1)}, bf16[2048,256]{1,0:T(8,128)(2,1)}, u32[]{:S(2)}, u32[]{:S(2)}) collective-permute-start(bf16[2048,256]{1,0:T(8,128)(2,1)S(1)} %bitcast.13), channel_id=1, source_target_pairs={{0,32},{32,0},{1,33},{33,1},{2,34},{34,2},{3,35},{35,3},{4,36},{36... | collective-permute-start | bytes 3145736 | tf_op jit(solution)/shard_map/weight_swap/cond/branch_1_fun/ppermute | solution.py:29
  65.0 11.1 %collective-permute-start.4 = (bf16[512,256]{1,0:T(8,128)(2,1)S(1)}, bf16[512,256]{1,0:T(8,128)(2,1)S(1)}, u32[]{:S(2)}, u32[]{:S(2)}) collective-permute-start(bf16[512,256]{1,0:T(8,128)(2,1)S(1)} %far_along_y.1.refs_0_), channel_id=1, source_target_pairs={{0,128},{32,160},{1,129},{33,161},{2,130},{34,162},{3,131},{35,163... | collective-permute-start | bytes 786440 | tf_op jit(solution)/shard_map/far_along_y/ppermute | solution.py:29
  66.9 15.3 %collective-permute-start.3 = (bf16[512,256]{1,0:T(8,128)(2,1)S(1)}, bf16[512,256]{1,0:T(8,128)(2,1)S(1)}, u32[]{:S(2)}, u32[]{:S(2)}) collective-permute-start(bf16[512,256]{1,0:T(8,128)(2,1)S(1)} %far_along_y.1.refs_0_), channel_id=1, source_target_pairs={{0,64},{32,96},{1,65},{33,97},{2,66},{34,98},{3,67},{35,99},{4,68}... | collective-permute-start | bytes 786440 | tf_op jit(solution)/shard_map/far_along_y/ppermute | solution.py:29
  69.2 13.1 %collective-permute-start.2 = (bf16[512,256]{1,0:T(8,128)(2,1)S(1)}, bf16[512,256]{1,0:T(8,128)(2,1)S(1)}, u32[]{:S(2)}, u32[]{:S(2)}) collective-permute-start(bf16[512,256]{1,0:T(8,128)(2,1)S(1)} %far_along_y.1.refs_0_), channel_id=1, source_target_pairs={{0,192},{32,224},{1,193},{33,225},{2,194},{34,226},{3,195},{35,227... | collective-permute-start | bytes 786440 | tf_op jit(solution)/shard_map/far_along_y/ppermute | solution.py:29
  82.7 3.5 %collective-permute-start.8 = (bf16[512,256]{1,0:T(8,128)(2,1)S(1)}, bf16[512,256]{1,0:T(8,128)(2,1)S(1)}, u32[]{:S(2)}, u32[]{:S(2)}) collective-permute-start(bf16[512,256]{1,0:T(8,128)(2,1)S(1)} %shard_map.85), channel_id=1, source_target_pairs={{0,32},{32,0},{1,33},{33,1},{2,34},{34,2},{3,35},{35,3},{4,36},{36... | collective-permute-start | bytes 786440 | tf_op jit(solution)/shard_map/sum_swap/ppermute | solution.py:29

commit v6 on v5

--- a/solution.py
+++ b/solution.py
@@ -160,7 +160,7 @@
     out_ref[...] = in_ref[...]
 
 
-def near_product(p0, p1, p2, p3, mine_ref, other_ref, mine_out, other_out, far_mine, far_other):
+def near_product(p0, p1, p2, p3, own_far, mine_ref, other_ref, mine_out, other_out, far_mine, far_other):
     here = lax.axis_index("tensor")
     core, y, z_hi = lax.rem(here, CORES), lax.rem(lax.div(here, CORES), Y), lax.div(here, Y * CORES)
 
@@ -176,12 +176,13 @@
             source = lax.rem(y + Y - AWAY[i], Y)
             total += jnp.dot(piece[...], block(weight, z_hi, source), preferred_element_type=jnp.float32)
             far[i] = block(weight, 1 - z_hi, source)
+        total += jnp.dot(own_far[...], far[0], preferred_element_type=jnp.float32)
         out[...] = total
 
 
-def far_product(p0, p1, p2, p3, weight_ref, start_ref, out_ref):
+def far_product(p1, p2, p3, weight_ref, start_ref, out_ref):
     total = start_ref[...]
-    for i, piece in enumerate((p0, p1, p2, p3)):
+    for i, piece in enumerate((p1, p2, p3), 1):
         total += jnp.dot(piece[...], weight_ref[i], preferred_element_type=jnp.float32)
     out_ref[...] = total.astype(out_ref.dtype)
 
@@ -288,19 +289,19 @@
     sums = shape(f32, tokens, columns)
     work = 2 * tokens * Y * width * columns
     picked = shape(bf16, Y, width, columns)
-    mine_sum, other_sum, far_mine, far_other = call(
-        near_product,
-        (*near, out_weight, other_weight),
-        (sums, sums, picked, picked),
-        flops=2 * work,
-    )
     with jax.named_scope("far_along_y"):
         (far,) = call(copy_kernel, (far,), (shape(bf16, tokens, width),), after=(other_weight,))
         far = [far] + [move(far, dy=d) for d in AWAY[1:]]
-    (other_sum,) = call(far_product, (*far, far_other, other_sum), (shape(bf16, tokens, columns),), flops=work)
+    mine_sum, other_sum, far_mine, far_other = call(
+        near_product,
+        (*near, far[0], out_weight, other_weight),
+        (sums, sums, picked, picked),
+        flops=2 * work,
+    )
+    (other_sum,) = call(far_product, (*far[1:], far_other, other_sum), (shape(bf16, tokens, columns),), flops=work)
     with jax.named_scope("sum_swap"):
         from_other = move(other_sum, dcore=1)
-    (mine_sum,) = call(far_product, (*far, far_mine, mine_sum), (sums,), flops=work)
+    (mine_sum,) = call(far_product, (*far[1:], far_mine, mine_sum), (sums,), flops=work)
     return (mine_sum + from_other.astype(f32)).astype(bf16)
 
 

time: 87.7 us -> 87.6 us (level)
  transfers between devices with their start and end apart: 10 -> 10, of which waited for: 4 -> 4; matrix products, arithmetic and copies ran while one was open for 2% -> 2% of each run, Pallas kernels for 6% -> 7%
where the time goes in v6:
time: 87.6 us; the launch traced here: 86.9 us
  starting transfers between devices  50.2 us (57%)
  waiting for transfers between devices  12.5 us (14%)
  Pallas kernels  9.46 us (11%)
  blocking collectives  8.11 us (9%)
  local copies, waits for them, and re-layouts  5.06 us (6%)
  other arithmetic  1.51 us (2%)
    ppermute x9, starting transfers between devices, move(): return lax.ppermute(array, AXES, pairs)  37.1 us
    all_to_all x1, starting transfers between devices, body(): ends = lax.all_to_all(ends, 'context', 0, 0, axis_index_groups=groups)  13.1 us
    ppermute x9, waiting for transfers between devices, move(): return lax.ppermute(array, AXES, pairs)  9.23 us
    all_to_all x1, blocking collectives, body(): rows = lax.all_to_all(rows, 'context', 0, 0, axis_index_groups=groups)  8.11 us
    pallas_call x8, Pallas kernels, call(): pl.pallas_call(run, grid=(1,), in_specs=[*[full(a) for a in args], *[pl.B...  6.8 us
    unnamed x10, local copies, waits for them, and re-layouts  3.76 us
    all_to_all x1, waiting for transfers between devices, body(): ends = lax.all_to_all(ends, 'context', 0, 0, axis_index_groups=groups)  3.25 us
    pallas_call x1, Pallas kernels, body(): pl.pallas_call(ends_kernel, grid=(halves,), in_specs=[pl.BlockSpec((rows,...  2.66 us
  transfers between devices with their start and end apart: 10, of which 4 were waited for; matrix products, arithmetic and copies ran while one was open for 2% of the time, Pallas kernels for 7%

profile of v6, /device:TPU:1, one launch (start us, length us, event | category | flops | bytes accessed | tf_op | source)
XLA Modules:
  0.0 86.9 jit_solution(3970832407073495519)
XLA Ops:
  0.0 2.7 %shard_map.79 = (bf16[8,32,256]{2,1,0:T(8,128)(2,1)}, f32[16,8,256]{2,1,0:T(8,128)}) custom-call(bf16[512,256]{1,0:T(8,128)(2,1)} %refs_1_.1, bf16[512,256]{1,0:T(8,128)(2,1)} %refs_2_.1, f32[16,256]{1,0:T(8,128)} %bitcast.14), custom_call_target="tpu_custom_call" | custom-call | flops 4194304 | bytes 786432 | tf_op jit(solution)/shard_map/pallas_call | solution.py:242
  2.7 13.1 %all-to-all-start = ((bf16[8,32,256]{2,1,0:T(8,128)(2,1)}), bf16[8,32,256]{2,1,0:T(8,128)(2,1)S(1)}, u32[]{:S(2)}, u32[]{:S(2)}) async-start(bf16[8,32,256]{2,1,0:T(8,128)(2,1)} %get-tuple-element.18), calls=%async_computation | async-start | bytes 262144 | tf_op jit(solution)/shard_map/states_along_z/all_to_all | solution.py:254
  15.7 0.8 pad_maximum_fusion.refs_3_
  16.5 0.9 %copy-done = bf16[512,256]{1,0:T(8,128)(2,1)S(1)} copy-done((bf16[512,256]{1,0:T(8,128)(2,1)S(1)}, bf16[512,256]{1,0:T(8,128)(2,1)}, u32[]{:S(2)}) %copy-start) | copy-done | bytes 262168
  17.5 0.9 %copy-done.2 = bf16[512,256]{1,0:T(8,128)(2,1)S(1)} copy-done((bf16[512,256]{1,0:T(8,128)(2,1)S(1)}, bf16[512,256]{1,0:T(8,128)(2,1)}, u32[]{:S(2)}) %copy-start.2) | copy-done | bytes 262168
  18.4 0.9 %copy-done.3 = bf16[512,256]{1,0:T(8,128)(2,1)S(1)} copy-done((bf16[512,256]{1,0:T(8,128)(2,1)S(1)}, bf16[512,256]{1,0:T(8,128)(2,1)}, u32[]{:S(2)}) %copy-start.3) | copy-done | bytes 262168
  19.4 0.9 %copy-done.4 = f32[16,8,256]{2,1,0:T(8,128)S(1)} copy-done((f32[16,8,256]{2,1,0:T(8,128)S(1)}, f32[16,8,256]{2,1,0:T(8,128)}, u32[]{:S(2)}) %copy-start.4) | copy-done | bytes 131096
  20.3 2.6 %shard_map.80.refs_1_.refs_2_ = f32[544,256]{1,0:T(8,128)S(1)} custom-call(bf16[512,256]{1,0:T(8,128)(2,1)S(1)} %copy-done, bf16[512,256]{1,0:T(8,128)(2,1)S(1)} %copy-done.2, bf16[512,256]{1,0:T(8,128)(2,1)S(1)} %copy-done.3, f32[33,256]{1,0:T(8,128)S(1)} %pad_maximum_fusion.refs_3_, f32[16,8,256]{2,1,0:T(8,128)S(1)} %copy-done.4), custom_call_target="tpu_custom_call" | custom-call | flops 8388608 | bytes 1508352 | tf_op jit(solution)/shard_map/pallas_call | solution.py:210
  22.8 3.2 %all-to-all-done.refs_0_ = bf16[8,32,256]{2,1,0:T(8,128)(2,1)S(1)} async-done(((bf16[8,32,256]{2,1,0:T(8,128)(2,1)}), bf16[8,32,256]{2,1,0:T(8,128)(2,1)S(1)}, u32[]{:S(2)}, u32[]{:S(2)}) %all-to-all-start) | async-done | bytes 131104 | tf_op jit(solution)/shard_map/states_along_z/all_to_all | solution.py:254
  26.1 8.1 %all_to_all.10.refs_0_ = bf16[4,16,256]{2,1,0:T(8,128)(2,1)S(1)} all-to-all(bf16[4,16,256]{2,1,0:T(8,128)(2,1)S(1)} %get-tuple-element.20), channel_id=1, replica_groups={{0,8,16,24},{1,9,17,25},{2,10,18,26},{3,11,19,27},{4,12,20,28},{5,13,21..., dimensions={0} | all-to-all | bytes 65536 | tf_op jit(solution)/shard_map/states_along_x/all_to_all | solution.py:267
  34.2 0.7 shard_map.82.refs_0_
  34.9 7.9 %collective-permute-start.1 = (bf16[512,256]{1,0:T(8,128)(2,1)S(1)}, bf16[512,256]{1,0:T(8,128)(2,1)S(1)}, u32[]{:S(2)}, u32[]{:S(2)}) collective-permute-start(bf16[512,256]{1,0:T(8,128)(2,1)S(1)} %shard_map.82.refs_0_), channel_id=1, source_target_pairs={{0,256},{32,288},{1,257},{33,289},{2,258},{34,290},{3,259},{35,291... | collective-permute-start | bytes 786440 | tf_op jit(solution)/shard_map/along_z/ppermute | solution.py:29
  42.9 4.8 %collective-permute-start.7 = (bf16[512,256]{1,0:T(8,128)(2,1)S(1)}, bf16[512,256]{1,0:T(8,128)(2,1)S(1)}, u32[]{:S(2)}, u32[]{:S(2)}) collective-permute-start(bf16[512,256]{1,0:T(8,128)(2,1)S(1)} %own_along_y.1.refs_0_), channel_id=1, source_target_pairs={{0,128},{32,160},{1,129},{33,161},{2,130},{34,162},{3,131},{35,163... | collective-permute-start | bytes 786440 | tf_op jit(solution)/shard_map/own_along_y/ppermute | solution.py:29
  47.7 2.3 %collective-permute-start.6 = (bf16[512,256]{1,0:T(8,128)(2,1)S(1)}, bf16[512,256]{1,0:T(8,128)(2,1)S(1)}, u32[]{:S(2)}, u32[]{:S(2)}) collective-permute-start(bf16[512,256]{1,0:T(8,128)(2,1)S(1)} %own_along_y.1.refs_0_), channel_id=1, source_target_pairs={{0,64},{32,96},{1,65},{33,97},{2,66},{34,98},{3,67},{35,99},{4,68}... | collective-permute-start | bytes 786440 | tf_op jit(solution)/shard_map/own_along_y/ppermute | solution.py:29
  50.0 4.2 %collective-permute-start.5 = (bf16[512,256]{1,0:T(8,128)(2,1)S(1)}, bf16[512,256]{1,0:T(8,128)(2,1)S(1)}, u32[]{:S(2)}, u32[]{:S(2)}) collective-permute-start(bf16[512,256]{1,0:T(8,128)(2,1)S(1)} %own_along_y.1.refs_0_), channel_id=1, source_target_pairs={{0,192},{32,224},{1,193},{33,225},{2,194},{34,226},{3,195},{35,227... | collective-permute-start | bytes 786440 | tf_op jit(solution)/shard_map/own_along_y/ppermute | solution.py:29
  54.2 10.7 %conditional.1 = (bf16[2048,256]{1,0:T(8,128)(2,1)}) conditional(s32[]{:T(128)} %convert_element_type.9, bf16[4096,256]{1,0:T(8,128)(2,1)} %refs_5_.1, bf16[4096,256]{1,0:T(8,128)(2,1)} %refs_5_.1), branch_computations={%region_0.1_spmd, %region_1.2_spmd} | conditional | flops 13 | bytes 6291649 | solution.py:287
  54.3 1.3 %constant_dynamic-slice_fusion.1 = bf16[8,1,256,256]{3,2,1,0:T(8,128)(2,1)S(1)} fusion(bf16[8,2,256,256]{3,2,1,0:T(8,128)(2,1)} %bitcast.12, s32[]{:T(128)S(6)} %select_n.6), kind=kLoop, calls=%fused_computation.1 | loop fusion | bytes 2097156 | tf_op jit(solution)/shard_map/weight_swap/cond/branch_1_fun/jit(dynamic_index_in_dim)/dynamic_slice | solution.py:282
  55.6 7.0 %collective-permute-start = (bf16[2048,256]{1,0:T(8,128)(2,1)S(1)}, bf16[2048,256]{1,0:T(8,128)(2,1)}, u32[]{:S(2)}, u32[]{:S(2)}) collective-permute-start(bf16[2048,256]{1,0:T(8,128)(2,1)S(1)} %bitcast.13), channel_id=1, source_target_pairs={{0,32},{32,0},{1,33},{33,1},{2,34},{34,2},{3,35},{35,3},{4,36},{36... | collective-permute-start | bytes 3145736 | tf_op jit(solution)/shard_map/weight_swap/cond/branch_1_fun/ppermute | solution.py:29
  62.6 2.4 %collective-permute-done = bf16[2048,256]{1,0:T(8,128)(2,1)} collective-permute-done((bf16[2048,256]{1,0:T(8,128)(2,1)S(1)}, bf16[2048,256]{1,0:T(8,128)(2,1)}, u32[]{:S(2)}, u32[]{:S(2)}) %collective-permute-start) | collective-permute-done | bytes 1048608 | tf_op jit(solution)/shard_map/weight_swap/cond/branch_1_fun/ppermute | solution.py:29
  65.0 1.9 %collective-permute-start.4 = (bf16[512,256]{1,0:T(8,128)(2,1)S(1)}, bf16[512,256]{1,0:T(8,128)(2,1)S(1)}, u32[]{:S(2)}, u32[]{:S(2)}) collective-permute-start(bf16[512,256]{1,0:T(8,128)(2,1)S(1)} %far_along_y.1.refs_4_), channel_id=1, source_target_pairs={{0,128},{32,160},{1,129},{33,161},{2,130},{34,162},{3,131},{35,163... | collective-permute-start | bytes 786440 | tf_op jit(solution)/shard_map/far_along_y/ppermute | solution.py:29
  66.9 2.2 %collective-permute-start.3 = (bf16[512,256]{1,0:T(8,128)(2,1)S(1)}, bf16[512,256]{1,0:T(8,128)(2,1)S(1)}, u32[]{:S(2)}, u32[]{:S(2)}) collective-permute-start(bf16[512,256]{1,0:T(8,128)(2,1)S(1)} %far_along_y.1.refs_4_), channel_id=1, source_target_pairs={{0,64},{32,96},{1,65},{33,97},{2,66},{34,98},{3,67},{35,99},{4,68}... | collective-permute-start | bytes 786440 | tf_op jit(solution)/shard_map/far_along_y/ppermute | solution.py:29
  69.2 0.0 collective-permute-done.7.refs_3_
  69.2 4.3 %collective-permute-start.2 = (bf16[512,256]{1,0:T(8,128)(2,1)S(1)}, bf16[512,256]{1,0:T(8,128)(2,1)S(1)}, u32[]{:S(2)}, u32[]{:S(2)}) collective-permute-start(bf16[512,256]{1,0:T(8,128)(2,1)S(1)} %far_along_y.1.refs_4_), channel_id=1, source_target_pairs={{0,192},{32,224},{1,193},{33,225},{2,194},{34,226},{3,195},{35,227... | collective-permute-start | bytes 786440 | tf_op jit(solution)/shard_map/far_along_y/ppermute | solution.py:29
  73.5 0.0 collective-permute-done.6.refs_2_
  73.5 2.7 %shard_map.83 = (f32[512,256]{1,0:T(8,128)S(1)}, f32[512,256]{1,0:T(8,128)S(1)}, bf16[4,256,256]{2,1,0:T(8,128)(2,1)S(1)}, bf16[4,256,256]{2,1,0:T(8,128)(2,1)S(1)}) custom-call(bf16[512,256]{1,0:T(8,128)(2,1)S(1)} %own_along_y.1.refs_0_, bf16[512,256]{1,0:T(8,128)(2,1)S(1)} %collective-permute-done.5.refs_1_, ...), custom_call_target="tpu_custom_call" | custom-call | flops 536870912 | bytes 6553600 | tf_op jit(solution)/shard_map/pallas_call | solution.py:210
  76.2 0.0 collective-permute-done.4.refs_2_
  76.2 6.1 %collective-permute-done.3.refs_1_ = bf16[512,256]{1,0:T(8,128)(2,1)S(1)} collective-permute-done((bf16[512,256]{1,0:T(8,128)(2,1)S(1)}, bf16[512,256]{1,0:T(8,128)(2,1)S(1)}, u32[]{:S(2)}, u32[]{:S(2)}) %collective-permute-start.3) | collective-permute-done | bytes 262176 | tf_op jit(solution)/shard_map/far_along_y/ppermute | solution.py:29
  82.3 0.4 shard_map.85
  82.7 2.4 %collective-permute-start.8 = (bf16[512,256]{1,0:T(8,128)(2,1)S(1)}, bf16[512,256]{1,0:T(8,128)(2,1)S(1)}, u32[]{:S(2)}, u32[]{:S(2)}) collective-permute-start(bf16[512,256]{1,0:T(8,128)(2,1)S(1)} %shard_map.85), channel_id=1, source_target_pairs={{0,32},{32,0},{1,33},{33,1},{2,34},{34,2},{3,35},{35,3},{4,36},{36... | collective-permute-start | bytes 786440 | tf_op jit(solution)/shard_map/sum_swap/ppermute | solution.py:29
  85.1 0.4 shard_map.84
  85.4 0.8 collective-permute-done.8
  86.2 0.8 add_convert_fusion
  (12 shorter events, 0.1 us)
Async XLA Ops:
  0.0 34.2 %copy-start.1 = (bf16[512,256]{1,0:T(8,128)(2,1)S(1)}, bf16[512,256]{1,0:T(8,128)(2,1)}, u32[]{:S(2)}) copy-start(bf16[512,256]{1,0:T(8,128)(2,1)} %refs_3_.1) | copy-start | bytes 786436
  2.7 23.4 %all-to-all-start = ((bf16[8,32,256]{2,1,0:T(8,128)(2,1)}), bf16[8,32,256]{2,1,0:T(8,128)(2,1)S(1)}, u32[]{:S(2)}, u32[]{:S(2)}) async-start(bf16[8,32,256]{2,1,0:T(8,128)(2,1)} %get-tuple-element.18), calls=%async_computation | async-start | bytes 262144 | tf_op jit(solution)/shard_map/states_along_z/all_to_all | solution.py:254
  16.5 0.9 %copy-start = (bf16[512,256]{1,0:T(8,128)(2,1)S(1)}, bf16[512,256]{1,0:T(8,128)(2,1)}, u32[]{:S(2)}) copy-start(bf16[512,256]{1,0:T(8,128)(2,1)} %refs_3_.1) | copy-start | bytes 786436
  17.4 0.9 %copy-start.2 = (bf16[512,256]{1,0:T(8,128)(2,1)S(1)}, bf16[512,256]{1,0:T(8,128)(2,1)}, u32[]{:S(2)}) copy-start(bf16[512,256]{1,0:T(8,128)(2,1)} %refs_1_.1) | copy-start | bytes 786436
  18.4 0.9 %copy-start.3 = (bf16[512,256]{1,0:T(8,128)(2,1)S(1)}, bf16[512,256]{1,0:T(8,128)(2,1)}, u32[]{:S(2)}) copy-start(bf16[512,256]{1,0:T(8,128)(2,1)} %refs_2_.1) | copy-start | bytes 786436
  19.4 0.9 %copy-start.4 = (f32[16,8,256]{2,1,0:T(8,128)S(1)}, f32[16,8,256]{2,1,0:T(8,128)}, u32[]{:S(2)}) copy-start(f32[16,8,256]{2,1,0:T(8,128)} %get-tuple-element.19.refs_4_) | copy-start | bytes 393220
  34.9 30.1 %collective-permute-start.1 = (bf16[512,256]{1,0:T(8,128)(2,1)S(1)}, bf16[512,256]{1,0:T(8,128)(2,1)S(1)}, u32[]{:S(2)}, u32[]{:S(2)}) collective-permute-start(bf16[512,256]{1,0:T(8,128)(2,1)S(1)} %shard_map.82.refs_0_), channel_id=1, source_target_pairs={{0,256},{32,288},{1,257},{33,289},{2,258},{34,290},{3,259},{35,291... | collective-permute-start | bytes 786440 | tf_op jit(solution)/shard_map/along_z/ppermute | solution.py:29
  42.9 26.3 %collective-permute-start.7 = (bf16[512,256]{1,0:T(8,128)(2,1)S(1)}, bf16[512,256]{1,0:T(8,128)(2,1)S(1)}, u32[]{:S(2)}, u32[]{:S(2)}) collective-permute-start(bf16[512,256]{1,0:T(8,128)(2,1)S(1)} %own_along_y.1.refs_0_), channel_id=1, source_target_pairs={{0,128},{32,160},{1,129},{33,161},{2,130},{34,162},{3,131},{35,163... | collective-permute-start | bytes 786440 | tf_op jit(solution)/shard_map/own_along_y/ppermute | solution.py:29
  47.7 25.7 %collective-permute-start.6 = (bf16[512,256]{1,0:T(8,128)(2,1)S(1)}, bf16[512,256]{1,0:T(8,128)(2,1)S(1)}, u32[]{:S(2)}, u32[]{:S(2)}) collective-permute-start(bf16[512,256]{1,0:T(8,128)(2,1)S(1)} %own_along_y.1.refs_0_), channel_id=1, source_target_pairs={{0,64},{32,96},{1,65},{33,97},{2,66},{34,98},{3,67},{35,99},{4,68}... | collective-permute-start | bytes 786440 | tf_op jit(solution)/shard_map/own_along_y/ppermute | solution.py:29
  50.0 23.4 %collective-permute-start.5 = (bf16[512,256]{1,0:T(8,128)(2,1)S(1)}, bf16[512,256]{1,0:T(8,128)(2,1)S(1)}, u32[]{:S(2)}, u32[]{:S(2)}) collective-permute-start(bf16[512,256]{1,0:T(8,128)(2,1)S(1)} %own_along_y.1.refs_0_), channel_id=1, source_target_pairs={{0,192},{32,224},{1,193},{33,225},{2,194},{34,226},{3,195},{35,227... | collective-permute-start | bytes 786440 | tf_op jit(solution)/shard_map/own_along_y/ppermute | solution.py:29
  55.6 9.4 %collective-permute-start = (bf16[2048,256]{1,0:T(8,128)(2,1)S(1)}, bf16[2048,256]{1,0:T(8,128)(2,1)}, u32[]{:S(2)}, u32[]{:S(2)}) collective-permute-start(bf16[2048,256]{1,0:T(8,128)(2,1)S(1)} %bitcast.13), channel_id=1, source_target_pairs={{0,32},{32,0},{1,33},{33,1},{2,34},{34,2},{3,35},{35,3},{4,36},{36... | collective-permute-start | bytes 3145736 | tf_op jit(solution)/shard_map/weight_swap/cond/branch_1_fun/ppermute | solution.py:29
  65.0 11.2 %collective-permute-start.4 = (bf16[512,256]{1,0:T(8,128)(2,1)S(1)}, bf16[512,256]{1,0:T(8,128)(2,1)S(1)}, u32[]{:S(2)}, u32[]{:S(2)}) collective-permute-start(bf16[512,256]{1,0:T(8,128)(2,1)S(1)} %far_along_y.1.refs_4_), channel_id=1, source_target_pairs={{0,128},{32,160},{1,129},{33,161},{2,130},{34,162},{3,131},{35,163... | collective-permute-start | bytes 786440 | tf_op jit(solution)/shard_map/far_along_y/ppermute | solution.py:29
  66.9 15.3 %collective-permute-start.3 = (bf16[512,256]{1,0:T(8,128)(2,1)S(1)}, bf16[512,256]{1,0:T(8,128)(2,1)S(1)}, u32[]{:S(2)}, u32[]{:S(2)}) collective-permute-start(bf16[512,256]{1,0:T(8,128)(2,1)S(1)} %far_along_y.1.refs_4_), channel_id=1, source_target_pairs={{0,64},{32,96},{1,65},{33,97},{2,66},{34,98},{3,67},{35,99},{4,68}... | collective-permute-start | bytes 786440 | tf_op jit(solution)/shard_map/far_along_y/ppermute | solution.py:29
  69.2 13.1 %collective-permute-start.2 = (bf16[512,256]{1,0:T(8,128)(2,1)S(1)}, bf16[512,256]{1,0:T(8,128)(2,1)S(1)}, u32[]{:S(2)}, u32[]{:S(2)}) collective-permute-start(bf16[512,256]{1,0:T(8,128)(2,1)S(1)} %far_along_y.1.refs_4_), channel_id=1, source_target_pairs={{0,192},{32,224},{1,193},{33,225},{2,194},{34,226},{3,195},{35,227... | collective-permute-start | bytes 786440 | tf_op jit(solution)/shard_map/far_along_y/ppermute | solution.py:29
  82.7 3.5 %collective-permute-start.8 = (bf16[512,256]{1,0:T(8,128)(2,1)S(1)}, bf16[512,256]{1,0:T(8,128)(2,1)S(1)}, u32[]{:S(2)}, u32[]{:S(2)}) collective-permute-start(bf16[512,256]{1,0:T(8,128)(2,1)S(1)} %shard_map.85), channel_id=1, source_target_pairs={{0,32},{32,0},{1,33},{33,1},{2,34},{34,2},{3,35},{35,3},{4,36},{36... | collective-permute-start | bytes 786440 | tf_op jit(solution)/shard_map/sum_swap/ppermute | solution.py:29
